TPU v7x, 32 devices: a whole 2x2x4 slice. The times are simulated.
32 devices in a mesh: space: 4 (over z), node: 4 (over x, core), tm: 2 (over y).
Axes of the slice: x: 2, y: 2, z: 4, core: 2. Of those that a mesh axis runs over, the one named last changes fastest.
Arguments:
- start_old: float32 [2, 32, 128, 256], P('tm', 'space'), may hold values from -4 to 4
- nodes_old: float32 [2, 4, 32, 128, 256], P('tm', 'node', 'space'), may hold values from -4 to 4
Outputs:
- nodes_new: float32 [2, 4, 32, 128, 256], P('tm', 'node', 'space')
- end_new: float32 [2, 32, 128, 256], P('tm', 'space')
All inputs are finite; a program needn't handle non-finite values.
Results may differ from a plain program's by a relative error of at most 0.00002.
Values sent between devices are 32-bit elements; how exact they have to be, the bound alone decides.
No kernel may reach another device: no remote copies, remote signals or barrier semaphores. Data moves between devices by JAX's collectives and lax.ppermute only.
A program may use at most 64 MiB of HBM per device.

v0:
```python
import jax
import jax.numpy as jnp
from jax import lax
from jax.sharding import PartitionSpec as P

NODES = 4
PASSES = 4


time_step = 0.25
diffusion = 4.0
reaction = 1.0


def padded_2(block, sides, width):
    for axis, dim in sides:
        count = lax.axis_size(axis)
        forward = [(i, i + 1) for i in range(count - 1)]
        forward.append((count - 1, 0))
        backward = [(target, source) for source, target in forward]
        low = lax.ppermute(
            lax.slice_in_dim(block, block.shape[dim] - width, None, axis=dim), axis, forward
        )
        high = lax.ppermute(lax.slice_in_dim(block, 0, width, axis=dim), axis, backward)
        block = jnp.concatenate([low, block, high], axis=dim)
    return block


def shifted_2(array, axis, by):
    size = lax.axis_size(axis)
    pairs = [(i, i + by) for i in range(size) if 0 <= i + by < size]
    return lax.ppermute(array, axis, pairs)


def collocation(count):
    points = [-0.8611363115940526, -0.3399810435848563, 0.3399810435848563, 0.8611363115940526]
    raw_weights = [0.3478548451374538, 0.6521451548625461, 0.6521451548625461, 0.3478548451374538]
    node_times = [(point + 1.0) / 2.0 for point in points]
    quadrature = [[0.0 for column in range(count)] for target in range(count)]
    for source in range(count):
        coeffs = [1.0]
        scaling = 1.0
        for other in range(count):
            if other != source:
                other_time = node_times[other]
                shifted = [0.0] + coeffs
                for power in range(len(coeffs)):
                    shifted[power] = shifted[power] - other_time * coeffs[power]
                coeffs = shifted
                scaling = scaling * (node_times[source] - other_time)
        for target in range(count):
            target_time = node_times[target]
            integral = 0.0
            for power in range(len(coeffs)):
                integral = integral + coeffs[power] * target_time ** (power + 1) / (power + 1)
            quadrature[target][source] = integral / scaling
    return (node_times, quadrature, [weight / 2.0 for weight in raw_weights])


def neighbour_sum(padded):
    inner = padded[1:-1]
    total = padded[2:] + padded[:-2]
    total = total + jnp.roll(inner, -1, 1) + jnp.roll(inner, 1, 1)
    total = total + jnp.roll(inner, -1, 2) + jnp.roll(inner, 1, 2)
    return total


def forcing(values, padded):
    laplace = neighbour_sum(padded) - 6.0 * values
    return (laplace, diffusion * laplace + reaction * (values - values * values * values))


def on_device(start_old, nodes_old):
    node_times, quadrature, weights = collocation(NODES)
    node_index = lax.axis_index("node")
    node_time = jnp.asarray(node_times, jnp.float32)[node_index]
    weight_table = jnp.asarray(weights, jnp.float32)
    node_weight = weight_table[node_index]
    quad_table = jnp.asarray(quadrature, jnp.float32)
    state_old = nodes_old[0, 0]
    start_state = start_old[0]
    padded = padded_2(state_old, (("space", 0),), 1)
    laplace_old, force_old = forcing(state_old, padded)
    quad_row = quad_table[node_index]
    shard_piece = lax.all_gather(force_old[None], "node", axis=0, tiled=True)
    quad_part = jnp.sum(quad_row[:, None, None, None] * shard_piece, axis=0)
    weight_part = jnp.sum(weight_table[:, None, None, None] * shard_piece, axis=0)
    end_old = start_state + time_step * weight_part
    received = shifted_2(end_old, "tm", 1)
    begin_state = jnp.where(lax.axis_index("tm") == 0, start_state, received)
    implicit = time_step * diffusion * node_time
    right_side = begin_state + time_step * quad_part - implicit * laplace_old
    divisor = 1.0 + 6.0 * implicit
    iterate = state_old
    for step_index in range(PASSES):
        widened = padded_2(iterate, (("space", 0),), 1)
        iterate = (right_side + implicit * neighbour_sum(widened)) / divisor
    padded_new = padded_2(iterate, (("space", 0),), 1)
    laplace_new, force_new = forcing(iterate, padded_new)
    weighted_new = lax.psum(node_weight * force_new, "node")
    end_new = begin_state + time_step * weighted_new
    return (iterate[None, None], end_new[None])


def solution(mesh):
    return jax.shard_map(
        on_device,
        mesh=mesh,
        in_specs=(P("tm", "space", None, None), P("tm", "node", "space", None, None)),
        out_specs=(P("tm", "node", "space", None, None), P("tm", "space", None, None)),
        check_vma=False,
    )
```

profile of v0, /device:TPU:0, one launch (start us, length us, event | category | flops | bytes accessed | tf_op | source)
XLA Modules:
  0.0 176.7 jit_solution(7567872669622339965)
XLA Ops:
  8.3 5.1 %collective-permute-start = (f32[1,128,256]{2,1,0:T(8,128)S(1)}, f32[1,128,256]{2,1,0:T(8,128)S(1)}, u32[]{:S(2)}, u32[]{:S(2)}) collective-permute-start(f32[1,128,256]{2,1,0:T(8,128)S(1)} %get-tuple-element.48), channel_id=1, source_target_pairs={{8,0},{16,8},{24,16},{0,24},{9,1},{17,9},{25,17},{1,25},{10,2},{18... | collective-permute-start | bytes 393224 | tf_op jit(solution)/shard_map/ppermute | solution.py:24
  13.4 1.4 fusion.63
  14.8 1.9 %fusion.62 = (f32[8,128,255]{2,1,0:T(8,128)S(1)}, f32[8,128,255]{2,1,0:T(8,128)S(1)}) fusion(f32[8,128,256]{2,1,0:T(8,128)} %bitcast.25), kind=kLoop, calls=%fused_computation.84 | loop fusion | bytes 4177920 | tf_op jit(solution)/shard_map/jit(_roll_static)/slice | solution.py:64
  17.3 2.9 %collective-permute-done.1 = f32[1,128,256]{2,1,0:T(8,128)S(1)} collective-permute-done((f32[1,128,256]{2,1,0:T(8,128)S(1)}, f32[1,128,256]{2,1,0:T(8,128)S(1)}, u32[]{:S(2)}, u32[]{:S(2)}) %collective-permute-start.1) | collective-permute-done | bytes 131104 | tf_op jit(solution)/shard_map/ppermute | solution.py:21
  20.2 2.2 %fusion = (f32[8,128,256]{2,1,0:T(8,128)}, f32[8,128,256]{2,1,0:T(8,128)}) fusion(f32[1,1,8,128,256]{4,3,2,1,0:T(8,128)S(1)} %copy-done, f32[8,128,255]{2,1,0:T(8,128)S(1)} %get-tuple-element.55, f32[8,128,1]{2,1,0:T(8,128)S(1)} %get-tuple-element.57, f32[8,128,1]{2,1,0:T(8,128)S(1)} %get-tuple-element.56, f32[8,128,255]{2,1,0:T(8,128)S(1)} %get-tuple-element.54, ...), kind=kLoop, calls=%fused_computation.4 | loop fusion | flops 4718592 | bytes 8650752 | tf_op jit(solution)/shard_map/add | solution.py:70
  23.2 32.9 %all-gather.3.cloned.1.call-done = f32[32,128,256]{2,1,0:T(8,128)} async-done(((f32[8,128,256]{2,1,0:T(8,128)}), f32[32,128,256]{2,1,0:T(8,128)}) %all-gather.3.cloned.1.call-update) | async-done | bytes 4194320 | tf_op jit(solution)/shard_map/all_gather | solution.py:85
  56.1 4.1 %multiply_reduce_fusion.1 = (f32[8,128,256]{2,1,0:T(8,128)S(1)}, f32[8,128,256]{2,1,0:T(8,128)}) fusion(f32[4,8,128,256]{3,2,1,0:T(8,128)} %bitcast.30, f32[4]{0:T(128)S(1)} %copy-done.3, f32[4]{0:T(128)S(1)} %dynamic-slice_bitcast_fusion), kind=kLoop, calls=%fused_computation.1 | loop fusion | flops 3670016 | bytes 6291488 | tf_op jit(solution)/shard_map/reduce_sum | solution.py:87
  61.3 3.4 %collective-permute-start.2 = (f32[8,128,256]{2,1,0:T(8,128)}, f32[8,128,256]{2,1,0:T(8,128)S(1)}, u32[]{:S(2)}, u32[]{:S(2)}) collective-permute-start(f32[8,128,256]{2,1,0:T(8,128)} %bitcast_add_fusion), channel_id=1, source_target_pairs={{0,1},{2,3},{4,5},{6,7},{8,9},{10,11},{12,13},{14,15},{16,17},{18,... | collective-permute-start | bytes 3145736 | tf_op jit(solution)/shard_map/ppermute | solution.py:32
  66.5 21.3 %collective-permute-done.2 = f32[8,128,256]{2,1,0:T(8,128)S(1)} collective-permute-done((f32[8,128,256]{2,1,0:T(8,128)}, f32[8,128,256]{2,1,0:T(8,128)S(1)}, u32[]{:S(2)}, u32[]{:S(2)}) %collective-permute-start.2) | collective-permute-done | bytes 1048608 | tf_op jit(solution)/shard_map/ppermute | solution.py:32
  87.8 2.5 %add_divide_fusion = (f32[8,128,256]{2,1,0:T(8,128)S(1)}, f32[8,128,256]{2,1,0:T(8,128)S(1)}) fusion(f32[8,128,256]{2,1,0:T(8,128)} %get-tuple-element.7, f32[]{:T(128)S(6)} %add.127, f32[]{:T(128)} %bitcast.6, f32[1,1,8,128,256]{4,3,2,1,0:T(8,128)S(1)} %copy-done, f32[8,128,256]{2,1,0:T(8,128)} %get-tuple-element.3, ...), kind=kLoop, calls=%fused_computation.56 | loop fusion | flops 2621440 | bytes 7340041 | tf_op jit(solution)/shard_map/div | solution.py:97
  91.1 3.4 %collective-permute-start.3 = (f32[1,128,256]{2,1,0:T(8,128)S(1)}, f32[1,128,256]{2,1,0:T(8,128)S(1)}, u32[]{:S(2)}, u32[]{:S(2)}) collective-permute-start(f32[1,128,256]{2,1,0:T(8,128)S(1)} %get-tuple-element.46), channel_id=1, source_target_pairs={{8,0},{16,8},{24,16},{0,24},{9,1},{17,9},{25,17},{1,25},{10,2},{18... | collective-permute-start | bytes 393224 | tf_op jit(solution)/shard_map/ppermute | solution.py:24
  94.5 3.7 %collective-permute-done.3 = f32[1,128,256]{2,1,0:T(8,128)S(1)} collective-permute-done((f32[1,128,256]{2,1,0:T(8,128)S(1)}, f32[1,128,256]{2,1,0:T(8,128)S(1)}, u32[]{:S(2)}, u32[]{:S(2)}) %collective-permute-start.3) | collective-permute-done | bytes 131104 | tf_op jit(solution)/shard_map/ppermute | solution.py:24
  98.2 3.0 %collective-permute-done.4 = f32[1,128,256]{2,1,0:T(8,128)S(1)} collective-permute-done((f32[1,128,256]{2,1,0:T(8,128)S(1)}, f32[1,128,256]{2,1,0:T(8,128)S(1)}, u32[]{:S(2)}, u32[]{:S(2)}) %collective-permute-start.4) | collective-permute-done | bytes 131104 | tf_op jit(solution)/shard_map/ppermute | solution.py:21
  105.4 3.5 %collective-permute-done.5 = f32[1,128,256]{2,1,0:T(8,128)S(1)} collective-permute-done((f32[1,128,256]{2,1,0:T(8,128)S(1)}, f32[1,128,256]{2,1,0:T(8,128)S(1)}, u32[]{:S(2)}, u32[]{:S(2)}) %collective-permute-start.5) | collective-permute-done | bytes 131104 | tf_op jit(solution)/shard_map/ppermute | solution.py:24
  108.9 2.5 %collective-permute-done.6 = f32[1,128,256]{2,1,0:T(8,128)S(1)} collective-permute-done((f32[1,128,256]{2,1,0:T(8,128)S(1)}, f32[1,128,256]{2,1,0:T(8,128)S(1)}, u32[]{:S(2)}, u32[]{:S(2)}) %collective-permute-start.6) | collective-permute-done | bytes 131104 | tf_op jit(solution)/shard_map/ppermute | solution.py:21
  113.6 1.9 %collective-permute-start.8 = (f32[1,128,256]{2,1,0:T(8,128)S(1)}, f32[1,128,256]{2,1,0:T(8,128)S(1)}, u32[]{:S(2)}, u32[]{:S(2)}) collective-permute-start(f32[1,128,256]{2,1,0:T(8,128)S(1)} %get-tuple-element.27), channel_id=1, source_target_pairs={{0,8},{8,16},{16,24},{24,0},{1,9},{9,17},{17,25},{25,1},{2,10},{10... | collective-permute-start | bytes 393224 | tf_op jit(solution)/shard_map/ppermute | solution.py:21
  115.5 2.9 %collective-permute-done.7 = f32[1,128,256]{2,1,0:T(8,128)S(1)} collective-permute-done((f32[1,128,256]{2,1,0:T(8,128)S(1)}, f32[1,128,256]{2,1,0:T(8,128)S(1)}, u32[]{:S(2)}, u32[]{:S(2)}) %collective-permute-start.7) | collective-permute-done | bytes 131104 | tf_op jit(solution)/shard_map/ppermute | solution.py:24
  118.4 2.0 %collective-permute-done.8 = f32[1,128,256]{2,1,0:T(8,128)S(1)} collective-permute-done((f32[1,128,256]{2,1,0:T(8,128)S(1)}, f32[1,128,256]{2,1,0:T(8,128)S(1)}, u32[]{:S(2)}, u32[]{:S(2)}) %collective-permute-start.8) | collective-permute-done | bytes 131104 | tf_op jit(solution)/shard_map/ppermute | solution.py:21
  122.4 1.4 collective-permute-start.9
  124.5 2.9 %collective-permute-done.9 = f32[1,128,256]{2,1,0:T(8,128)S(1)} collective-permute-done((f32[1,128,256]{2,1,0:T(8,128)S(1)}, f32[1,128,256]{2,1,0:T(8,128)S(1)}, u32[]{:S(2)}, u32[]{:S(2)}) %collective-permute-start.9) | collective-permute-done | bytes 131104 | tf_op jit(solution)/shard_map/ppermute | solution.py:24
  127.4 3.2 %collective-permute-done.10 = f32[1,128,256]{2,1,0:T(8,128)S(1)} collective-permute-done((f32[1,128,256]{2,1,0:T(8,128)S(1)}, f32[1,128,256]{2,1,0:T(8,128)S(1)}, u32[]{:S(2)}, u32[]{:S(2)}) %collective-permute-start.10) | collective-permute-done | bytes 131104 | tf_op jit(solution)/shard_map/ppermute | solution.py:21
  130.6 2.4 %fusion.2 = f32[8,128,256]{2,1,0:T(8,128)} fusion(f32[8,128,256]{2,1,0:T(8,128)S(1)} %fusion.17, f32[1,128,256]{2,1,0:T(8,128)S(1)} %collective-permute-done.10, f32[1,128,256]{2,1,0:T(8,128)S(1)} %collective-permute-done.9, f32[8,1,256]{2,1,0:T(1,128)S(1)} %get-tuple-element.13, f32[8,127,256]{2,1,0:T(8,128)S(1)} %get-tuple-element.15, ...), kind=kLoop, calls=%fused_computation.6 | loop fusion | flops 4980736 | bytes 6553604 | tf_op jit(solution)/shard_map/mul | solution.py:100
  133.0 34.4 %all-reduce.2.cloned.1.call-done = f32[8,128,256]{2,1,0:T(8,128)} async-done(((f32[8,128,256]{2,1,0:T(8,128)}), f32[8,128,256]{2,1,0:T(8,128)}) %all-reduce.2.cloned.1.call-update) | async-done | bytes 1048592 | tf_op jit(solution)/shard_map/psum | solution.py:100
  167.5 2.4 %add_bitcast_fusion = f32[1,8,128,256]{3,2,1,0:T(8,128)} fusion(f32[8,128,256]{2,1,0:T(8,128)} %all-reduce.2.cloned.1.call-done, f32[8,128,256]{2,1,0:T(8,128)S(1)} %collective-permute-done.2, f32[1,8,128,256]{3,2,1,0:T(8,128)S(1)} %copy-done.2, pred[]{:T(512)S(6)} %eq.3), kind=kLoop, calls=%fused_computation.55 | loop fusion | flops 786432 | bytes 4194305 | tf_op jit(solution)/shard_map/broadcast_in_dim | solution.py:102
  (51 shorter events, 14.6 us)
Async XLA Ops:
  7.2 9.5 %copy-start = (f32[1,1,8,128,256]{4,3,2,1,0:T(8,128)S(1)}, f32[1,1,8,128,256]{4,3,2,1,0:T(8,128)}, u32[]{:S(2)}) copy-start(f32[1,1,8,128,256]{4,3,2,1,0:T(8,128)} %param.6) | copy-start | bytes 3145732
  7.2 49.0 %all-gather.3.cloned.1.call-start = ((), (), s32[]{:S(2)}) async-start(), calls=%async_computation.1 | async-start | bytes 5242880 | tf_op jit(solution)/shard_map/all_gather | solution.py:85
  8.3 9.0 %collective-permute-start = (f32[1,128,256]{2,1,0:T(8,128)S(1)}, f32[1,128,256]{2,1,0:T(8,128)S(1)}, u32[]{:S(2)}, u32[]{:S(2)}) collective-permute-start(f32[1,128,256]{2,1,0:T(8,128)S(1)} %get-tuple-element.48), channel_id=1, source_target_pairs={{8,0},{16,8},{24,16},{0,24},{9,1},{17,9},{25,17},{1,25},{10,2},{18... | collective-permute-start | bytes 393224 | tf_op jit(solution)/shard_map/ppermute | solution.py:24
  13.4 6.8 %collective-permute-start.1 = (f32[1,128,256]{2,1,0:T(8,128)S(1)}, f32[1,128,256]{2,1,0:T(8,128)S(1)}, u32[]{:S(2)}, u32[]{:S(2)}) collective-permute-start(f32[1,128,256]{2,1,0:T(8,128)S(1)} %get-tuple-element.49), channel_id=1, source_target_pairs={{0,8},{8,16},{16,24},{24,0},{1,9},{9,17},{17,25},{25,1},{2,10},{10... | collective-permute-start | bytes 393224 | tf_op jit(solution)/shard_map/ppermute | solution.py:21
  20.2 36.0 %copy-start.3 = (f32[4]{0:T(128)S(1)}, f32[4]{0:T(128)}, u32[]{:S(2)}) copy-start(f32[4]{0:T(128)} %constant.30.clone) | copy-start | bytes 52
  22.4 37.8 %copy-start.2 = (f32[1,8,128,256]{3,2,1,0:T(8,128)S(1)}, f32[1,8,128,256]{3,2,1,0:T(8,128)}, u32[]{:S(2)}) copy-start(f32[1,8,128,256]{3,2,1,0:T(8,128)} %param.5) | copy-start | bytes 3145732
  22.4 145.1 %all-reduce.2.cloned.1.call-start = ((), (), s32[]{:S(2)}) async-start(), calls=%async_computation | async-start | bytes 2097152 | tf_op jit(solution)/shard_map/psum | solution.py:100
  56.1 9.3 %copy-start.4 = (f32[4]{0:T(128)S(1)}, f32[4]{0:T(128)}, u32[]{:S(2)}) copy-start(f32[4]{0:T(128)} %constant.29.clone) | copy-start | bytes 52
  61.3 26.5 %collective-permute-start.2 = (f32[8,128,256]{2,1,0:T(8,128)}, f32[8,128,256]{2,1,0:T(8,128)S(1)}, u32[]{:S(2)}, u32[]{:S(2)}) collective-permute-start(f32[8,128,256]{2,1,0:T(8,128)} %bitcast_add_fusion), channel_id=1, source_target_pairs={{0,1},{2,3},{4,5},{6,7},{8,9},{10,11},{12,13},{14,15},{16,17},{18,... | collective-permute-start | bytes 3145736 | tf_op jit(solution)/shard_map/ppermute | solution.py:32
  91.1 7.1 %collective-permute-start.3 = (f32[1,128,256]{2,1,0:T(8,128)S(1)}, f32[1,128,256]{2,1,0:T(8,128)S(1)}, u32[]{:S(2)}, u32[]{:S(2)}) collective-permute-start(f32[1,128,256]{2,1,0:T(8,128)S(1)} %get-tuple-element.46), channel_id=1, source_target_pairs={{8,0},{16,8},{24,16},{0,24},{9,1},{17,9},{25,17},{1,25},{10,2},{18... | collective-permute-start | bytes 393224 | tf_op jit(solution)/shard_map/ppermute | solution.py:24
  94.5 6.8 %collective-permute-start.4 = (f32[1,128,256]{2,1,0:T(8,128)S(1)}, f32[1,128,256]{2,1,0:T(8,128)S(1)}, u32[]{:S(2)}, u32[]{:S(2)}) collective-permute-start(f32[1,128,256]{2,1,0:T(8,128)S(1)} %get-tuple-element.47), channel_id=1, source_target_pairs={{0,8},{8,16},{16,24},{24,0},{1,9},{9,17},{17,25},{25,1},{2,10},{10... | collective-permute-start | bytes 393224 | tf_op jit(solution)/shard_map/ppermute | solution.py:21
  103.3 5.6 %collective-permute-start.5 = (f32[1,128,256]{2,1,0:T(8,128)S(1)}, f32[1,128,256]{2,1,0:T(8,128)S(1)}, u32[]{:S(2)}, u32[]{:S(2)}) collective-permute-start(f32[1,128,256]{2,1,0:T(8,128)S(1)} %get-tuple-element.36), channel_id=1, source_target_pairs={{8,0},{16,8},{24,16},{0,24},{9,1},{17,9},{25,17},{1,25},{10,2},{18... | collective-permute-start | bytes 393224 | tf_op jit(solution)/shard_map/ppermute | solution.py:24
  104.6 6.8 %collective-permute-start.6 = (f32[1,128,256]{2,1,0:T(8,128)S(1)}, f32[1,128,256]{2,1,0:T(8,128)S(1)}, u32[]{:S(2)}, u32[]{:S(2)}) collective-permute-start(f32[1,128,256]{2,1,0:T(8,128)S(1)} %get-tuple-element.37), channel_id=1, source_target_pairs={{0,8},{8,16},{16,24},{24,0},{1,9},{9,17},{17,25},{25,1},{2,10},{10... | collective-permute-start | bytes 393224 | tf_op jit(solution)/shard_map/ppermute | solution.py:21
  113.4 5.0 %collective-permute-start.7 = (f32[1,128,256]{2,1,0:T(8,128)S(1)}, f32[1,128,256]{2,1,0:T(8,128)S(1)}, u32[]{:S(2)}, u32[]{:S(2)}) collective-permute-start(f32[1,128,256]{2,1,0:T(8,128)S(1)} %get-tuple-element.26), channel_id=1, source_target_pairs={{8,0},{16,8},{24,16},{0,24},{9,1},{17,9},{25,17},{1,25},{10,2},{18... | collective-permute-start | bytes 393224 | tf_op jit(solution)/shard_map/ppermute | solution.py:24
  113.6 6.8 %collective-permute-start.8 = (f32[1,128,256]{2,1,0:T(8,128)S(1)}, f32[1,128,256]{2,1,0:T(8,128)S(1)}, u32[]{:S(2)}, u32[]{:S(2)}) collective-permute-start(f32[1,128,256]{2,1,0:T(8,128)S(1)} %get-tuple-element.27), channel_id=1, source_target_pairs={{0,8},{8,16},{16,24},{24,0},{1,9},{9,17},{17,25},{25,1},{2,10},{10... | collective-permute-start | bytes 393224 | tf_op jit(solution)/shard_map/ppermute | solution.py:21
  121.6 9.0 %copy-start.1 = (f32[8,128,256]{2,1,0:T(8,128)}, f32[8,128,256]{2,1,0:T(8,128)S(1)}, u32[]{:S(2)}) copy-start(f32[8,128,256]{2,1,0:T(8,128)S(1)} %fusion.17) | copy-start | bytes 3145732
  122.4 5.0 %collective-permute-start.9 = (f32[1,128,256]{2,1,0:T(8,128)S(1)}, f32[1,128,256]{2,1,0:T(8,128)S(1)}, u32[]{:S(2)}, u32[]{:S(2)}) collective-permute-start(f32[1,128,256]{2,1,0:T(8,128)S(1)} %get-tuple-element.16), channel_id=1, source_target_pairs={{8,0},{16,8},{24,16},{0,24},{9,1},{17,9},{25,17},{1,25},{10,2},{18... | collective-permute-start | bytes 393224 | tf_op jit(solution)/shard_map/ppermute | solution.py:24
  123.8 6.8 %collective-permute-start.10 = (f32[1,128,256]{2,1,0:T(8,128)S(1)}, f32[1,128,256]{2,1,0:T(8,128)S(1)}, u32[]{:S(2)}, u32[]{:S(2)}) collective-permute-start(f32[1,128,256]{2,1,0:T(8,128)S(1)} %get-tuple-element.17), channel_id=1, source_target_pairs={{0,8},{8,16},{16,24},{24,0},{1,9},{9,17},{17,25},{25,1},{2,10},{10... | collective-permute-start | bytes 393224 | tf_op jit(solution)/shard_map/ppermute | solution.py:21
Sparse Core Ops, SparseCore 0:
  22.5 33.5 all-gather.2
  133.2 34.2 all-reduce.1
where the time goes:
time: 177 us
  waiting for transfers between devices  116 us (66%)
  other arithmetic  18.3 us (10%)
  starting transfers between devices  18.2 us (10%)
  between operations  14.8 us (8%)
  local copies, waits for them, and re-layouts  9.72 us (5%)
    psum x1, waiting for transfers between devices, on_device(): weighted_new = lax.psum(node_weight * force_new, 'node')  34.4 us
    all_gather x1, waiting for transfers between devices, on_device(): shard_piece = lax.all_gather(force_old[None], 'node', axis=0, tiled=True)  32.9 us
    ppermute x1, waiting for transfers between devices, shifted_2(): return lax.ppermute(array, axis, pairs)  21.3 us
    ppermute x5, waiting for transfers between devices, padded_2(): lax.ppermute(lax.slice_in_dim(block, block.shape[dim] - width, None, axis...  13.5 us
    ppermute x5, waiting for transfers between devices, padded_2(): lax.ppermute(lax.slice_in_dim(block, 0, width, axis=dim), axis, backward)  13.5 us
    ppermute x5, starting transfers between devices, padded_2(): lax.ppermute(lax.slice_in_dim(block, 0, width, axis=dim), axis, backward)  11.4 us
    div x4, other arithmetic, on_device(): iterate = (right_side + implicit * neighbour_sum(widened)) / divisor  6.12 us
    slice x10, local copies, waits for them, and re-layouts, neighbour_sum(): total = total + jnp.roll(inner, -1, 2) + jnp.roll(inner, 1, 2)  5.53 us
  transfers between devices with their start and end apart: 13, of which 13 were waited for; matrix products, arithmetic and copies ran while one was open for 3% of the time, Pallas kernels for 0%

commit v1 on v0

v1 whole, which is shorter than its diff:
```python
import functools

import jax
import jax.numpy as jnp
import numpy as np
from jax import lax
from jax.experimental import pallas as pl
from jax.experimental.pallas import tpu as pltpu
from jax.sharding import PartitionSpec as P

NODES = 4
PASSES = 4
DEPTH = PASSES + 1

time_step = 0.25
diffusion = 4.0
reaction = 1.0

F32 = jnp.float32


def collocation(count):
    points = [-0.8611363115940526, -0.3399810435848563, 0.3399810435848563, 0.8611363115940526]
    raw_weights = [0.3478548451374538, 0.6521451548625461, 0.6521451548625461, 0.3478548451374538]
    node_times = [(point + 1.0) / 2.0 for point in points]
    quadrature = [[0.0 for column in range(count)] for target in range(count)]
    for source in range(count):
        coeffs = [1.0]
        scaling = 1.0
        for other in range(count):
            if other != source:
                other_time = node_times[other]
                shifted = [0.0] + coeffs
                for power in range(len(coeffs)):
                    shifted[power] = shifted[power] - other_time * coeffs[power]
                coeffs = shifted
                scaling = scaling * (node_times[source] - other_time)
        for target in range(count):
            target_time = node_times[target]
            integral = 0.0
            for power in range(len(coeffs)):
                integral = integral + coeffs[power] * target_time ** (power + 1) / (power + 1)
            quadrature[target][source] = integral / scaling
    return (node_times, quadrature, [weight / 2.0 for weight in raw_weights])


LIN, CUB, WEIGHT, MIX, SCALE, FIRST, CORE, COUNT = 0, 8, 16, 20, 22, 24, 25, 26


def scalar_table():
    times, quad, weights = collocation(NODES)
    table = np.zeros((NODES, COUNT), np.float64)
    for node in range(NODES):
        sources = [node, node ^ 2, node ^ 1, node ^ 3]
        for place, target in enumerate([node, node ^ 2]):
            implicit = time_step * diffusion * times[target]
            for index, source in enumerate(sources):
                lin = time_step * diffusion * quad[target][source]
                table[node, LIN + 4 * place + index] = lin - (implicit if source == target else 0.0)
                table[node, CUB + 4 * place + index] = time_step * reaction * quad[target][source]
            table[node, MIX + place] = implicit / (1.0 + 6.0 * implicit)
            table[node, SCALE + place] = 1.0 / (1.0 + 6.0 * implicit)
        for index, source in enumerate(sources):
            table[node, WEIGHT + index] = weights[source]
        table[node, CORE] = node & 1
    return table.astype(np.float32)


def flat_sum(plane):
    rows, columns = plane.shape
    vertical = pltpu.roll(plane, 1, 0) + pltpu.roll(plane, rows - 1, 0)
    return vertical + (pltpu.roll(plane, 1, 1) + pltpu.roll(plane, columns - 1, 1))


def mixed(scalars, base, planes):
    own, across, beside, corner = (scalars[base + index] * plane for index, plane in enumerate(planes))
    return (own + across) + (beside + corner)


def joined(core, mine, other):
    return jnp.where(core, other, mine), jnp.where(core, mine, other)


def end_kernel(upper, scalars, own, across, beside, corner, start, out, total):
    shift = 3 if upper else 0
    half = out.shape[1]
    core = scalars[CORE] > 0.5

    def gathered(plane):
        return [ref[plane] for ref in (own, across, beside, corner)]

    for plane in range(5):
        total[plane] = mixed(scalars, WEIGHT, gathered(plane))
    for place in range(5):
        plane = place + 4 if upper else place - 1
        if plane in (-1, 8):
            value = (time_step * diffusion) * total[0 if plane < 0 else 4]
        else:
            middle = total[plane - shift]
            around = flat_sum(middle)
            if plane + 1 < 8:
                around = around + total[plane + 1 - shift]
            if plane > 0:
                around = around + total[plane - 1 - shift]
            states = gathered(plane - shift)
            local = mixed(scalars, WEIGHT, [state - state * state * state for state in states])
            force = diffusion * (around - 6.0 * middle) + reaction * local
            value = start[plane - shift] + time_step * force
        out[place] = jnp.where(core, value[half:], value[:half])


def sweep_kernel(scalars, *refs):
    names = ["own", "across_a", "across_b", "beside", "corner_a", "corner_b"]
    names += [f"{side}{part}_{who}" for side in ("low", "high") for part in "ab" for who in ("own", "across", "beside", "corner")]
    names += ["start", "start_low", "start_low_", "start_high", "start_high_"]
    names += [f"{kind}{end}" for kind in ("end_low", "end_high", "above_low", "below_high") for end in ("", "_")]
    names += ["out", "share", "x_own", "x_across", "y_own", "y_across", "r_own", "r_across", "begin"]
    r = dict(zip(names, refs, strict=True))
    slab = r["own"].shape[0]
    core = scalars[CORE] > 0.5
    first = scalars[FIRST]
    half = r["start_low"].shape[1]
    edge = DEPTH

    begin = r["begin"]

    def put(place, value_low, value_high):
        begin[place, :half] = value_low
        begin[place, half:] = value_high

    def both(name, index):
        return joined(core, r[name][index], r[name + "_"][index])

    def add(first_pair, second_pair):
        return first_pair[0] + second_pair[0], first_pair[1] + second_pair[1]

    for index in range(4):
        pair = add(both("start_low", index), both("below_high", index))
        if index == 3:
            pair = add(pair, both("end_low", 0))
        put(index, *pair)
        pair = add(both("start_high", index), both("above_low", index + 1))
        if index == 0:
            pair = add(pair, both("end_high", 4))
        put(index + 12, *pair)
        pair = both("end_low", index + 1)
        if index == 0:
            pair = add(pair, both("below_high", 4))
        mine = first * r["start"][index]
        put(index + 4, *add(pair, (mine[:half], mine[half:])))
        pair = both("end_high", index)
        if index == 3:
            pair = add(pair, both("above_low", 0))
        mine = first * r["start"][index + 4]
        put(index + 8, *add(pair, (mine[:half], mine[half:])))

    def pointwise(place, count, sources, offset):
        def body(index, carry):
            states = [source[offset[number] + index] for number, source in enumerate(sources)]
            local = [state - state * state * state for state in states]
            r["x_own"][place + index] = states[0]
            r["x_across"][place + index] = states[1]
            r["y_own"][place + index] = mixed(scalars, LIN, states)
            r["y_across"][place + index] = mixed(scalars, LIN + 4, states)
            r["r_own"][place + index] = mixed(scalars, CUB, local)
            r["r_across"][place + index] = mixed(scalars, CUB + 4, local)
            return carry

        lax.fori_loop(0, count, body, 0)

    who = ("own", "across", "beside", "corner")
    pointwise(0, 2, [r["lowb_" + name] for name in who], (0,) * 4)
    pointwise(2, 3, [r["lowa_" + name] for name in who], (0,) * 4)
    pointwise(edge, 5, [r["own"], r["across_a"], r["beside"], r["corner_a"]], (0,) * 4)
    pointwise(edge + 5, 3, [r["own"], r["across_b"], r["beside"], r["corner_b"]], (5, 0, 5, 0))
    pointwise(edge + slab, 3, [r["higha_" + name] for name in who], (0,) * 4)
    pointwise(edge + slab + 3, 2, [r["highb_" + name] for name in who], (0,) * 4)

    def grouped(low, high, group, step):
        count = (high - low) // group

        def body(index, carry):
            for member in range(group):
                step(low + index * group + member)
            return carry

        lax.fori_loop(0, count, body, 0)
        for place in range(low + count * group, high):
            step(place)

    def around(ref, place):
        return (ref[place + 1] + ref[place - 1]) + flat_sum(ref[place])

    def right(place):
        for index, name in enumerate(("own", "across")):
            potential = r["y_" + name]
            value = (around(potential, place) - 6.0 * potential[place]) + r["r_" + name][place]
            r["r_" + name][place] = scalars[SCALE + index] * (value + begin[place - 1])

    grouped(1, 2 * edge + slab - 1, 4, right)

    for step_index in range(PASSES):
        source, target = ("x_", "y_") if step_index % 2 == 0 else ("y_", "x_")

        def relax(place, source=source, target=target):
            for index, name in enumerate(("own", "across")):
                value = scalars[MIX + index] * around(r[source + name], place)
                r[target + name][place] = r["r_" + name][place] + value

        grouped(1 + step_index, 2 * edge + slab - 1 - step_index, 4, relax)

    final, spare = ("x_", "y_") if PASSES % 2 == 0 else ("y_", "x_")
    weights = (scalars[WEIGHT], scalars[WEIGHT + 1])

    def weigh(place):
        r[spare + "own"][place] = weights[0] * r[final + "own"][place] + weights[1] * r[final + "across"][place]

    grouped(edge - 1, edge + slab + 1, 5, weigh)

    def finish(place):
        total = r[spare + "own"]
        states = [r[final + name][place] for name in ("own", "across")]
        local = [state - state * state * state for state in states]
        force = diffusion * (around(total, place) - 6.0 * total[place])
        force = force + reaction * (weights[0] * local[0] + weights[1] * local[1])
        r["out"][place - edge] = states[0]
        r["share"][place - edge] = time_step * force + 0.5 * begin[place - 1]

    grouped(edge, edge + slab, 4, finish)


def in_vmem(count):
    return [pl.BlockSpec(memory_space=pltpu.SMEM)] + [pl.BlockSpec(memory_space=pltpu.VMEM)] * count


def end_call(upper, scalars, sources, start):
    planes, rows, columns = sources[0].shape
    return pl.pallas_call(
        functools.partial(end_kernel, upper),
        out_shape=jax.ShapeDtypeStruct((5, rows // 2, columns), F32),
        in_specs=in_vmem(5),
        out_specs=pl.BlockSpec(memory_space=pltpu.VMEM),
        scratch_shapes=[pltpu.VMEM((5, rows, columns), F32)],
        compiler_params=pltpu.CompilerParams(vmem_limit_bytes=16 << 20),
        cost_estimate=pl.CostEstimate(flops=5 * rows * columns * 40, bytes_accessed=30 * rows * columns * 4, transcendentals=0),
    )(scalars, *sources, start)


def sweep_call(scalars, operands, shape):
    slab, rows, columns = shape
    wide = pltpu.VMEM((slab + 2 * DEPTH, rows, columns), F32)
    return pl.pallas_call(
        sweep_kernel,
        out_shape=[jax.ShapeDtypeStruct(shape, F32)] * 2,
        in_specs=in_vmem(len(operands)),
        out_specs=[pl.BlockSpec(memory_space=pltpu.VMEM)] * 2,
        scratch_shapes=[wide] * 6 + [pltpu.VMEM((slab + 2 * DEPTH - 2, rows, columns), F32)],
        compiler_params=pltpu.CompilerParams(vmem_limit_bytes=40 << 20),
        cost_estimate=pl.CostEstimate(flops=200 * rows * columns * 20, bytes_accessed=300 * rows * columns * 4, transcendentals=0),
    )(scalars, *operands)


def on_device(start_old, nodes_old):
    slabs, slices = lax.axis_size("space"), lax.axis_size("tm")
    node_index = lax.axis_index("node")
    slice_index = lax.axis_index("tm")
    state, start = nodes_old[0, 0], start_old[0]
    slab, rows, columns = state.shape
    half = rows // 2
    core = lax.rem(node_index, 2)
    scalars = jnp.asarray(scalar_table())[node_index]
    scalars = scalars.at[FIRST].set((slice_index == 0).astype(F32))

    def across(array):
        return lax.ppermute(array, "node", [(node, node ^ 2) for node in range(NODES)])

    def beside(array):
        return lax.ppermute(array, "node", [(node, node ^ 1) for node in range(NODES)])

    def along(array, by):
        return lax.ppermute(array, "space", [(slab_, (slab_ + by) % slabs) for slab_ in range(slabs)])

    def onward(array, by, source=None):
        if source is None:
            steps = [(slice_, slice_ + 1) for slice_ in range(slices - 1)]
        else:
            steps = [(0, 0)]
        pairs = [
            (slab_ * slices + here, ((slab_ + by) % slabs) * slices + there) for slab_ in range(slabs) for here, there in steps
        ]
        return lax.ppermute(array, ("space", "tm"), pairs)

    across_a = across(state[:5])
    across_b = across(state[5:])
    low_a, high_a = along(state[5:], 1), along(state[:3], -1)
    low_b, high_b = along(state[3:5], 1), along(state[3:5], -1)
    own_beside = beside(state)
    halo = {"lowa": low_a, "lowb": low_b, "higha": high_a, "highb": high_b}
    far = {name: across(array) for name, array in halo.items()}

    corner_a, corner_b = beside(across_a), beside(across_b)
    middle = jnp.concatenate([across_a[3:], across_b], axis=0)
    corner_middle = jnp.concatenate([corner_a[3:], corner_b], axis=0)
    end_low = end_call(False, scalars, [state[:5], across_a, own_beside[:5], corner_a], start[:5])
    end_high = end_call(True, scalars, [state[3:], middle, own_beside[3:], corner_middle], start[3:])
    got = {
        "end_low": onward(end_low, 0),
        "end_high": onward(end_high, 0),
        "above_low": onward(end_low, -1),
        "below_high": onward(end_high, 1),
    }
    mine = lax.dynamic_slice_in_dim(start, core * half, half, axis=1)
    start_low = onward(mine[4:], 1, source=0)
    start_high = onward(mine[:4], -1, source=0)

    operands = [state, across_a, across_b, own_beside, corner_a, corner_b]
    for name in ("lowa", "lowb", "higha", "highb"):
        operands += [halo[name], far[name], beside(halo[name]), beside(far[name])]
    operands += [start, start_low, beside(start_low), start_high, beside(start_high)]
    for name in ("end_low", "end_high", "above_low", "below_high"):
        operands += [got[name], beside(got[name])]
    state_new, share = sweep_call(scalars, operands, state.shape)
    end_new = share + beside(share)
    return (state_new[None, None], end_new[None])


def solution(mesh):
    return jax.shard_map(
        on_device,
        mesh=mesh,
        in_specs=(P("tm", "space", None, None), P("tm", "node", "space", None, None)),
        out_specs=(P("tm", "node", "space", None, None), P("tm", "space", None, None)),
        check_vma=False,
    )
```

time: 177 us -> 138 us (0.78)
  waiting for transfers between devices: 116 us -> 64.5 us
  Pallas kernels: 0 us -> 23.3 us
  starting transfers between devices: 18.2 us -> 35.4 us
  other arithmetic: 18.3 us -> 3.36 us
  between operations: 14.8 us -> 1.03 us
    psum x1 -> x0, waiting for transfers between devices: 34.4 us -> none  [on_device(): weighted_new = lax.psum(node_weight * force_new, 'node')]
    all_gather x1 -> x0, waiting for transfers between devices: 32.9 us -> none  [on_device(): shard_piece = lax.all_gather(force_old[None], 'node', axis=0, tiled=True)]
    pallas_call x0 -> x3, Pallas kernels: none -> 23.3 us  [the longest x1 20.5 us: sweep_call(): pl.pallas_call(sweep_kernel, out_shape=[jax.ShapeDtypeStruct(shape, F32)]...]
    ppermute x11 -> x34, starting transfers between devices: 18.2 us -> 35.4 us  [the longest x6 15.1 us: onward(): return lax.ppermute(array, ('space', 'tm'), pairs)]
    ppermute x11 -> x34, waiting for transfers between devices: 48.3 us -> 64.5 us  [the longest x6 23.7 us: onward(): return lax.ppermute(array, ('space', 'tm'), pairs)]
    div x4 -> x0, other arithmetic: 6.12 us -> none  [on_device(): iterate = (right_side + implicit * neighbour_sum(widened)) / divisor]
    unnamed x10 -> x54, local copies, waits for them, and re-layouts: 0.02 us -> 5.43 us
    slice x25 -> x8, local copies, waits for them, and re-layouts: 7.72 us -> 3.6 us  [the longest x1 1.24 us: on_device(): start[3:]]
  transfers between devices with their start and end apart: 13 -> 34, of which waited for: 13 -> 13; matrix products, arithmetic and copies ran while one was open for 3% -> 4% of each run, Pallas kernels for 0% -> 2%
where the time goes in v1:
time: 138 us; the launch traced here: 137 us
  waiting for transfers between devices  64.5 us (47%)
  starting transfers between devices  35.4 us (26%)
  Pallas kernels  23.3 us (17%)
  local copies, waits for them, and re-layouts  9.74 us (7%)
  other arithmetic  3.36 us (2%)
    ppermute x6, waiting for transfers between devices, onward(): return lax.ppermute(array, ('space', 'tm'), pairs)  23.7 us
    ppermute x4, waiting for transfers between devices, along(): lax.ppermute(array, 'space', [(slab_, (slab_ + by) % slabs) for slab_ in...  20.9 us
    pallas_call x1, Pallas kernels, sweep_call(): pl.pallas_call(sweep_kernel, out_shape=[jax.ShapeDtypeStruct(shape, F32)]...  20.5 us
    ppermute x6, waiting for transfers between devices, across(): lax.ppermute(array, 'node', [(node, node ^ 2) for node in range(NODES)])  15.7 us
    ppermute x6, starting transfers between devices, onward(): return lax.ppermute(array, ('space', 'tm'), pairs)  15.1 us
    ppermute x4, starting transfers between devices, along(): lax.ppermute(array, 'space', [(slab_, (slab_ + by) % slabs) for slab_ in...  9.23 us
    ppermute x6, starting transfers between devices, across(): lax.ppermute(array, 'node', [(node, node ^ 2) for node in range(NODES)])  7.55 us
    unnamed x54, local copies, waits for them, and re-layouts  5.43 us
  transfers between devices with their start and end apart: 34, of which 13 were waited for; matrix products, arithmetic and copies ran while one was open for 4% of the time, Pallas kernels for 2%

profile of v1, /device:TPU:0, one launch (start us, length us, event | category | flops | bytes accessed | tf_op | source)
XLA Modules:
  0.0 137.3 jit_solution(12473726769096120463)
XLA Ops:
  1.8 4.9 %collective-permute-start.21 = (f32[4,64,256]{2,1,0:T(8,128)S(1)}, f32[4,64,256]{2,1,0:T(8,128)S(1)}, u32[]{:S(2)}, u32[]{:S(2)}) collective-permute-start(f32[4,64,256]{2,1,0:T(8,128)S(1)} %get-tuple-element.25), channel_id=1, source_target_pairs={{0,8},{8,16},{16,24},{24,0},{2,10},{10,18},{18,26},{26,2},{4,12},{... | collective-permute-start | bytes 786440 | tf_op jit(solution)/shard_map/ppermute | solution.py:291
  6.8 3.9 %collective-permute-start.23 = (f32[4,64,256]{2,1,0:T(8,128)S(1)}, f32[4,64,256]{2,1,0:T(8,128)S(1)}, u32[]{:S(2)}, u32[]{:S(2)}) collective-permute-start(f32[4,64,256]{2,1,0:T(8,128)S(1)} %get-tuple-element.24), channel_id=1, source_target_pairs={{0,24},{8,0},{16,8},{24,16},{2,26},{10,2},{18,10},{26,18},{4,28},{... | collective-permute-start | bytes 786440 | tf_op jit(solution)/shard_map/ppermute | solution.py:291
  10.8 1.8 %collective-permute-start.1 = (f32[3,128,256]{2,1,0:T(8,128)S(1)}, f32[3,128,256]{2,1,0:T(8,128)}, u32[]{:S(2)}, u32[]{:S(2)}) collective-permute-start(f32[3,128,256]{2,1,0:T(8,128)S(1)} %get-tuple-element.27), channel_id=1, source_target_pairs={{0,4},{2,6},{4,0},{6,2},{1,5},{3,7},{5,1},{7,3},{8,12},{10,14},{12... | collective-permute-start | bytes 1179656 | tf_op jit(solution)/shard_map/ppermute | solution.py:275
  12.6 1.4 %collective-permute-start.9 = (f32[2,128,256]{2,1,0:T(8,128)S(1)}, f32[2,128,256]{2,1,0:T(8,128)S(1)}, u32[]{:S(2)}, u32[]{:S(2)}) collective-permute-start(f32[2,128,256]{2,1,0:T(8,128)S(1)} %slice_bitcast_fusion.6), channel_id=1, source_target_pairs={{0,8},{8,16},{16,24},{24,0},{1,9},{9,17},{17,25},{25,1},{2,10},{10... | collective-permute-start | bytes 786440 | tf_op jit(solution)/shard_map/ppermute | solution.py:281
  14.0 1.9 %collective-permute-done.21.refs_23_ = f32[4,64,256]{2,1,0:T(8,128)S(1)} collective-permute-done((f32[4,64,256]{2,1,0:T(8,128)S(1)}, f32[4,64,256]{2,1,0:T(8,128)S(1)}, u32[]{:S(2)}, u32[]{:S(2)}) %collective-permute-start.21) | collective-permute-done | bytes 262176 | tf_op jit(solution)/shard_map/ppermute | solution.py:291
  16.0 7.5 %collective-permute-start.17 = (f32[2,128,256]{2,1,0:T(8,128)S(1)}, f32[2,128,256]{2,1,0:T(8,128)S(1)}, u32[]{:S(2)}, u32[]{:S(2)}) collective-permute-start(f32[2,128,256]{2,1,0:T(8,128)S(1)} %slice_bitcast_fusion.6), channel_id=1, source_target_pairs={{0,24},{8,0},{16,8},{24,16},{1,25},{9,1},{17,9},{25,17},{2,26},{10... | collective-permute-start | bytes 786440 | tf_op jit(solution)/shard_map/ppermute | solution.py:281
  24.7 10.9 %collective-permute-done.9.refs_10_ = f32[2,128,256]{2,1,0:T(8,128)S(1)} collective-permute-done((f32[2,128,256]{2,1,0:T(8,128)S(1)}, f32[2,128,256]{2,1,0:T(8,128)S(1)}, u32[]{:S(2)}, u32[]{:S(2)}) %collective-permute-start.9) | collective-permute-done | bytes 262176 | tf_op jit(solution)/shard_map/ppermute | solution.py:281
  35.7 1.7 %collective-permute-start = (f32[5,128,256]{2,1,0:T(8,128)S(1)}, f32[5,128,256]{2,1,0:T(8,128)S(1)}, u32[]{:S(2)}, u32[]{:S(2)}) collective-permute-start(f32[5,128,256]{2,1,0:T(8,128)S(1)} %get-tuple-element.23.own), channel_id=1, source_target_pairs={{0,4},{2,6},{4,0},{6,2},{1,5},{3,7},{5,1},{7,3},{8,12},{10,14},{12... | collective-permute-start | bytes 1966088 | tf_op jit(solution)/shard_map/ppermute | solution.py:275
  38.2 2.2 %collective-permute-done.17.refs_18_ = f32[2,128,256]{2,1,0:T(8,128)S(1)} collective-permute-done((f32[2,128,256]{2,1,0:T(8,128)S(1)}, f32[2,128,256]{2,1,0:T(8,128)S(1)}, u32[]{:S(2)}, u32[]{:S(2)}) %collective-permute-start.17) | collective-permute-done | bytes 262176 | tf_op jit(solution)/shard_map/ppermute | solution.py:281
  41.1 7.7 %collective-permute-done.13.refs_14_ = f32[3,128,256]{2,1,0:T(8,128)S(1)} collective-permute-done((f32[3,128,256]{2,1,0:T(8,128)S(1)}, f32[3,128,256]{2,1,0:T(8,128)S(1)}, u32[]{:S(2)}, u32[]{:S(2)}) %collective-permute-start.13) | collective-permute-done | bytes 393248 | tf_op jit(solution)/shard_map/ppermute | solution.py:281
  48.8 1.5 %collective-permute-start.10 = (f32[2,128,256]{2,1,0:T(8,128)S(1)}, f32[2,128,256]{2,1,0:T(8,128)}, u32[]{:S(2)}, u32[]{:S(2)}) collective-permute-start(f32[2,128,256]{2,1,0:T(8,128)S(1)} %collective-permute-done.9.refs_10_), channel_id=1, source_target_pairs={{0,4},{2,6},{4,0},{6,2},{1,5},{3,7},{5,1},{7,3},{8,12},{10,14},{12... | collective-permute-start | bytes 786440 | tf_op jit(solution)/shard_map/ppermute | solution.py:275
  53.0 5.1 %collective-permute-done.10.refs_11_ = f32[2,128,256]{2,1,0:T(8,128)} collective-permute-done((f32[2,128,256]{2,1,0:T(8,128)S(1)}, f32[2,128,256]{2,1,0:T(8,128)}, u32[]{:S(2)}, u32[]{:S(2)}) %collective-permute-start.10) | collective-permute-done | bytes 262176 | tf_op jit(solution)/shard_map/ppermute | solution.py:275
  59.3 3.4 %collective-permute-done.18.refs_19_ = f32[2,128,256]{2,1,0:T(8,128)S(1)} collective-permute-done((f32[2,128,256]{2,1,0:T(8,128)S(1)}, f32[2,128,256]{2,1,0:T(8,128)S(1)}, u32[]{:S(2)}, u32[]{:S(2)}) %collective-permute-start.18) | collective-permute-done | bytes 262176 | tf_op jit(solution)/shard_map/ppermute | solution.py:275
  63.4 1.5 %collective-permute-start.6 = (f32[3,128,256]{2,1,0:T(8,128)}, f32[3,128,256]{2,1,0:T(8,128)}, u32[]{:S(2)}, u32[]{:S(2)}) collective-permute-start(f32[3,128,256]{2,1,0:T(8,128)} %collective-permute-done.5.refs_6_), channel_id=1, source_target_pairs={{0,4},{2,6},{4,0},{6,2},{1,5},{3,7},{5,1},{7,3},{8,12},{10,14},{12... | collective-permute-start | bytes 1179656 | tf_op jit(solution)/shard_map/ppermute | solution.py:275
  69.8 5.8 %collective-permute-done.6.refs_7_ = f32[3,128,256]{2,1,0:T(8,128)} collective-permute-done((f32[3,128,256]{2,1,0:T(8,128)}, f32[3,128,256]{2,1,0:T(8,128)}, u32[]{:S(2)}, u32[]{:S(2)}) %collective-permute-start.6) | collective-permute-done | bytes 393248 | tf_op jit(solution)/shard_map/ppermute | solution.py:275
  77.8 1.4 %shard_map.51 = f32[5,64,256]{2,1,0:T(8,128)S(1)} custom-call(f32[26]{0:T(128)S(1)} %constant_dynamic-update-slice_fusion.scalars, f32[5,128,256]{2,1,0:T(8,128)S(1)} %copy-done.3, f32[5,128,256]{2,1,0:T(8,128)S(1)} %pad_maximum_fusion.across, f32[5,128,256]{2,1,0:T(8,128)S(1)} %get-tuple-element.20.beside, f32[5,128,256]{2,1,0:T(8,128)S(1)} %pad_maximum_fusion.1.corner, ...), custom_call_target="tpu_custom_call" | custom-call | flops 6553600 | bytes 3932160 | tf_op jit(solution)/shard_map/pallas_call | solution.py:238
  79.3 1.4 %shard_map.50 = f32[5,64,256]{2,1,0:T(8,128)S(1)} custom-call(f32[26]{0:T(128)S(1)} %constant_dynamic-update-slice_fusion.scalars, f32[5,128,256]{2,1,0:T(8,128)S(1)} %copy-done.2, f32[5,128,256]{2,1,0:T(8,128)S(1)} %collective-permute-done.across.refs_1_, f32[5,128,256]{2,1,0:T(8,128)S(1)} %get-tuple-element.21.beside, ...), custom_call_target="tpu_custom_call" | custom-call | flops 6553600 | bytes 3932160 | tf_op jit(solution)/shard_map/pallas_call | solution.py:238
  80.7 1.3 collective-permute-start.27
  82.0 1.5 %collective-permute-done.14.refs_15_ = f32[3,128,256]{2,1,0:T(8,128)S(1)} collective-permute-done((f32[3,128,256]{2,1,0:T(8,128)S(1)}, f32[3,128,256]{2,1,0:T(8,128)S(1)}, u32[]{:S(2)}, u32[]{:S(2)}) %collective-permute-start.14) | collective-permute-done | bytes 393248 | tf_op jit(solution)/shard_map/ppermute | solution.py:275
  86.1 2.3 %collective-permute-start.29 = (f32[5,64,256]{2,1,0:T(8,128)S(1)}, f32[5,64,256]{2,1,0:T(8,128)S(1)}, u32[]{:S(2)}, u32[]{:S(2)}) collective-permute-start(f32[5,64,256]{2,1,0:T(8,128)S(1)} %shard_map.50), channel_id=1, source_target_pairs={{0,25},{8,1},{16,9},{24,17},{2,27},{10,3},{18,11},{26,19},{4,29},{... | collective-permute-start | bytes 983048 | tf_op jit(solution)/shard_map/ppermute | solution.py:291
  88.6 15.5 %collective-permute-done.27.refs_29_ = f32[5,64,256]{2,1,0:T(8,128)S(1)} collective-permute-done((f32[5,64,256]{2,1,0:T(8,128)S(1)}, f32[5,64,256]{2,1,0:T(8,128)S(1)}, u32[]{:S(2)}, u32[]{:S(2)}) %collective-permute-start.27) | collective-permute-done | bytes 327712 | tf_op jit(solution)/shard_map/ppermute | solution.py:291
  104.6 6.3 %collective-permute-done.25.refs_27_ = f32[5,64,256]{2,1,0:T(8,128)S(1)} collective-permute-done((f32[5,64,256]{2,1,0:T(8,128)S(1)}, f32[5,64,256]{2,1,0:T(8,128)S(1)}, u32[]{:S(2)}, u32[]{:S(2)}) %collective-permute-start.25) | collective-permute-done | bytes 327712 | tf_op jit(solution)/shard_map/ppermute | solution.py:291
  113.1 20.5 %shard_map.52 = (f32[8,128,256]{2,1,0:T(8,128)}, f32[8,128,256]{2,1,0:T(8,128)S(1)}) custom-call(f32[26]{0:T(128)S(1)} %constant_dynamic-update-slice_fusion.scalars, f32[8,128,256]{2,1,0:T(8,128)S(1)} %bitcast.27, f32[5,128,256]{2,1,0:T(8,128)S(1)} %collective-permute-done.across.refs_1_, f32[3,128,256]{2,1,0:T(8,128)} %collective-permute-done.1.refs_2_, ...), custom_call_target="tpu_custom_call" | custom-call | flops 131072000 | bytes 39321600 | tf_op jit(solution)/shard_map/pallas_call | solution.py:252
  133.7 2.5 %collective-permute-done.33 = f32[8,128,256]{2,1,0:T(8,128)S(1)} collective-permute-done((f32[8,128,256]{2,1,0:T(8,128)S(1)}, f32[8,128,256]{2,1,0:T(8,128)S(1)}, u32[]{:S(2)}, u32[]{:S(2)}) %collective-permute-start.33) | collective-permute-done | bytes 1048608 | tf_op jit(solution)/shard_map/ppermute | solution.py:278
  (114 shorter events, 22.2 us)
Async XLA Ops:
  1.8 14.1 %collective-permute-start.21 = (f32[4,64,256]{2,1,0:T(8,128)S(1)}, f32[4,64,256]{2,1,0:T(8,128)S(1)}, u32[]{:S(2)}, u32[]{:S(2)}) collective-permute-start(f32[4,64,256]{2,1,0:T(8,128)S(1)} %get-tuple-element.25), channel_id=1, source_target_pairs={{0,8},{8,16},{16,24},{24,0},{2,10},{10,18},{18,26},{26,2},{4,12},{... | collective-permute-start | bytes 786440 | tf_op jit(solution)/shard_map/ppermute | solution.py:291
  6.8 16.7 %collective-permute-start.23 = (f32[4,64,256]{2,1,0:T(8,128)S(1)}, f32[4,64,256]{2,1,0:T(8,128)S(1)}, u32[]{:S(2)}, u32[]{:S(2)}) collective-permute-start(f32[4,64,256]{2,1,0:T(8,128)S(1)} %get-tuple-element.24), channel_id=1, source_target_pairs={{0,24},{8,0},{16,8},{24,16},{2,26},{10,2},{18,10},{26,18},{4,28},{... | collective-permute-start | bytes 786440 | tf_op jit(solution)/shard_map/ppermute | solution.py:291
  10.8 29.6 %collective-permute-start.1 = (f32[3,128,256]{2,1,0:T(8,128)S(1)}, f32[3,128,256]{2,1,0:T(8,128)}, u32[]{:S(2)}, u32[]{:S(2)}) collective-permute-start(f32[3,128,256]{2,1,0:T(8,128)S(1)} %get-tuple-element.27), channel_id=1, source_target_pairs={{0,4},{2,6},{4,0},{6,2},{1,5},{3,7},{5,1},{7,3},{8,12},{10,14},{12... | collective-permute-start | bytes 1179656 | tf_op jit(solution)/shard_map/ppermute | solution.py:275
  12.6 28.4 %collective-permute-start.5 = (f32[3,128,256]{2,1,0:T(8,128)S(1)}, f32[3,128,256]{2,1,0:T(8,128)}, u32[]{:S(2)}, u32[]{:S(2)}) collective-permute-start(f32[3,128,256]{2,1,0:T(8,128)S(1)} %get-tuple-element.27), channel_id=1, source_target_pairs={{0,8},{8,16},{16,24},{24,0},{1,9},{9,17},{17,25},{25,1},{2,10},{10... | collective-permute-start | bytes 1179656 | tf_op jit(solution)/shard_map/ppermute | solution.py:281
  12.6 23.1 %collective-permute-start.9 = (f32[2,128,256]{2,1,0:T(8,128)S(1)}, f32[2,128,256]{2,1,0:T(8,128)S(1)}, u32[]{:S(2)}, u32[]{:S(2)}) collective-permute-start(f32[2,128,256]{2,1,0:T(8,128)S(1)} %slice_bitcast_fusion.6), channel_id=1, source_target_pairs={{0,8},{8,16},{16,24},{24,0},{1,9},{9,17},{17,25},{25,1},{2,10},{10... | collective-permute-start | bytes 786440 | tf_op jit(solution)/shard_map/ppermute | solution.py:281
  16.0 24.5 %collective-permute-start.17 = (f32[2,128,256]{2,1,0:T(8,128)S(1)}, f32[2,128,256]{2,1,0:T(8,128)S(1)}, u32[]{:S(2)}, u32[]{:S(2)}) collective-permute-start(f32[2,128,256]{2,1,0:T(8,128)S(1)} %slice_bitcast_fusion.6), channel_id=1, source_target_pairs={{0,24},{8,0},{16,8},{24,16},{1,25},{9,1},{17,9},{25,17},{2,26},{10... | collective-permute-start | bytes 786440 | tf_op jit(solution)/shard_map/ppermute | solution.py:281
  23.5 25.3 %collective-permute-start.13 = (f32[3,128,256]{2,1,0:T(8,128)S(1)}, f32[3,128,256]{2,1,0:T(8,128)S(1)}, u32[]{:S(2)}, u32[]{:S(2)}) collective-permute-start(f32[3,128,256]{2,1,0:T(8,128)S(1)} %get-tuple-element.26), channel_id=1, source_target_pairs={{0,24},{8,0},{16,8},{24,16},{1,25},{9,1},{17,9},{25,17},{2,26},{10... | collective-permute-start | bytes 1179656 | tf_op jit(solution)/shard_map/ppermute | solution.py:281
  35.7 23.1 %collective-permute-start = (f32[5,128,256]{2,1,0:T(8,128)S(1)}, f32[5,128,256]{2,1,0:T(8,128)S(1)}, u32[]{:S(2)}, u32[]{:S(2)}) collective-permute-start(f32[5,128,256]{2,1,0:T(8,128)S(1)} %get-tuple-element.23.own), channel_id=1, source_target_pairs={{0,4},{2,6},{4,0},{6,2},{1,5},{3,7},{5,1},{7,3},{8,12},{10,14},{12... | collective-permute-start | bytes 1966088 | tf_op jit(solution)/shard_map/ppermute | solution.py:275
  40.5 35.2 %collective-permute-start.2 = (f32[8,128,256]{2,1,0:T(8,128)S(1)}, f32[8,128,256]{2,1,0:T(8,128)S(1)}, u32[]{:S(2)}, u32[]{:S(2)}) collective-permute-start(f32[8,128,256]{2,1,0:T(8,128)S(1)} %bitcast.26), channel_id=1, source_target_pairs={{0,2},{2,0},{4,6},{6,4},{1,3},{3,1},{5,7},{7,5},{8,10},{10,8},{12,... | collective-permute-start | bytes 3145736 | tf_op jit(solution)/shard_map/ppermute | solution.py:278
  40.5 9.8 %collective-permute-start.22 = (f32[4,64,256]{2,1,0:T(8,128)S(1)}, f32[4,64,256]{2,1,0:T(8,128)S(1)}, u32[]{:S(2)}, u32[]{:S(2)}) collective-permute-start(f32[4,64,256]{2,1,0:T(8,128)S(1)} %collective-permute-done.21.refs_23_), channel_id=1, source_target_pairs={{0,2},{2,0},{4,6},{6,4},{1,3},{3,1},{5,7},{7,5},{8,10},{10,8},{12,... | collective-permute-start | bytes 786440 | tf_op jit(solution)/shard_map/ppermute | solution.py:278
  41.0 10.5 %collective-permute-start.24 = (f32[4,64,256]{2,1,0:T(8,128)S(1)}, f32[4,64,256]{2,1,0:T(8,128)S(1)}, u32[]{:S(2)}, u32[]{:S(2)}) collective-permute-start(f32[4,64,256]{2,1,0:T(8,128)S(1)} %collective-permute-done.23.refs_25_), channel_id=1, source_target_pairs={{0,2},{2,0},{4,6},{6,4},{1,3},{3,1},{5,7},{7,5},{8,10},{10,8},{12,... | collective-permute-start | bytes 786440 | tf_op jit(solution)/shard_map/ppermute | solution.py:278
  51.0 11.6 %collective-permute-start.18 = (f32[2,128,256]{2,1,0:T(8,128)S(1)}, f32[2,128,256]{2,1,0:T(8,128)S(1)}, u32[]{:S(2)}, u32[]{:S(2)}) collective-permute-start(f32[2,128,256]{2,1,0:T(8,128)S(1)} %collective-permute-done.17.refs_18_), channel_id=1, source_target_pairs={{0,4},{2,6},{4,0},{6,2},{1,5},{3,7},{5,1},{7,3},{8,12},{10,14},{12... | collective-permute-start | bytes 786440 | tf_op jit(solution)/shard_map/ppermute | solution.py:275
  52.2 10.4 %collective-permute-start.11 = (f32[2,128,256]{2,1,0:T(8,128)S(1)}, f32[2,128,256]{2,1,0:T(8,128)S(1)}, u32[]{:S(2)}, u32[]{:S(2)}) collective-permute-start(f32[2,128,256]{2,1,0:T(8,128)S(1)} %collective-permute-done.9.refs_10_), channel_id=1, source_target_pairs={{0,2},{2,0},{4,6},{6,4},{1,3},{3,1},{5,7},{7,5},{8,10},{10,8},{12,... | collective-permute-start | bytes 786440 | tf_op jit(solution)/shard_map/ppermute | solution.py:278
  58.8 17.4 %collective-permute-start.3 = (f32[5,128,256]{2,1,0:T(8,128)S(1)}, f32[5,128,256]{2,1,0:T(8,128)S(1)}, u32[]{:S(2)}, u32[]{:S(2)}) collective-permute-start(f32[5,128,256]{2,1,0:T(8,128)S(1)} %collective-permute-done.across.refs_1_), channel_id=1, source_target_pairs={{0,2},{2,0},{4,6},{6,4},{1,3},{3,1},{5,7},{7,5},{8,10},{10,8},{12,... | collective-permute-start | bytes 1966088 | tf_op jit(solution)/shard_map/ppermute | solution.py:278
  63.4 12.2 %collective-permute-start.6 = (f32[3,128,256]{2,1,0:T(8,128)}, f32[3,128,256]{2,1,0:T(8,128)}, u32[]{:S(2)}, u32[]{:S(2)}) collective-permute-start(f32[3,128,256]{2,1,0:T(8,128)} %collective-permute-done.5.refs_6_), channel_id=1, source_target_pairs={{0,4},{2,6},{4,0},{6,2},{1,5},{3,7},{5,1},{7,3},{8,12},{10,14},{12... | collective-permute-start | bytes 1179656 | tf_op jit(solution)/shard_map/ppermute | solution.py:275
  68.9 15.9 %collective-permute-start.7 = (f32[3,128,256]{2,1,0:T(8,128)}, f32[3,128,256]{2,1,0:T(8,128)S(1)}, u32[]{:S(2)}, u32[]{:S(2)}) collective-permute-start(f32[3,128,256]{2,1,0:T(8,128)} %collective-permute-done.5.refs_6_), channel_id=1, source_target_pairs={{0,2},{2,0},{4,6},{6,4},{1,3},{3,1},{5,7},{7,5},{8,10},{10,8},{12,... | collective-permute-start | bytes 1179656 | tf_op jit(solution)/shard_map/ppermute | solution.py:278
  69.3 14.2 %collective-permute-start.14 = (f32[3,128,256]{2,1,0:T(8,128)S(1)}, f32[3,128,256]{2,1,0:T(8,128)S(1)}, u32[]{:S(2)}, u32[]{:S(2)}) collective-permute-start(f32[3,128,256]{2,1,0:T(8,128)S(1)} %copy-done.7), channel_id=1, source_target_pairs={{0,4},{2,6},{4,0},{6,2},{1,5},{3,7},{5,1},{7,3},{8,12},{10,14},{12... | collective-permute-start | bytes 1179656 | tf_op jit(solution)/shard_map/ppermute | solution.py:275
  75.6 10.5 %collective-permute-start.15 = (f32[3,128,256]{2,1,0:T(8,128)S(1)}, f32[3,128,256]{2,1,0:T(8,128)S(1)}, u32[]{:S(2)}, u32[]{:S(2)}) collective-permute-start(f32[3,128,256]{2,1,0:T(8,128)S(1)} %copy-done.7), channel_id=1, source_target_pairs={{0,2},{2,0},{4,6},{6,4},{1,3},{3,1},{5,7},{7,5},{8,10},{10,8},{12,... | collective-permute-start | bytes 1179656 | tf_op jit(solution)/shard_map/ppermute | solution.py:278
  76.1 12.4 %collective-permute-start.8 = (f32[3,128,256]{2,1,0:T(8,128)}, f32[3,128,256]{2,1,0:T(8,128)S(1)}, u32[]{:S(2)}, u32[]{:S(2)}) collective-permute-start(f32[3,128,256]{2,1,0:T(8,128)} %collective-permute-done.6.refs_7_), channel_id=1, source_target_pairs={{0,2},{2,0},{4,6},{6,4},{1,3},{3,1},{5,7},{7,5},{8,10},{10,8},{12,... | collective-permute-start | bytes 1179656 | tf_op jit(solution)/shard_map/ppermute | solution.py:278
  80.7 23.4 %collective-permute-start.27 = (f32[5,64,256]{2,1,0:T(8,128)S(1)}, f32[5,64,256]{2,1,0:T(8,128)S(1)}, u32[]{:S(2)}, u32[]{:S(2)}) collective-permute-start(f32[5,64,256]{2,1,0:T(8,128)S(1)} %shard_map.51), channel_id=1, source_target_pairs={{0,1},{8,9},{16,17},{24,25},{2,3},{10,11},{18,19},{26,27},{4,5},{1... | collective-permute-start | bytes 983048 | tf_op jit(solution)/shard_map/ppermute | solution.py:291
  83.5 20.6 %collective-permute-start.31 = (f32[5,64,256]{2,1,0:T(8,128)S(1)}, f32[5,64,256]{2,1,0:T(8,128)S(1)}, u32[]{:S(2)}, u32[]{:S(2)}) collective-permute-start(f32[5,64,256]{2,1,0:T(8,128)S(1)} %shard_map.51), channel_id=1, source_target_pairs={{0,9},{8,17},{16,25},{24,1},{2,11},{10,19},{18,27},{26,3},{4,13},{... | collective-permute-start | bytes 983048 | tf_op jit(solution)/shard_map/ppermute | solution.py:291
  84.8 26.1 %collective-permute-start.25 = (f32[5,64,256]{2,1,0:T(8,128)S(1)}, f32[5,64,256]{2,1,0:T(8,128)S(1)}, u32[]{:S(2)}, u32[]{:S(2)}) collective-permute-start(f32[5,64,256]{2,1,0:T(8,128)S(1)} %shard_map.50), channel_id=1, source_target_pairs={{0,1},{8,9},{16,17},{24,25},{2,3},{10,11},{18,19},{26,27},{4,5},{1... | collective-permute-start | bytes 983048 | tf_op jit(solution)/shard_map/ppermute | solution.py:291
  86.1 24.8 %collective-permute-start.29 = (f32[5,64,256]{2,1,0:T(8,128)S(1)}, f32[5,64,256]{2,1,0:T(8,128)S(1)}, u32[]{:S(2)}, u32[]{:S(2)}) collective-permute-start(f32[5,64,256]{2,1,0:T(8,128)S(1)} %shard_map.50), channel_id=1, source_target_pairs={{0,25},{8,1},{16,9},{24,17},{2,27},{10,3},{18,11},{26,19},{4,29},{... | collective-permute-start | bytes 983048 | tf_op jit(solution)/shard_map/ppermute | solution.py:291
  88.5 22.9 %collective-permute-start.16 = (f32[3,128,256]{2,1,0:T(8,128)S(1)}, f32[3,128,256]{2,1,0:T(8,128)S(1)}, u32[]{:S(2)}, u32[]{:S(2)}) collective-permute-start(f32[3,128,256]{2,1,0:T(8,128)S(1)} %collective-permute-done.14.refs_15_), channel_id=1, source_target_pairs={{0,2},{2,0},{4,6},{6,4},{1,3},{3,1},{5,7},{7,5},{8,10},{10,8},{12,... | collective-permute-start | bytes 1179656 | tf_op jit(solution)/shard_map/ppermute | solution.py:278
  (37 other events, 449.0 us)

commit v2 on v0

v2 whole, which is shorter than its diff:
```python
import functools

import jax
import jax.numpy as jnp
import numpy as np
from jax import lax
from jax.experimental import pallas as pl
from jax.experimental.pallas import tpu as pltpu
from jax.sharding import PartitionSpec as P

NODES = 4
PASSES = 4
DEPTH = PASSES + 1

time_step = 0.25
diffusion = 4.0
reaction = 1.0

F32 = jnp.float32


def collocation(count):
    points = [-0.8611363115940526, -0.3399810435848563, 0.3399810435848563, 0.8611363115940526]
    raw_weights = [0.3478548451374538, 0.6521451548625461, 0.6521451548625461, 0.3478548451374538]
    node_times = [(point + 1.0) / 2.0 for point in points]
    quadrature = [[0.0 for column in range(count)] for target in range(count)]
    for source in range(count):
        coeffs = [1.0]
        scaling = 1.0
        for other in range(count):
            if other != source:
                other_time = node_times[other]
                shifted = [0.0] + coeffs
                for power in range(len(coeffs)):
                    shifted[power] = shifted[power] - other_time * coeffs[power]
                coeffs = shifted
                scaling = scaling * (node_times[source] - other_time)
        for target in range(count):
            target_time = node_times[target]
            integral = 0.0
            for power in range(len(coeffs)):
                integral = integral + coeffs[power] * target_time ** (power + 1) / (power + 1)
            quadrature[target][source] = integral / scaling
    return (node_times, quadrature, [weight / 2.0 for weight in raw_weights])


LIN, CUB, WEIGHT, MIX, SCALE, FIRST, CORE, COUNT = 0, 8, 16, 20, 22, 24, 25, 26


def scalar_table():
    times, quad, weights = collocation(NODES)
    table = np.zeros((NODES, COUNT), np.float64)
    for node in range(NODES):
        sources = [node, node ^ 2, node ^ 1, node ^ 3]
        for place, target in enumerate([node, node ^ 2]):
            implicit = time_step * diffusion * times[target]
            for index, source in enumerate(sources):
                lin = time_step * diffusion * quad[target][source]
                table[node, LIN + 4 * place + index] = lin - (implicit if source == target else 0.0)
                table[node, CUB + 4 * place + index] = time_step * reaction * quad[target][source]
            table[node, MIX + place] = implicit / (1.0 + 6.0 * implicit)
            table[node, SCALE + place] = 1.0 / (1.0 + 6.0 * implicit)
        for index, source in enumerate(sources):
            table[node, WEIGHT + index] = weights[source]
        table[node, CORE] = node & 1
    return table.astype(np.float32)


def flat_sum(plane):
    rows, columns = plane.shape
    vertical = pltpu.roll(plane, 1, 0) + pltpu.roll(plane, rows - 1, 0)
    return vertical + (pltpu.roll(plane, 1, 1) + pltpu.roll(plane, columns - 1, 1))


def mixed(scalars, base, planes):
    own, across, beside, corner = (scalars[base + index] * plane for index, plane in enumerate(planes))
    return (own + across) + (beside + corner)


def cubed(state):
    return state - state * state * state


def around(ref, place):
    return (ref[place + 1] + ref[place - 1]) + flat_sum(ref[place])


def grouped(low, high, group, step):
    count = (high - low) // group

    def body(index, carry):
        for member in range(group):
            step(low + index * group + member)
        return carry

    if count > 1:
        lax.fori_loop(0, count, body, 0)
    elif count:
        body(0, 0)
    for place in range(low + count * group, high):
        step(place)


def send_kernel(scalars, own, beside, start, halo_a, halo_b, halo_start):
    upwards = scalars[CORE] < 0.5
    slab = own.shape[0]

    def copy(first_a, first_start):
        for index in range(3):
            halo_a[index] = own[first_a + index]
            halo_a[index + 3] = beside[first_a + index]
        for index in range(4):
            halo_start[index] = start[first_start + index]

    pl.when(upwards)(lambda: copy(slab - 3, slab - 4))
    pl.when(jnp.logical_not(upwards))(lambda: copy(0, 0))
    for index in range(2):
        halo_b[index] = own[3 + index]
        halo_b[index + 2] = beside[3 + index]


def end_kernel(scalars, own, beside, across, corner, start, low, high, total):
    slab = own.shape[0]

    def states_at(plane):
        return own[plane], across[plane], beside[plane], corner[plane]

    total[0] = jnp.zeros_like(total[0])
    total[slab + 1] = jnp.zeros_like(total[0])

    def weigh(plane):
        total[plane + 1] = mixed(scalars, WEIGHT, states_at(plane))

    def force(plane, out, place):
        laplace = around(total, plane + 1) - 6.0 * total[plane + 1]
        local = mixed(scalars, WEIGHT, [cubed(state) for state in states_at(plane)])
        out[place] = start[plane] + time_step * (diffusion * laplace + reaction * local)

    grouped(0, slab, 4, weigh)
    grouped(0, 4, 4, lambda plane: force(plane, low, plane + 1))
    grouped(4, 8, 4, lambda plane: force(plane, high, plane - 4))
    low[0] = (time_step * diffusion) * total[1]
    high[4] = (time_step * diffusion) * total[slab]


def last_kernel(
    scalars, start, start_near, start_far, low_near, low_far, high_near, high_far, part_own, part_across,
    out, share, begin, once, twice, last_own, last_across, total,
):
    first = scalars[FIRST]
    upwards = scalars[CORE] < 0.5
    slab = out.shape[0]

    def assemble(start_low, start_high, end_low, above_low, end_high, below_high):
        for index in range(4):
            value = start_low[index] + below_high[index]
            begin[index] = value + end_low[0] if index == 3 else value
            value = start_high[index] + above_low[index + 1]
            begin[index + 12] = value + end_high[4] if index == 0 else value
            value = first * start[index] + end_low[index + 1]
            begin[index + 4] = value + below_high[4] if index == 0 else value
            value = first * start[index + 4] + end_high[index]
            begin[index + 8] = value + above_low[0] if index == 3 else value

    pl.when(upwards)(lambda: assemble(start_near, start_far, low_near, low_far, high_near, high_far))
    pl.when(jnp.logical_not(upwards))(lambda: assemble(start_far, start_near, low_far, low_near, high_far, high_near))

    def first_power(place):
        once[place] = around(begin, place)

    def second_power(place):
        twice[place] = around(once, place)

    weights = (scalars[WEIGHT], scalars[WEIGHT + 1])
    last, part = (last_own, last_across), (part_own, part_across)

    def combine(place):
        thrice = around(twice, place)
        for target in range(2):
            mix = scalars[MIX + target]
            value = begin[place] + mix * (once[place] + mix * (twice[place] + mix * thrice))
            last[target][place - 3] = part[target][place - 3] + scalars[SCALE + target] * value
        total[place - 3] = weights[0] * last_own[place - 3] + weights[1] * last_across[place - 3]

    def finish(place):
        states = (last_own[place], last_across[place])
        force = diffusion * (around(total, place) - 6.0 * total[place])
        force = force + reaction * (weights[0] * cubed(states[0]) + weights[1] * cubed(states[1]))
        out[place - 1] = states[0]
        share[place - 1] = time_step * force + 0.5 * begin[place + 3]

    grouped(1, 15, 7, first_power)
    grouped(2, 14, 6, second_power)
    grouped(3, 13, 5, combine)
    grouped(1, slab + 1, 4, finish)


EDGE_V, EDGE_R, EDGE_RIGHT, EDGE_1, EDGE_2, EDGE_3, EDGE_COUNT = 0, 4, 6, 12, 16, 20, 24


def inner_kernel(
    scalars, own, beside, across, corner, near, far, across_near, across_far,
    edge_own, edge_across, middle_own, middle_across, x_own, x_across, y_own, y_across, r_own, r_across,
):
    x, y, r = (x_own, x_across), (y_own, y_across), (r_own, r_across)
    edge, middle = (edge_own, edge_across), (middle_own, middle_across)

    def pointwise(place, count, sources, offsets):
        def step(index):
            states = [source[offset + index] for source, offset in zip(sources, offsets)]
            local = [cubed(state) for state in states]
            for target in range(2):
                x[target][place + index] = states[target]
                y[target][place + index] = mixed(scalars, LIN + 4 * target, states)
                r[target][place + index] = mixed(scalars, CUB + 4 * target, local)

        grouped(0, count, 2, step)

    upwards = scalars[CORE] < 0.5

    def halos(near_place, far_place):
        pointwise(near_place, 3, (near, across_near, near, across_near), (0, 0, 3, 3))
        pointwise(far_place, 3, (far, across_far, far, across_far), (3, 3, 0, 0))

    pl.when(upwards)(lambda: halos(2, 13))
    pl.when(jnp.logical_not(upwards))(lambda: halos(13, 2))
    pointwise(5, 8, (own, across, beside, corner), (0, 0, 0, 0))

    def keep(source, base, planes):
        for target in range(2):
            for index, plane in enumerate(planes):
                edge[target][base + index] = source[target][plane + 5]

    def right(place):
        for target in range(2):
            value = (around(y[target], place) - 6.0 * y[target][place]) + r[target][place]
            r[target][place] = scalars[SCALE + target] * value

    grouped(3, 15, 4, right)
    keep(y, EDGE_V, (-3, -2, 9, 10))
    keep(r, EDGE_R, (-3, 10))
    keep(r, EDGE_RIGHT, (-2, -1, 0, 7, 8, 9))

    def passed(source, sink, shift=0):
        def step(place):
            for target in range(2):
                value = scalars[MIX + target] * around(source[target], place)
                sink[target][place - shift] = r[target][place] + value

        return step

    grouped(3, 15, 4, passed(x, y))
    keep(y, EDGE_1, (-2, -1, 8, 9))
    grouped(4, 14, 5, passed(y, x))
    keep(x, EDGE_2, (-1, 0, 7, 8))
    grouped(5, 13, 4, passed(x, y))
    keep(y, EDGE_3, (0, 1, 6, 7))
    grouped(6, 12, 3, passed(y, middle, 6))


def outer_kernel(
    scalars, near_a, far_a, across_near_a, across_far_a, near_b, far_b, across_near_b, across_far_b,
    edge_own, edge_across, middle_own, middle_across, part_own, part_across, x0, v, right, x1, x2, x3,
):
    upwards = scalars[CORE] < 0.5
    edge, middle, part = (edge_own, edge_across), (middle_own, middle_across), (part_own, part_across)
    corners = [(target, end) for target in range(2) for end in range(2)]

    def outermost(end, a, across_a, b, across_b, offset_a, offset_b):
        for q in (5, 4, 3, 2):
            index = {0: {5: 0, 4: 1, 3: 0, 2: 1}, 1: {5: 1, 4: 0, 3: 2, 2: 1}}[end][q]
            if q >= 4:
                pair, offset, other = (b, across_b), offset_b, 2 - offset_b
            else:
                pair, offset, other = (a, across_a), offset_a, 3 - offset_a
            states = [ref[offset + index] for ref in pair]
            for target in range(2):
                x0[target, end, 5 - q] = states[target]
            if q >= 4:
                states += [ref[other + index] for ref in pair]
                for target in range(2):
                    v[target, end, 5 - q] = mixed(scalars, LIN + 4 * target, states)
                    if q == 4:
                        right[target, end, 0] = mixed(scalars, CUB + 4 * target, [cubed(state) for state in states])

    def ends(near_end, far_end):
        outermost(near_end, near_a, across_near_a, near_b, across_near_b, 0, 0)
        outermost(far_end, far_a, across_far_a, far_b, across_far_b, 3, 2)

    pl.when(upwards)(lambda: ends(0, 1))
    pl.when(jnp.logical_not(upwards))(lambda: ends(1, 0))

    def kept(target, end, base, count, q_order):
        return edge[target][base + (q_order if end == 0 else 2 * count - 1 - q_order)]

    def laplacian(outside, centre, inside):
        return ((outside + inside) + flat_sum(centre)) - 6.0 * centre

    def relaxed(target, base, outside, centre, inside):
        return base + scalars[MIX + target] * ((outside + inside) + flat_sum(centre))

    for target, end in corners:
        scale = scalars[SCALE + target]
        v3, v2 = (kept(target, end, EDGE_V, 2, order) for order in range(2))
        value = laplacian(v[target, end, 0], v[target, end, 1], v3) + right[target, end, 0]
        right[target, end, 0] = scale * value
        right[target, end, 1] = scale * (laplacian(v[target, end, 1], v3, v2) + kept(target, end, EDGE_R, 1, 0))
    for target, end in corners:
        for index in range(2):
            x1[target, end, index] = relaxed(
                target, right[target, end, index], x0[target, end, index], x0[target, end, index + 1], x0[target, end, index + 2]
            )
    for target, end in corners:
        near2, near1 = (kept(target, end, EDGE_1, 2, order) for order in range(2))
        right2 = kept(target, end, EDGE_RIGHT, 3, 0)
        x2[target, end, 0] = relaxed(target, right[target, end, 1], x1[target, end, 0], x1[target, end, 1], near2)
        x2[target, end, 1] = relaxed(target, right2, x1[target, end, 1], near2, near1)
    for target, end in corners:
        near1, near0 = (kept(target, end, EDGE_2, 2, order) for order in range(2))
        right2, right1 = (kept(target, end, EDGE_RIGHT, 3, order) for order in range(2))
        x3[target, end, 0] = relaxed(target, right2, x2[target, end, 0], x2[target, end, 1], near1)
        x3[target, end, 1] = relaxed(target, right1, x2[target, end, 1], near1, near0)
    for target, end in corners:
        near0, inside = (kept(target, end, EDGE_3, 2, order) for order in range(2))
        right1, right0 = (kept(target, end, EDGE_RIGHT, 3, order) for order in (1, 2))
        place1, place0 = (0, 1) if end == 0 else (9, 8)
        part[target][place1] = relaxed(target, right1, x3[target, end, 0], x3[target, end, 1], near0)
        part[target][place0] = relaxed(target, right0, x3[target, end, 1], near0, inside)
    for target in range(2):
        for index in range(6):
            part[target][index + 2] = middle[target][index]


def call(kernel, scalars, operands, outs, scratch, limit):
    return pl.pallas_call(
        kernel,
        out_shape=[jax.ShapeDtypeStruct(shape, F32) for shape in outs],
        in_specs=[pl.BlockSpec(memory_space=pltpu.SMEM)] + [pl.BlockSpec(memory_space=pltpu.VMEM)] * len(operands),
        out_specs=[pl.BlockSpec(memory_space=pltpu.VMEM)] * len(outs),
        scratch_shapes=[pltpu.VMEM(shape, F32) for shape in scratch],
        compiler_params=pltpu.CompilerParams(vmem_limit_bytes=limit << 20),
        cost_estimate=pl.CostEstimate(flops=1000, bytes_accessed=1000, transcendentals=0),
    )(scalars, *operands)


def on_device(start_old, nodes_old):
    slabs, slices = lax.axis_size("space"), lax.axis_size("tm")
    node_index = lax.axis_index("node")
    slice_index = lax.axis_index("tm")
    state, start = nodes_old[0, 0], start_old[0]
    slab, rows, columns = state.shape
    scalars = jnp.asarray(scalar_table())[node_index]
    scalars = scalars.at[FIRST].set((slice_index == 0).astype(F32))

    def after(array, other):
        return lax.optimization_barrier((array, other))[0]

    def planes(*lead):
        return (*lead, rows, columns)

    def across(array):
        return lax.ppermute(array, "node", [(node, node ^ 2) for node in range(NODES)])

    def beside(array):
        return lax.ppermute(array, "node", [(node, node ^ 1) for node in range(NODES)])

    def place(slab_, node, slice_):
        return ((slab_ % slabs) * NODES + node) * slices + slice_

    def spread(array, steps, by):
        pairs = [
            (place(slab_, node, here), place(slab_ + by[node % 2], node, there))
            for slab_ in range(slabs) for node in range(NODES) for here, there in steps
        ]
        return lax.ppermute(array, ("space", "node", "tm"), pairs)

    same = [(slice_, slice_) for slice_ in range(slices)]
    onward = [(slice_, slice_ + 1) for slice_ in range(slices - 1)]

    beside_state = beside(state)
    across_state = across(state)
    halo_a, halo_b, halo_start = call(
        send_kernel, scalars, [state, beside_state, start], [planes(6), planes(4), planes(4)], [], 16
    )
    near_a = spread(halo_a, same, (1, -1))
    near_b = spread(halo_b, same, (1, -1))

    corner_state = beside(after(across_state, halo_a))
    sources = [state, beside_state, across_state, corner_state]
    end_low, end_high = call(end_kernel, scalars, [*sources, start], [planes(5)] * 2, [planes(slab + 2)], 16)
    low_near = spread(end_low, onward, (0, -1))
    high_near = spread(end_high, onward, (0, 1))

    across_near_a = across(near_a)
    far_a = beside(after(near_a, end_low))
    across_near_b = across(near_b)
    start_near = spread(after(halo_start, near_b), [(0, 0)], (1, -1))
    across_far_a = beside(across_near_a)

    wide = planes(slab + 2 * DEPTH)
    edge_own, edge_across, middle_own, middle_across = call(
        inner_kernel, scalars, [*sources, near_a, far_a, across_near_a, across_far_a],
        [planes(EDGE_COUNT)] * 2 + [planes(slab - 2)] * 2, [wide] * 6, 36,
    )
    far_b = beside(near_b)
    across_far_b = beside(after(across_near_b, edge_own))
    part_own, part_across = call(
        outer_kernel, scalars,
        [
            near_a, far_a, across_near_a, across_far_a, near_b, far_b, across_near_b, across_far_b,
            edge_own, edge_across, middle_own, middle_across,
        ],
        [planes(slab + 2)] * 2, [planes(2, 2, 4)] + [planes(2, 2, 2)] * 5, 24,
    )
    high_far = beside(after(high_near, edge_own))
    state_new, share = call(
        last_kernel, scalars,
        [start, start_near, beside(start_near), low_near, beside(low_near), high_near, high_far, part_own, part_across],
        [planes(slab)] * 2, [planes(slab + 8)] * 3 + [planes(slab + 2)] * 3, 24,
    )
    end_new = share + beside(share)
    return (state_new[None, None], end_new[None])


def solution(mesh):
    return jax.shard_map(
        on_device,
        mesh=mesh,
        in_specs=(P("tm", "space", None, None), P("tm", "node", "space", None, None)),
        out_specs=(P("tm", "node", "space", None, None), P("tm", "space", None, None)),
        check_vma=False,
    )
```

time: 177 us -> 96.9 us (0.55)
  waiting for transfers between devices: 116 us -> 35.7 us
  Pallas kernels: 0 us -> 27.6 us
  other arithmetic: 18.3 us -> 1.11 us
  between operations: 14.8 us -> 0.77 us
  starting transfers between devices: 18.2 us -> 28.3 us
  local copies, waits for them, and re-layouts: 9.72 us -> 3.16 us
    psum x1 -> x0, waiting for transfers between devices: 34.4 us -> none  [on_device(): weighted_new = lax.psum(node_weight * force_new, 'node')]
    all_gather x1 -> x0, waiting for transfers between devices: 32.9 us -> none  [on_device(): shard_piece = lax.all_gather(force_old[None], 'node', axis=0, tiled=True)]
    pallas_call x0 -> x5, Pallas kernels: none -> 27.6 us  [call(): pl.pallas_call(kernel, out_shape=[jax.ShapeDtypeStruct(shape, F32) for sh...]
    ppermute x11 -> x18, waiting for transfers between devices: 48.3 us -> 35.7 us  [the longest x3 26.1 us: across(): lax.ppermute(array, 'node', [(node, node ^ 2) for node in range(NODES)])]
    ppermute x11 -> x18, starting transfers between devices: 18.2 us -> 28.3 us  [the longest x5 12.2 us: spread(): return lax.ppermute(array, ('space', 'node', 'tm'), pairs)]
    slice x25 -> x0, local copies, waits for them, and re-layouts: 7.72 us -> none  [the longest x10 5.53 us: neighbour_sum(): total = total + jnp.roll(inner, -1, 2) + jnp.roll(inner, 1, 2)]
    div x4 -> x0, other arithmetic: 6.12 us -> none  [on_device(): iterate = (right_side + implicit * neighbour_sum(widened)) / divisor]
    reduce_sum x1 -> x0, other arithmetic: 4.06 us -> none  [on_device(): jnp.sum(weight_table[:, None, None, None] * shard_piece, axis=0)]
  transfers between devices with their start and end apart: 13 -> 18, of which waited for: 13 -> 7; matrix products, arithmetic and copies ran while one was open for 3% -> 1% of each run, Pallas kernels for 0% -> 22%
where the time goes in v2:
time: 96.9 us; the launch traced here: 96.6 us
  waiting for transfers between devices  35.7 us (37%)
  starting transfers between devices  28.3 us (29%)
  Pallas kernels  27.6 us (28%)
  local copies, waits for them, and re-layouts  3.16 us (3%)
  other arithmetic  1.11 us (1%)
    pallas_call x5, Pallas kernels, call(): pl.pallas_call(kernel, out_shape=[jax.ShapeDtypeStruct(shape, F32) for sh...  27.6 us
    ppermute x3, waiting for transfers between devices, across(): lax.ppermute(array, 'node', [(node, node ^ 2) for node in range(NODES)])  26.1 us
    ppermute x5, starting transfers between devices, spread(): return lax.ppermute(array, ('space', 'node', 'tm'), pairs)  12.2 us
    ppermute x10, starting transfers between devices, beside(): lax.ppermute(array, 'node', [(node, node ^ 1) for node in range(NODES)])  11.2 us
    ppermute x10, waiting for transfers between devices, beside(): lax.ppermute(array, 'node', [(node, node ^ 1) for node in range(NODES)])  5.11 us
    ppermute x3, starting transfers between devices, across(): lax.ppermute(array, 'node', [(node, node ^ 2) for node in range(NODES)])  4.81 us
    ppermute x5, waiting for transfers between devices, spread(): return lax.ppermute(array, ('space', 'node', 'tm'), pairs)  4.58 us
    unnamed x8, local copies, waits for them, and re-layouts  2.45 us
  transfers between devices with their start and end apart: 18, of which 7 were waited for; matrix products, arithmetic and copies ran while one was open for 1% of the time, Pallas kernels for 22%

profile of v2, /device:TPU:0, one launch (start us, length us, event | category | flops | bytes accessed | tf_op | source)
XLA Modules:
  0.0 96.6 jit_solution(5462534196717220525)
XLA Ops:
  1.1 2.6 %collective-permute-start.4 = (f32[8,128,256]{2,1,0:T(8,128)}, f32[8,128,256]{2,1,0:T(8,128)S(1)}, u32[]{:S(2)}, u32[]{:S(2)}) collective-permute-start(f32[8,128,256]{2,1,0:T(8,128)} %bitcast.9), channel_id=1, source_target_pairs={{0,4},{2,6},{4,0},{6,2},{1,5},{3,7},{5,1},{7,3},{8,12},{10,14},{12... | collective-permute-start | bytes 3145736 | tf_op jit(solution)/shard_map/ppermute | solution.py:362
  4.4 1.2 %copy-done = f32[1,1,8,128,256]{4,3,2,1,0:T(8,128)S(1)} copy-done((f32[1,1,8,128,256]{4,3,2,1,0:T(8,128)S(1)}, f32[1,1,8,128,256]{4,3,2,1,0:T(8,128)}, u32[]{:S(2)}) %copy-start) | copy-done | bytes 1048600
  5.7 1.2 %copy-done.2 = f32[1,8,128,256]{3,2,1,0:T(8,128)S(1)} copy-done((f32[1,8,128,256]{3,2,1,0:T(8,128)S(1)}, f32[1,8,128,256]{3,2,1,0:T(8,128)}, u32[]{:S(2)}) %copy-start.2) | copy-done | bytes 1048600
  7.6 2.2 %collective-permute-start.9 = (f32[6,128,256]{2,1,0:T(8,128)S(1)}, f32[6,128,256]{2,1,0:T(8,128)S(1)}, u32[]{:S(2)}, u32[]{:S(2)}) collective-permute-start(f32[6,128,256]{2,1,0:T(8,128)S(1)} %get-tuple-element.35), channel_id=1, source_target_pairs={{0,8},{1,9},{2,26},{3,27},{4,12},{5,13},{6,30},{7,31},{8,16},{9,17... | collective-permute-start | bytes 2359304 | tf_op jit(solution)/shard_map/ppermute | solution.py:375
  9.8 17.9 %collective-permute-done.4.across = f32[8,128,256]{2,1,0:T(8,128)S(1)} collective-permute-done((f32[8,128,256]{2,1,0:T(8,128)}, f32[8,128,256]{2,1,0:T(8,128)S(1)}, u32[]{:S(2)}, u32[]{:S(2)}) %collective-permute-start.4) | collective-permute-done | bytes 1048608 | tf_op jit(solution)/shard_map/ppermute | solution.py:362
  27.7 2.1 %collective-permute-done.9.near.near_a = f32[6,128,256]{2,1,0:T(8,128)S(1)} collective-permute-done((f32[6,128,256]{2,1,0:T(8,128)S(1)}, f32[6,128,256]{2,1,0:T(8,128)S(1)}, u32[]{:S(2)}, u32[]{:S(2)}) %collective-permute-start.9) | collective-permute-done | bytes 786464 | tf_op jit(solution)/shard_map/ppermute | solution.py:375
  29.8 1.5 %collective-permute-start.11 = (f32[6,128,256]{2,1,0:T(8,128)S(1)}, f32[6,128,256]{2,1,0:T(8,128)S(1)}, u32[]{:S(2)}, u32[]{:S(2)}) collective-permute-start(f32[6,128,256]{2,1,0:T(8,128)S(1)} %collective-permute-done.9.near.near_a), channel_id=1, source_target_pairs={{0,4},{2,6},{4,0},{6,2},{1,5},{3,7},{5,1},{7,3},{8,12},{10,14},{12... | collective-permute-start | bytes 2359304 | tf_op jit(solution)/shard_map/ppermute | solution.py:362
  31.3 2.3 %shard_map.51 = (f32[5,128,256]{2,1,0:T(8,128)S(1)}, f32[5,128,256]{2,1,0:T(8,128)S(1)}) custom-call(f32[26]{0:T(128)S(1)} %constant_dynamic-update-slice_fusion.scalars, f32[8,128,256]{2,1,0:T(8,128)S(1)} %bitcast.11, f32[8,128,256]{2,1,0:T(8,128)S(1)} %collective-permute-done.beside, f32[8,128,256]{2,1,0:T(8,128)S(1)} %collective-permute-done.4.across, ...), custom_call_target="tpu_custom_call" | custom-call | flops 1000 | bytes 1000 | tf_op jit(solution)/shard_map/pallas_call | solution.py:335
  33.6 3.5 %collective-permute-start.6 = (f32[5,128,256]{2,1,0:T(8,128)S(1)}, f32[5,128,256]{2,1,0:T(8,128)S(1)}, u32[]{:S(2)}, u32[]{:S(2)}) collective-permute-start(f32[5,128,256]{2,1,0:T(8,128)S(1)} %get-tuple-element.37), channel_id=1, source_target_pairs={{0,1},{2,27},{4,5},{6,31},{8,9},{10,3},{12,13},{14,7},{16,17},{18,... | collective-permute-start | bytes 1966088 | tf_op jit(solution)/shard_map/ppermute | solution.py:375
  37.1 0.9 collective-permute-start.1
  38.0 1.5 %collective-permute-start.10 = (f32[6,128,256]{2,1,0:T(8,128)S(1)}, f32[6,128,256]{2,1,0:T(8,128)S(1)}, u32[]{:S(2)}, u32[]{:S(2)}) collective-permute-start(f32[6,128,256]{2,1,0:T(8,128)S(1)} %collective-permute-done.9.near.near_a), channel_id=1, source_target_pairs={{0,2},{2,0},{4,6},{6,4},{1,3},{3,1},{5,7},{7,5},{8,10},{10,8},{12,... | collective-permute-start | bytes 2359304 | tf_op jit(solution)/shard_map/ppermute | solution.py:365
  39.5 8.2 %collective-permute-done.11.across_near.across_near_a = f32[6,128,256]{2,1,0:T(8,128)S(1)} collective-permute-done((f32[6,128,256]{2,1,0:T(8,128)S(1)}, f32[6,128,256]{2,1,0:T(8,128)S(1)}, u32[]{:S(2)}, u32[]{:S(2)}) %collective-permute-start.11) | collective-permute-done | bytes 786464 | tf_op jit(solution)/shard_map/ppermute | solution.py:362
  47.7 3.7 %collective-permute-start.8 = (f32[5,128,256]{2,1,0:T(8,128)S(1)}, f32[5,128,256]{2,1,0:T(8,128)S(1)}, u32[]{:S(2)}, u32[]{:S(2)}) collective-permute-start(f32[5,128,256]{2,1,0:T(8,128)S(1)} %get-tuple-element.38), channel_id=1, source_target_pairs={{0,1},{2,11},{4,5},{6,15},{8,9},{10,19},{12,13},{14,23},{16,17},{1... | collective-permute-start | bytes 1966088 | tf_op jit(solution)/shard_map/ppermute | solution.py:375
  51.4 2.4 %collective-permute-done.1.near_b = f32[4,128,256]{2,1,0:T(8,128)S(1)} collective-permute-done((f32[4,128,256]{2,1,0:T(8,128)S(1)}, f32[4,128,256]{2,1,0:T(8,128)S(1)}, u32[]{:S(2)}, u32[]{:S(2)}) %collective-permute-start.1) | collective-permute-done | bytes 524320 | tf_op jit(solution)/shard_map/ppermute | solution.py:375
  53.8 0.8 collective-permute-start.15
  54.6 1.9 %collective-permute-start.2 = (f32[4,128,256]{2,1,0:T(8,128)S(1)}, f32[4,128,256]{2,1,0:T(8,128)S(1)}, u32[]{:S(2)}, u32[]{:S(2)}) collective-permute-start(f32[4,128,256]{2,1,0:T(8,128)S(1)} %get-tuple-element.34), channel_id=1, source_target_pairs={{0,8},{2,26},{4,12},{6,30},{8,16},{10,2},{12,20},{14,6},{16,24},{1... | collective-permute-start | bytes 1572872 | tf_op jit(solution)/shard_map/ppermute | solution.py:375
  56.5 8.0 %collective-permute-start.7 = (f32[5,128,256]{2,1,0:T(8,128)S(1)}, f32[5,128,256]{2,1,0:T(8,128)S(1)}, u32[]{:S(2)}, u32[]{:S(2)}) collective-permute-start(f32[5,128,256]{2,1,0:T(8,128)S(1)} %collective-permute-done.6.low_near), channel_id=1, source_target_pairs={{0,2},{2,0},{4,6},{6,4},{1,3},{3,1},{5,7},{7,5},{8,10},{10,8},{12,... | collective-permute-start | bytes 1966088 | tf_op jit(solution)/shard_map/ppermute | solution.py:365
  64.5 12.6 %shard_map.52 = (f32[24,128,256]{2,1,0:T(8,128)S(1)}, f32[24,128,256]{2,1,0:T(8,128)S(1)}, f32[6,128,256]{2,1,0:T(8,128)S(1)}, f32[6,128,256]{2,1,0:T(8,128)S(1)}) custom-call(f32[26]{0:T(128)S(1)} %constant_dynamic-update-slice_fusion.scalars, f32[8,128,256]{2,1,0:T(8,128)S(1)} %bitcast.12, f32[8,128,256]{2,1,0:T(8,128)S(1)} %collective-permute-done.beside, ...), custom_call_target="tpu_custom_call" | custom-call | flops 1000 | bytes 1000 | tf_op jit(solution)/shard_map/pallas_call | solution.py:335
  78.2 1.8 %collective-permute-done.14.far_b = f32[4,128,256]{2,1,0:T(8,128)S(1)} collective-permute-done((f32[4,128,256]{2,1,0:T(8,128)S(1)}, f32[4,128,256]{2,1,0:T(8,128)S(1)}, u32[]{:S(2)}, u32[]{:S(2)}) %collective-permute-start.14) | collective-permute-done | bytes 524320 | tf_op jit(solution)/shard_map/ppermute | solution.py:365
  80.0 0.7 collective-permute-done.16.across_far_b
  80.8 5.4 %shard_map.53 = (f32[10,128,256]{2,1,0:T(8,128)S(1)}, f32[10,128,256]{2,1,0:T(8,128)S(1)}) custom-call(f32[26]{0:T(128)S(1)} %constant_dynamic-update-slice_fusion.scalars, f32[6,128,256]{2,1,0:T(8,128)S(1)} %collective-permute-done.9.near.near_a, f32[6,128,256]{2,1,0:T(8,128)S(1)} %collective-permute-done.10.far.far_a, ...), custom_call_target="tpu_custom_call" | custom-call | flops 1000 | bytes 1000 | tf_op jit(solution)/shard_map/pallas_call | solution.py:335
  86.2 6.6 %shard_map.54 = (f32[8,128,256]{2,1,0:T(8,128)}, f32[8,128,256]{2,1,0:T(8,128)S(1)}) custom-call(f32[26]{0:T(128)S(1)} %constant_dynamic-update-slice_fusion.scalars, f32[8,128,256]{2,1,0:T(8,128)S(1)} %bitcast.15, f32[4,128,256]{2,1,0:T(8,128)S(1)} %collective-permute-done.2.start_near, f32[4,128,256]{2,1,0:T(8,128)S(1)} %collective-permute-done.3.start_far, ...), custom_call_target="tpu_custom_call" | custom-call | flops 1000 | bytes 1000 | tf_op jit(solution)/shard_map/pallas_call | solution.py:335
  92.9 2.5 %collective-permute-done.17 = f32[8,128,256]{2,1,0:T(8,128)S(1)} collective-permute-done((f32[8,128,256]{2,1,0:T(8,128)S(1)}, f32[8,128,256]{2,1,0:T(8,128)S(1)}, u32[]{:S(2)}, u32[]{:S(2)}) %collective-permute-start.17) | collective-permute-done | bytes 1048608 | tf_op jit(solution)/shard_map/ppermute | solution.py:365
  95.5 1.1 %add_bitcast_fusion = f32[1,8,128,256]{3,2,1,0:T(8,128)} fusion(f32[8,128,256]{2,1,0:T(8,128)S(1)} %get-tuple-element.49, f32[8,128,256]{2,1,0:T(8,128)S(1)} %collective-permute-done.17), kind=kLoop, calls=%fused_computation | loop fusion | flops 262144 | bytes 3145728 | tf_op jit(solution)/shard_map/broadcast_in_dim | solution.py:422
  (28 shorter events, 3.2 us)
Async XLA Ops:
  0.6 3.8 %collective-permute-start = (f32[8,128,256]{2,1,0:T(8,128)}, f32[8,128,256]{2,1,0:T(8,128)S(1)}, u32[]{:S(2)}, u32[]{:S(2)}) collective-permute-start(f32[8,128,256]{2,1,0:T(8,128)} %bitcast.8), channel_id=1, source_target_pairs={{0,2},{2,0},{4,6},{6,4},{1,3},{3,1},{5,7},{7,5},{8,10},{10,8},{12,... | collective-permute-start | bytes 3145736 | tf_op jit(solution)/shard_map/ppermute | solution.py:365
  1.1 26.5 %collective-permute-start.4 = (f32[8,128,256]{2,1,0:T(8,128)}, f32[8,128,256]{2,1,0:T(8,128)S(1)}, u32[]{:S(2)}, u32[]{:S(2)}) collective-permute-start(f32[8,128,256]{2,1,0:T(8,128)} %bitcast.9), channel_id=1, source_target_pairs={{0,4},{2,6},{4,0},{6,2},{1,5},{3,7},{5,1},{7,3},{8,12},{10,14},{12... | collective-permute-start | bytes 3145736 | tf_op jit(solution)/shard_map/ppermute | solution.py:362
  4.4 1.2 %copy-start = (f32[1,1,8,128,256]{4,3,2,1,0:T(8,128)S(1)}, f32[1,1,8,128,256]{4,3,2,1,0:T(8,128)}, u32[]{:S(2)}) copy-start(f32[1,1,8,128,256]{4,3,2,1,0:T(8,128)} %param.6) | copy-start | bytes 3145732
  5.6 1.2 %copy-start.2 = (f32[1,8,128,256]{3,2,1,0:T(8,128)S(1)}, f32[1,8,128,256]{3,2,1,0:T(8,128)}, u32[]{:S(2)}) copy-start(f32[1,8,128,256]{3,2,1,0:T(8,128)} %param.5) | copy-start | bytes 3145732
  7.5 56.9 %copy-start.1 = (f32[1,1,8,128,256]{4,3,2,1,0:T(8,128)S(1)}, f32[1,1,8,128,256]{4,3,2,1,0:T(8,128)}, u32[]{:S(2)}) copy-start(f32[1,1,8,128,256]{4,3,2,1,0:T(8,128)} %param.6) | copy-start | bytes 3145732
  7.6 22.3 %collective-permute-start.9 = (f32[6,128,256]{2,1,0:T(8,128)S(1)}, f32[6,128,256]{2,1,0:T(8,128)S(1)}, u32[]{:S(2)}, u32[]{:S(2)}) collective-permute-start(f32[6,128,256]{2,1,0:T(8,128)S(1)} %get-tuple-element.35), channel_id=1, source_target_pairs={{0,8},{1,9},{2,26},{3,27},{4,12},{5,13},{6,30},{7,31},{8,16},{9,17... | collective-permute-start | bytes 2359304 | tf_op jit(solution)/shard_map/ppermute | solution.py:375
  27.7 3.6 %collective-permute-start.5 = (f32[8,128,256]{2,1,0:T(8,128)S(1)}, f32[8,128,256]{2,1,0:T(8,128)S(1)}, u32[]{:S(2)}, u32[]{:S(2)}) collective-permute-start(f32[8,128,256]{2,1,0:T(8,128)S(1)} %collective-permute-done.4.across), channel_id=1, source_target_pairs={{0,2},{2,0},{4,6},{6,4},{1,3},{3,1},{5,7},{7,5},{8,10},{10,8},{12,... | collective-permute-start | bytes 3145736 | tf_op jit(solution)/shard_map/ppermute | solution.py:365
  29.8 17.8 %collective-permute-start.11 = (f32[6,128,256]{2,1,0:T(8,128)S(1)}, f32[6,128,256]{2,1,0:T(8,128)S(1)}, u32[]{:S(2)}, u32[]{:S(2)}) collective-permute-start(f32[6,128,256]{2,1,0:T(8,128)S(1)} %collective-permute-done.9.near.near_a), channel_id=1, source_target_pairs={{0,4},{2,6},{4,0},{6,2},{1,5},{3,7},{5,1},{7,3},{8,12},{10,14},{12... | collective-permute-start | bytes 2359304 | tf_op jit(solution)/shard_map/ppermute | solution.py:362
  33.6 21.0 %collective-permute-start.6 = (f32[5,128,256]{2,1,0:T(8,128)S(1)}, f32[5,128,256]{2,1,0:T(8,128)S(1)}, u32[]{:S(2)}, u32[]{:S(2)}) collective-permute-start(f32[5,128,256]{2,1,0:T(8,128)S(1)} %get-tuple-element.37), channel_id=1, source_target_pairs={{0,1},{2,27},{4,5},{6,31},{8,9},{10,3},{12,13},{14,7},{16,17},{18,... | collective-permute-start | bytes 1966088 | tf_op jit(solution)/shard_map/ppermute | solution.py:375
  37.1 16.7 %collective-permute-start.1 = (f32[4,128,256]{2,1,0:T(8,128)S(1)}, f32[4,128,256]{2,1,0:T(8,128)S(1)}, u32[]{:S(2)}, u32[]{:S(2)}) collective-permute-start(f32[4,128,256]{2,1,0:T(8,128)S(1)} %get-tuple-element.33), channel_id=1, source_target_pairs={{0,8},{1,9},{2,26},{3,27},{4,12},{5,13},{6,30},{7,31},{8,16},{9,17... | collective-permute-start | bytes 1572872 | tf_op jit(solution)/shard_map/ppermute | solution.py:375
  38.0 18.5 %collective-permute-start.10 = (f32[6,128,256]{2,1,0:T(8,128)S(1)}, f32[6,128,256]{2,1,0:T(8,128)S(1)}, u32[]{:S(2)}, u32[]{:S(2)}) collective-permute-start(f32[6,128,256]{2,1,0:T(8,128)S(1)} %collective-permute-done.9.near.near_a), channel_id=1, source_target_pairs={{0,2},{2,0},{4,6},{6,4},{1,3},{3,1},{5,7},{7,5},{8,10},{10,8},{12,... | collective-permute-start | bytes 2359304 | tf_op jit(solution)/shard_map/ppermute | solution.py:365
  47.7 16.8 %collective-permute-start.12 = (f32[6,128,256]{2,1,0:T(8,128)S(1)}, f32[6,128,256]{2,1,0:T(8,128)S(1)}, u32[]{:S(2)}, u32[]{:S(2)}) collective-permute-start(f32[6,128,256]{2,1,0:T(8,128)S(1)} %collective-permute-done.11.across_near.across_near_a), channel_id=1, source_target_pairs={{0,2},{2,0},{4,6},{6,4},{1,3},{3,1},{5,7},{7,5},{8,10},{10,8},{12,... | collective-permute-start | bytes 2359304 | tf_op jit(solution)/shard_map/ppermute | solution.py:365
  47.7 29.4 %collective-permute-start.8 = (f32[5,128,256]{2,1,0:T(8,128)S(1)}, f32[5,128,256]{2,1,0:T(8,128)S(1)}, u32[]{:S(2)}, u32[]{:S(2)}) collective-permute-start(f32[5,128,256]{2,1,0:T(8,128)S(1)} %get-tuple-element.38), channel_id=1, source_target_pairs={{0,1},{2,11},{4,5},{6,15},{8,9},{10,19},{12,13},{14,23},{16,17},{1... | collective-permute-start | bytes 1966088 | tf_op jit(solution)/shard_map/ppermute | solution.py:375
  53.8 23.9 %collective-permute-start.15 = (f32[4,128,256]{2,1,0:T(8,128)S(1)}, f32[4,128,256]{2,1,0:T(8,128)S(1)}, u32[]{:S(2)}, u32[]{:S(2)}) collective-permute-start(f32[4,128,256]{2,1,0:T(8,128)S(1)} %collective-permute-done.1.near_b), channel_id=1, source_target_pairs={{0,4},{2,6},{4,0},{6,2},{1,5},{3,7},{5,1},{7,3},{8,12},{10,14},{12... | collective-permute-start | bytes 1572872 | tf_op jit(solution)/shard_map/ppermute | solution.py:362
  54.6 23.2 %collective-permute-start.2 = (f32[4,128,256]{2,1,0:T(8,128)S(1)}, f32[4,128,256]{2,1,0:T(8,128)S(1)}, u32[]{:S(2)}, u32[]{:S(2)}) collective-permute-start(f32[4,128,256]{2,1,0:T(8,128)S(1)} %get-tuple-element.34), channel_id=1, source_target_pairs={{0,8},{2,26},{4,12},{6,30},{8,16},{10,2},{12,20},{14,6},{16,24},{1... | collective-permute-start | bytes 1572872 | tf_op jit(solution)/shard_map/ppermute | solution.py:375
  56.5 29.7 %collective-permute-start.7 = (f32[5,128,256]{2,1,0:T(8,128)S(1)}, f32[5,128,256]{2,1,0:T(8,128)S(1)}, u32[]{:S(2)}, u32[]{:S(2)}) collective-permute-start(f32[5,128,256]{2,1,0:T(8,128)S(1)} %collective-permute-done.6.low_near), channel_id=1, source_target_pairs={{0,2},{2,0},{4,6},{6,4},{1,3},{3,1},{5,7},{7,5},{8,10},{10,8},{12,... | collective-permute-start | bytes 1966088 | tf_op jit(solution)/shard_map/ppermute | solution.py:365
  77.1 9.1 %collective-permute-start.13 = (f32[5,128,256]{2,1,0:T(8,128)S(1)}, f32[5,128,256]{2,1,0:T(8,128)S(1)}, u32[]{:S(2)}, u32[]{:S(2)}) collective-permute-start(f32[5,128,256]{2,1,0:T(8,128)S(1)} %collective-permute-done.8.high_near), channel_id=1, source_target_pairs={{0,2},{2,0},{4,6},{6,4},{1,3},{3,1},{5,7},{7,5},{8,10},{10,8},{12,... | collective-permute-start | bytes 1966088 | tf_op jit(solution)/shard_map/ppermute | solution.py:365
  77.2 2.8 %collective-permute-start.14 = (f32[4,128,256]{2,1,0:T(8,128)S(1)}, f32[4,128,256]{2,1,0:T(8,128)S(1)}, u32[]{:S(2)}, u32[]{:S(2)}) collective-permute-start(f32[4,128,256]{2,1,0:T(8,128)S(1)} %collective-permute-done.1.near_b), channel_id=1, source_target_pairs={{0,2},{2,0},{4,6},{6,4},{1,3},{3,1},{5,7},{7,5},{8,10},{10,8},{12,... | collective-permute-start | bytes 1572872 | tf_op jit(solution)/shard_map/ppermute | solution.py:365
  77.7 3.1 %collective-permute-start.16 = (f32[4,128,256]{2,1,0:T(8,128)S(1)}, f32[4,128,256]{2,1,0:T(8,128)S(1)}, u32[]{:S(2)}, u32[]{:S(2)}) collective-permute-start(f32[4,128,256]{2,1,0:T(8,128)S(1)} %collective-permute-done.15.across_near_b), channel_id=1, source_target_pairs={{0,2},{2,0},{4,6},{6,4},{1,3},{3,1},{5,7},{7,5},{8,10},{10,8},{12,... | collective-permute-start | bytes 1572872 | tf_op jit(solution)/shard_map/ppermute | solution.py:365
  77.8 8.4 %collective-permute-start.3 = (f32[4,128,256]{2,1,0:T(8,128)S(1)}, f32[4,128,256]{2,1,0:T(8,128)S(1)}, u32[]{:S(2)}, u32[]{:S(2)}) collective-permute-start(f32[4,128,256]{2,1,0:T(8,128)S(1)} %collective-permute-done.2.start_near), channel_id=1, source_target_pairs={{0,2},{2,0},{4,6},{6,4},{1,3},{3,1},{5,7},{7,5},{8,10},{10,8},{12,... | collective-permute-start | bytes 1572872 | tf_op jit(solution)/shard_map/ppermute | solution.py:365
  80.8 5.5 %copy-start.3 = (f32[1,8,128,256]{3,2,1,0:T(8,128)S(1)}, f32[1,8,128,256]{3,2,1,0:T(8,128)}, u32[]{:S(2)}) copy-start(f32[1,8,128,256]{3,2,1,0:T(8,128)} %param.5) | copy-start | bytes 3145732
  92.8 2.7 %collective-permute-start.17 = (f32[8,128,256]{2,1,0:T(8,128)S(1)}, f32[8,128,256]{2,1,0:T(8,128)S(1)}, u32[]{:S(2)}, u32[]{:S(2)}) collective-permute-start(f32[8,128,256]{2,1,0:T(8,128)S(1)} %get-tuple-element.49), channel_id=1, source_target_pairs={{0,2},{2,0},{4,6},{6,4},{1,3},{3,1},{5,7},{7,5},{8,10},{10,8},{12,... | collective-permute-start | bytes 3145736 | tf_op jit(solution)/shard_map/ppermute | solution.py:365

commit v3 on v0

v3 whole, which is shorter than its diff:
```python
import functools

import jax
import jax.numpy as jnp
import numpy as np
from jax import lax
from jax.experimental import pallas as pl
from jax.experimental.pallas import tpu as pltpu
from jax.sharding import PartitionSpec as P

NODES = 4
PASSES = 4

time_step = 0.25
diffusion = 4.0
reaction = 1.0

F32 = jnp.float32

OUTER = 5
SLAB = 8
HALF = 4


def collocation(count):
    points = [-0.8611363115940526, -0.3399810435848563, 0.3399810435848563, 0.8611363115940526]
    raw_weights = [0.3478548451374538, 0.6521451548625461, 0.6521451548625461, 0.3478548451374538]
    node_times = [(point + 1.0) / 2.0 for point in points]
    quadrature = [[0.0 for column in range(count)] for target in range(count)]
    for source in range(count):
        coeffs = [1.0]
        scaling = 1.0
        for other in range(count):
            if other != source:
                other_time = node_times[other]
                shifted = [0.0] + coeffs
                for power in range(len(coeffs)):
                    shifted[power] = shifted[power] - other_time * coeffs[power]
                coeffs = shifted
                scaling = scaling * (node_times[source] - other_time)
        for target in range(count):
            target_time = node_times[target]
            integral = 0.0
            for power in range(len(coeffs)):
                integral = integral + coeffs[power] * target_time ** (power + 1) / (power + 1)
            quadrature[target][source] = integral / scaling
    return (node_times, quadrature, [weight / 2.0 for weight in raw_weights])


LIN, CUB, WEIGHT, MIX, SCALE, FIRST, CORE, COUNT = 0, 16, 32, 36, 40, 44, 45, 46


def scalar_table():
    times, quad, weights = collocation(NODES)
    table = np.zeros((NODES, COUNT), np.float64)
    for node in range(NODES):
        order = [node, node ^ 2, node ^ 1, node ^ 3]
        for place, target in enumerate(order):
            implicit = time_step * diffusion * times[target]
            for index, source in enumerate(order):
                lin = time_step * diffusion * quad[target][source]
                table[node, LIN + 4 * place + index] = lin - (implicit if source == target else 0.0)
                table[node, CUB + 4 * place + index] = time_step * reaction * quad[target][source]
            table[node, WEIGHT + place] = weights[target]
            table[node, MIX + place] = implicit / (1.0 + 6.0 * implicit)
            table[node, SCALE + place] = 1.0 / (1.0 + 6.0 * implicit)
        table[node, CORE] = node & 1
    return table.astype(np.float32)


def flat_sum(plane):
    rows, columns = plane.shape
    vertical = pltpu.roll(plane, 1, 0) + pltpu.roll(plane, rows - 1, 0)
    return vertical + (pltpu.roll(plane, 1, 1) + pltpu.roll(plane, columns - 1, 1))


def around(outside, centre, inside):
    return (outside + inside) + flat_sum(centre)


def laplacian(outside, centre, inside):
    return around(outside, centre, inside) - 6.0 * centre


def mixed(scalars, base, planes):
    own, across, beside, corner = (scalars[base + index] * plane for index, plane in enumerate(planes))
    return (own + across) + (beside + corner)


def cubed(state):
    return state - state * state * state


def counter(scalars):
    upper = (scalars[CORE] > 0.5).astype(jnp.int32)
    base, sign = upper * (SLAB - 1), 1 - 2 * upper
    return lambda place: base + sign * (place - OUTER)


def send_kernel(scalars, own, beside, start, halo_a, halo_b, halo_start):
    plane = counter(scalars)
    for index in range(3):
        halo_a[index] = own[plane(10 + index)]
        halo_a[index + 3] = beside[plane(10 + index)]
    for index in range(2):
        halo_b[index] = own[plane(8 + index)]
        halo_b[index + 2] = beside[plane(8 + index)]
    for index in range(4):
        halo_start[index] = start[plane(9 + index)]


def end_kernel(scalars, own, across, beside, corner, start, near, away, total):
    plane = counter(scalars)
    total[0] = jnp.zeros_like(total[0])
    total[SLAB + 1] = jnp.zeros_like(total[0])
    sources = (own, across, beside, corner)
    for index in range(SLAB):
        total[index + 1] = mixed(scalars, WEIGHT, [source[plane(index + OUTER)] for source in sources])

    for index in range(SLAB):
        here = plane(index + OUTER)
        local = mixed(scalars, WEIGHT, [cubed(source[here]) for source in sources])
        force = diffusion * laplacian(total[index], total[index + 1], total[index + 2]) + reaction * local
        value = start[here] + time_step * force
        if index < HALF:
            near[index + 1] = value
        else:
            away[index - HALF] = value
    near[0] = (time_step * diffusion) * total[1]
    away[HALF] = (time_step * diffusion) * total[SLAB]


class Stack:
    def __init__(self, ref, places):
        self.ref, self.index = ref, {place: index for index, place in enumerate(places)}

    def __getitem__(self, key):
        target, place = key
        return self.ref[target, self.index[place]]

    def __setitem__(self, key, value):
        target, place = key
        self.ref[target, self.index[place]] = value

    def __contains__(self, place):
        return place in self.index


class Chain:
    def __init__(self, *stacks):
        self.stacks = stacks

    def find(self, place):
        return next(stack for stack in self.stacks if place in stack)

    def __getitem__(self, key):
        return self.find(key[1])[key]

    def __setitem__(self, key, value):
        self.find(key[1])[key] = value


STAGES = [
    {"v": range(5, 13), "r": range(5, 12), "g": range(6, 12), "x1": range(6, 12), "x2": range(7, 11), "x3": range(8, 10), "x4": range(0)},
    {"v": range(2, 5), "r": range(2, 5), "g": range(3, 6), "x1": range(3, 6), "x2": range(4, 7), "x3": range(5, 8), "x4": range(6, 9)},
    {"v": range(0, 2), "r": range(1, 2), "g": range(1, 3), "x1": range(1, 3), "x2": range(2, 4), "x3": range(3, 5), "x4": range(4, 6)},
]
NAMES = ("v", "r", "g", "x1", "x2", "x3", "x4")
KEPT = [
    {"v": (5, 6), "r": (5,), "g": (6, 7, 8), "x1": (6, 7), "x2": (7, 8), "x3": (8, 9), "x4": ()},
    {"v": (2, 3), "r": (2,), "g": (3, 4, 5), "x1": (3, 4), "x2": (4, 5), "x3": (5, 6), "x4": (6, 7, 8)},
]


def kept_count(stage):
    return sum(len(places) for places in KEPT[stage].values())


def kept_stacks(ref, stage):
    stacks, first = {}, 0
    for name in NAMES:
        places = KEPT[stage][name]
        stacks[name] = Stack(ref.at[:, first : first + len(places)], places) if places else Stack(None, ())
        first += len(places)
    return stacks


def run_stage(stage, scalars, state, old, new):
    both = {name: Chain(new[name], *(stacks[name] for stacks in old)) for name in NAMES}
    targets = range(NODES)
    for place in STAGES[stage]["v"]:
        states = [state(source, place) for source in range(NODES)]
        for target in targets:
            new["v"][target, place] = mixed(scalars, LIN + 4 * target, states)
        if place in STAGES[stage]["r"]:
            local = [cubed(value) for value in states]
            for target in targets:
                new["r"][target, place] = mixed(scalars, CUB + 4 * target, local)
    for place in STAGES[stage]["g"]:
        for target in targets:
            value = laplacian(*(both["v"][target, place + by] for by in (-1, 0, 1)))
            new["g"][target, place] = scalars[SCALE + target] * (value + both["r"][target, place])
    for name, before in (("x1", None), ("x2", "x1"), ("x3", "x2"), ("x4", "x3")):
        for place in STAGES[stage][name]:
            for target in targets:
                if before is None:
                    planes = [state(target, place + by) for by in (-1, 0, 1)]
                else:
                    planes = [both[before][target, place + by] for by in (-1, 0, 1)]
                new[name][target, place] = both["g"][target, place] + scalars[MIX + target] * around(*planes)


def stage_scratch(stage, planes):
    return [planes(NODES, len(STAGES[stage][name])) for name in NAMES if len(STAGES[stage][name])]


def stage_stacks(stage, refs):
    refs = iter(refs)
    return {name: Stack(next(refs), places) if len(places) else Stack(None, ()) for name, places in STAGES[stage].items()}


def keep(stage, new, out):
    kept = kept_stacks(out, stage)
    for name in NAMES:
        for place in KEPT[stage][name]:
            for target in range(NODES):
                kept[name][target, place] = new[name][target, place]


def first_kernel(scalars, own, across, beside, corner, out, *scratch):
    plane = counter(scalars)
    sources = (own, across, beside, corner)
    new = stage_stacks(0, scratch)
    run_stage(0, scalars, lambda source, place: sources[source][plane(place)], [], new)
    keep(0, new, out)


def halo_state(halo, halo_across, first, count):
    def state(source, place):
        ref = (halo, halo_across, halo, halo_across)[source]
        return ref[(count if source >= 2 else 0) + place - first]

    return state


def second_kernel(scalars, own, across, beside, corner, halo_a, across_a, kept, out, *scratch):
    plane = counter(scalars)
    sources = (own, across, beside, corner)
    outer = halo_state(halo_a, across_a, 2, 3)

    def state(source, place):
        return outer(source, place) if place < OUTER else sources[source][plane(place)]

    new = stage_stacks(1, scratch)
    run_stage(1, scalars, state, [kept_stacks(kept, 0)], new)
    keep(1, new, out)


def third_kernel(scalars, halo_a, across_a, halo_b, across_b, kept, out, *scratch):
    inner, outer = halo_state(halo_a, across_a, 2, 3), halo_state(halo_b, across_b, 0, 2)

    def state(source, place):
        return outer(source, place) if place < 2 else inner(source, place)

    new = stage_stacks(2, scratch)
    old = kept_stacks(kept, 1)
    run_stage(2, scalars, state, [old], new)
    for target in range(NODES):
        for place in range(4, 9):
            source = new if place in new["x4"] else old
            out[target, place - 4] = source["x4"][target, place]


def last_kernel(scalars, start, halo_start, near, far, away, part, mine, swap, begin, once, twice, last, total):
    plane = counter(scalars)
    first = scalars[FIRST]
    for place in range(1, 4):
        begin[place] = halo_start[place - 1] + away[place - 1]
    begin[4] = (halo_start[3] + away[3]) + near[0]
    begin[5] = (first * start[plane(5)] + near[1]) + away[4]
    for place in range(6, 9):
        begin[place] = first * start[plane(place)] + near[place - 4]
    for place in range(9, 12):
        begin[place] = first * start[plane(place)] + far[11 - place]

    for place in range(2, 11):
        once[place] = around(*(begin[place + by] for by in (-1, 0, 1)))
    for place in range(3, 10):
        twice[place] = around(*(once[place + by] for by in (-1, 0, 1)))
    for place in range(4, 9):
        thrice = around(*(twice[place + by] for by in (-1, 0, 1)))
        for target in range(NODES):
            mix = scalars[MIX + target]
            value = begin[place] + mix * (once[place] + mix * (twice[place] + mix * thrice))
            last[target, place - 4] = part[target, place - 4] + scalars[SCALE + target] * value
        total[place - 4] = mixed(scalars, WEIGHT, [last[target, place - 4] for target in range(NODES)])
    total[5] = jnp.zeros_like(total[5])
    for place in range(OUTER, OUTER + HALF):
        index = place - 4
        local = mixed(scalars, WEIGHT, [cubed(last[target, index]) for target in range(NODES)])
        force = diffusion * laplacian(total[index - 1], total[index], total[index + 1]) + reaction * local
        mine[index - 1] = last[0, index]
        mine[index - 1 + HALF] = begin[place] + time_step * force
        swap[index - 1] = last[2, index]
        swap[index - 1 + HALF] = begin[place] + time_step * force
    mine[2 * HALF] = total[HALF]
    swap[2 * HALF] = total[HALF]


def join_kernel(scalars, mine, other, state, end):
    plane = counter(scalars)
    for index in range(HALF):
        near, far = plane(OUTER + index), plane(OUTER + SLAB - 1 - index)
        state[near] = mine[index]
        state[far] = other[index]
        own, others = mine[HALF + index], other[HALF + index]
        if index == HALF - 1:
            own = own + (time_step * diffusion) * other[2 * HALF]
            others = others + (time_step * diffusion) * mine[2 * HALF]
        end[near] = own
        end[far] = others


def call(kernel, scalars, operands, outs, scratch, limit):
    return pl.pallas_call(
        kernel,
        out_shape=[jax.ShapeDtypeStruct(shape, F32) for shape in outs],
        in_specs=[pl.BlockSpec(memory_space=pltpu.SMEM)] + [pl.BlockSpec(memory_space=pltpu.VMEM)] * len(operands),
        out_specs=[pl.BlockSpec(memory_space=pltpu.VMEM)] * len(outs),
        scratch_shapes=[pltpu.VMEM(shape, F32) for shape in scratch],
        compiler_params=pltpu.CompilerParams(vmem_limit_bytes=limit << 20),
        cost_estimate=pl.CostEstimate(flops=1000, bytes_accessed=1000, transcendentals=0),
    )(scalars, *operands)


def on_device(start_old, nodes_old):
    slabs, slices = lax.axis_size("space"), lax.axis_size("tm")
    node_index = lax.axis_index("node")
    slice_index = lax.axis_index("tm")
    state, start = nodes_old[0, 0], start_old[0]
    slab, rows, columns = state.shape
    scalars = jnp.asarray(scalar_table())[node_index]
    scalars = scalars.at[FIRST].set((slice_index == 0).astype(F32))

    def after(array, other):
        return lax.optimization_barrier((array, other))[0]

    def planes(*lead):
        return (*lead, rows, columns)

    def across(array):
        return lax.ppermute(array, "node", [(node, node ^ 2) for node in range(NODES)])

    def beside(array):
        return lax.ppermute(array, "node", [(node, node ^ 1) for node in range(NODES)])

    always = scalars[WEIGHT] > 0.0

    def swapped(array):
        return lax.cond(always, beside, lambda array: array, array)

    def device(slab_, node, slice_):
        return ((slab_ % slabs) * NODES + node) * slices + slice_

    def spread(array, steps, by):
        pairs = [
            (device(slab_, node, here), device(slab_ + by[node % 2], node, there))
            for slab_ in range(slabs) for node in range(NODES) for here, there in steps
        ]
        return lax.ppermute(array, ("space", "node", "tm"), pairs)

    same = [(slice_, slice_) for slice_ in range(slices)]
    onward = [(slice_, slice_ + 1) for slice_ in range(slices - 1)]

    beside_state = beside(state)
    across_state = across(state)
    send_a, send_b, send_start = call(
        send_kernel, scalars, [state, beside_state, start], [planes(6), planes(4), planes(4)], [], 16
    )
    halo_a = spread(send_a, same, (1, -1))
    halo_b = spread(send_b, same, (1, -1))
    corner_state = swapped(after(across_state, send_a))
    sources = [state, across_state, beside_state, corner_state]
    send_near, send_away = call(end_kernel, scalars, [*sources, start], [planes(5)] * 2, [planes(slab + 2)], 16)
    near = spread(send_near, onward, (0, 0))
    away = spread(send_away, onward, (1, -1))
    across_a = across(after(halo_a, across_state))
    across_b = across(halo_b)
    halo_start = spread(after(send_start, corner_state), [(0, 0)], (1, -1))

    (kept,) = call(first_kernel, scalars, sources, [planes(NODES, kept_count(0))], stage_scratch(0, planes), 30)
    (kept,) = call(
        second_kernel, scalars, [*sources, halo_a, across_a, kept], [planes(NODES, kept_count(1))], stage_scratch(1, planes), 24
    )
    (part,) = call(
        third_kernel, scalars, [halo_a, across_a, halo_b, across_b, kept], [planes(NODES, 5)], stage_scratch(2, planes), 24
    )
    far = beside(after(near, part)[2:])
    mine, swap = call(
        last_kernel, scalars, [start, halo_start, near, far, away, part], [planes(2 * HALF + 1)] * 2,
        [planes(12), planes(11), planes(10), planes(NODES, 5), planes(6)], 24,
    )
    state_new, end_new = call(join_kernel, scalars, [mine, beside(swap)], [planes(slab)] * 2, [], 16)
    return (state_new[None, None], end_new[None])


def solution(mesh):
    return jax.shard_map(
        on_device,
        mesh=mesh,
        in_specs=(P("tm", "space", None, None), P("tm", "node", "space", None, None)),
        out_specs=(P("tm", "node", "space", None, None), P("tm", "space", None, None)),
        check_vma=False,
    )
```

time: 177 us -> 86.1 us (0.49)
  waiting for transfers between devices: 116 us -> 26.3 us
  Pallas kernels: 0 us -> 34.4 us
  other arithmetic: 18.3 us -> 0 us
  between operations: 14.8 us -> 1.46 us
  local copies, waits for them, and re-layouts: 9.72 us -> 4.62 us
    pallas_call x0 -> x7, Pallas kernels: none -> 34.4 us  [call(): pl.pallas_call(kernel, out_shape=[jax.ShapeDtypeStruct(shape, F32) for sh...]
    psum x1 -> x0, waiting for transfers between devices: 34.4 us -> none  [on_device(): weighted_new = lax.psum(node_weight * force_new, 'node')]
    all_gather x1 -> x0, waiting for transfers between devices: 32.9 us -> none  [on_device(): shard_piece = lax.all_gather(force_old[None], 'node', axis=0, tiled=True)]
    ppermute x11 -> x12, waiting for transfers between devices: 48.3 us -> 26.3 us  [the longest x3 14.9 us: across(): lax.ppermute(array, 'node', [(node, node ^ 2) for node in range(NODES)])]
    slice x25 -> x2, local copies, waits for them, and re-layouts: 7.72 us -> 0.67 us  [the longest x1 0.64 us: on_device(): always = scalars[WEIGHT] > 0.0]
    div x4 -> x0, other arithmetic: 6.12 us -> none  [on_device(): iterate = (right_side + implicit * neighbour_sum(widened)) / divisor]
    reduce_sum x1 -> x0, other arithmetic: 4.06 us -> none  [on_device(): jnp.sum(weight_table[:, None, None, None] * shard_piece, axis=0)]
    add x2 -> x0, other arithmetic: 3.34 us -> none  [the longest x1 2.21 us: forcing(): diffusion * laplace + reaction * (values - values * values * values)]
  transfers between devices with their start and end apart: 13 -> 12, of which waited for: 13 -> 5; matrix products, arithmetic and copies ran while one was open for 3% -> 2% of each run, Pallas kernels for 0% -> 33%
where the time goes in v3:
time: 86.1 us; the launch traced here: 85.7 us
  Pallas kernels  34.4 us (40%)
  waiting for transfers between devices  26.3 us (31%)
  starting transfers between devices  18.9 us (22%)
  local copies, waits for them, and re-layouts  4.62 us (5%)
  between operations  1.46 us (2%)
    pallas_call x7, Pallas kernels, call(): pl.pallas_call(kernel, out_shape=[jax.ShapeDtypeStruct(shape, F32) for sh...  34.4 us
    ppermute x3, waiting for transfers between devices, across(): lax.ppermute(array, 'node', [(node, node ^ 2) for node in range(NODES)])  14.9 us
    ppermute x5, starting transfers between devices, spread(): return lax.ppermute(array, ('space', 'node', 'tm'), pairs)  13.1 us
    ppermute x4, waiting for transfers between devices, beside(): lax.ppermute(array, 'node', [(node, node ^ 1) for node in range(NODES)])  7.39 us
    ppermute x3, starting transfers between devices, across(): lax.ppermute(array, 'node', [(node, node ^ 2) for node in range(NODES)])  4.91 us
    ppermute x5, waiting for transfers between devices, spread(): return lax.ppermute(array, ('space', 'node', 'tm'), pairs)  3.96 us
    unnamed x12, local copies, waits for them, and re-layouts  3.25 us
  transfers between devices with their start and end apart: 12, of which 5 were waited for; matrix products, arithmetic and copies ran while one was open for 2% of the time, Pallas kernels for 33%

profile of v3, /device:TPU:0, one launch (start us, length us, event | category | flops | bytes accessed | tf_op | source)
XLA Modules:
  0.0 85.7 jit_solution(2380280392226887862)
XLA Ops:
  1.1 2.6 %collective-permute-start.2 = (f32[8,128,256]{2,1,0:T(8,128)}, f32[8,128,256]{2,1,0:T(8,128)}, u32[]{:S(2)}, u32[]{:S(2)}) collective-permute-start(f32[8,128,256]{2,1,0:T(8,128)} %bitcast.9), channel_id=1, source_target_pairs={{0,4},{2,6},{4,0},{6,2},{1,5},{3,7},{5,1},{7,3},{8,12},{10,14},{12... | collective-permute-start | bytes 3145736 | tf_op jit(solution)/shard_map/ppermute | solution.py:352
  3.7 0.7 dynamic-slice_bitcast_fusion
  4.4 1.2 %copy-done = f32[1,1,8,128,256]{4,3,2,1,0:T(8,128)S(1)} copy-done((f32[1,1,8,128,256]{4,3,2,1,0:T(8,128)S(1)}, f32[1,1,8,128,256]{4,3,2,1,0:T(8,128)}, u32[]{:S(2)}) %copy-start) | copy-done | bytes 1048600
  5.7 1.2 %copy-done.2 = f32[1,8,128,256]{3,2,1,0:T(8,128)S(1)} copy-done((f32[1,8,128,256]{3,2,1,0:T(8,128)S(1)}, f32[1,8,128,256]{3,2,1,0:T(8,128)}, u32[]{:S(2)}) %copy-start.2) | copy-done | bytes 1048600
  6.9 1.5 %shard_map.50 = (f32[6,128,256]{2,1,0:T(8,128)S(1)}, f32[4,128,256]{2,1,0:T(8,128)}, f32[4,128,256]{2,1,0:T(8,128)S(1)}) custom-call(f32[46]{0:T(128)S(1)} %constant_dynamic-update-slice_fusion.scalars, f32[8,128,256]{2,1,0:T(8,128)S(1)} %bitcast.10, f32[8,128,256]{2,1,0:T(8,128)S(1)} %collective-permute-done.1.beside, f32[8,128,256]{2,1,0:T(8,128)S(1)} %bitcast.14), custom_call_target="tpu_custom_call" | custom-call | flops 1000 | bytes 1000 | tf_op jit(solution)/shard_map/pallas_call | solution.py:325
  8.3 0.8 copy-done.4
  9.1 2.2 %collective-permute-start.5 = (f32[6,128,256]{2,1,0:T(8,128)S(1)}, f32[6,128,256]{2,1,0:T(8,128)}, u32[]{:S(2)}, u32[]{:S(2)}) collective-permute-start(f32[6,128,256]{2,1,0:T(8,128)S(1)} %get-tuple-element.33), channel_id=1, source_target_pairs={{0,8},{1,9},{2,26},{3,27},{4,12},{5,13},{6,30},{7,31},{8,16},{9,17... | collective-permute-start | bytes 2359304 | tf_op jit(solution)/shard_map/ppermute | solution.py:370
  11.3 1.6 %collective-permute-start.7 = (f32[4,128,256]{2,1,0:T(8,128)}, f32[4,128,256]{2,1,0:T(8,128)}, u32[]{:S(2)}, u32[]{:S(2)}) collective-permute-start(f32[4,128,256]{2,1,0:T(8,128)} %get-tuple-element.38), channel_id=1, source_target_pairs={{0,8},{1,9},{2,26},{3,27},{4,12},{5,13},{6,30},{7,31},{8,16},{9,17... | collective-permute-start | bytes 1572872 | tf_op jit(solution)/shard_map/ppermute | solution.py:370
  12.9 14.9 %collective-permute-done.2.across = f32[8,128,256]{2,1,0:T(8,128)} collective-permute-done((f32[8,128,256]{2,1,0:T(8,128)}, f32[8,128,256]{2,1,0:T(8,128)}, u32[]{:S(2)}, u32[]{:S(2)}) %collective-permute-start.2) | collective-permute-done | bytes 1048608 | tf_op jit(solution)/shard_map/ppermute | solution.py:352
  27.8 4.0 %collective-permute-done.5.halo_a = f32[6,128,256]{2,1,0:T(8,128)} collective-permute-done((f32[6,128,256]{2,1,0:T(8,128)S(1)}, f32[6,128,256]{2,1,0:T(8,128)}, u32[]{:S(2)}, u32[]{:S(2)}) %collective-permute-start.5) | collective-permute-done | bytes 786464 | tf_op jit(solution)/shard_map/ppermute | solution.py:370
  31.7 1.7 %collective-permute-start.6 = (f32[6,128,256]{2,1,0:T(8,128)}, f32[6,128,256]{2,1,0:T(8,128)}, u32[]{:S(2)}, u32[]{:S(2)}) collective-permute-start(f32[6,128,256]{2,1,0:T(8,128)} %collective-permute-done.5.halo_a), channel_id=1, source_target_pairs={{0,4},{2,6},{4,0},{6,2},{1,5},{3,7},{5,1},{7,3},{8,12},{10,14},{12... | collective-permute-start | bytes 2359304 | tf_op jit(solution)/shard_map/ppermute | solution.py:352
  34.8 3.1 %conditional.1 = (f32[8,128,256]{2,1,0:T(8,128)}) conditional(s32[]{:T(128)} %bitcast.4, f32[8,128,256]{2,1,0:T(8,128)} %collective-permute-done.2.across, f32[8,128,256]{2,1,0:T(8,128)} %collective-permute-done.2.across), branch_computations={%region_0.0_spmd, %region_1.0_spmd} | conditional | bytes 4194352 | solution.py:360
  34.9 3.0 %collective-permute-done = f32[8,128,256]{2,1,0:T(8,128)} collective-permute-done((f32[8,128,256]{2,1,0:T(8,128)}, f32[8,128,256]{2,1,0:T(8,128)}, u32[]{:S(2)}, u32[]{:S(2)}) %collective-permute-start) | collective-permute-done | bytes 1048608 | tf_op jit(solution)/shard_map/cond/branch_1_fun/ppermute | solution.py:355
  37.9 3.2 %shard_map.51 = (f32[5,128,256]{2,1,0:T(8,128)S(1)}, f32[5,128,256]{2,1,0:T(8,128)S(1)}) custom-call(f32[46]{0:T(128)S(1)} %constant_dynamic-update-slice_fusion.scalars, f32[8,128,256]{2,1,0:T(8,128)S(1)} %bitcast.11, f32[8,128,256]{2,1,0:T(8,128)} %collective-permute-done.2.across, f32[8,128,256]{2,1,0:T(8,128)S(1)} %collective-permute-done.1.beside, ...), custom_call_target="tpu_custom_call" | custom-call | flops 1000 | bytes 1000 | tf_op jit(solution)/shard_map/pallas_call | solution.py:325
  41.1 3.5 %collective-permute-start.4 = (f32[5,128,256]{2,1,0:T(8,128)S(1)}, f32[5,128,256]{2,1,0:T(8,128)S(1)}, u32[]{:S(2)}, u32[]{:S(2)}) collective-permute-start(f32[5,128,256]{2,1,0:T(8,128)S(1)} %get-tuple-element.36), channel_id=1, source_target_pairs={{0,1},{2,3},{4,5},{6,7},{8,9},{10,11},{12,13},{14,15},{16,17},{18,... | collective-permute-start | bytes 1966088 | tf_op jit(solution)/shard_map/ppermute | solution.py:370
  45.2 1.3 %collective-permute-start.10 = (f32[5,128,256]{2,1,0:T(8,128)S(1)}, f32[5,128,256]{2,1,0:T(8,128)S(1)}, u32[]{:S(2)}, u32[]{:S(2)}) collective-permute-start(f32[5,128,256]{2,1,0:T(8,128)S(1)} %get-tuple-element.40), channel_id=1, source_target_pairs={{0,9},{2,27},{4,13},{6,31},{8,17},{10,3},{12,21},{14,7},{16,25},{1... | collective-permute-start | bytes 1966088 | tf_op jit(solution)/shard_map/ppermute | solution.py:370
  46.5 4.6 %collective-permute-start.3 = (f32[4,128,256]{2,1,0:T(8,128)S(1)}, f32[4,128,256]{2,1,0:T(8,128)S(1)}, u32[]{:S(2)}, u32[]{:S(2)}) collective-permute-start(f32[4,128,256]{2,1,0:T(8,128)S(1)} %copy-done.5), channel_id=1, source_target_pairs={{0,8},{2,26},{4,12},{6,30},{8,16},{10,2},{12,20},{14,6},{16,24},{1... | collective-permute-start | bytes 1572872 | tf_op jit(solution)/shard_map/ppermute | solution.py:370
  51.1 9.7 %shard_map.52.kept = f32[4,12,128,256]{3,2,1,0:T(8,128)S(1)} custom-call(f32[46]{0:T(128)S(1)} %constant_dynamic-update-slice_fusion.scalars, f32[8,128,256]{2,1,0:T(8,128)S(1)} %bitcast.12, f32[8,128,256]{2,1,0:T(8,128)} %collective-permute-done.2.across, f32[8,128,256]{2,1,0:T(8,128)S(1)} %collective-permute-done.1.beside, ...), custom_call_target="tpu_custom_call" | custom-call | flops 1000 | bytes 1000 | tf_op jit(solution)/shard_map/pallas_call | solution.py:325
  60.8 8.5 %shard_map.53.kept = f32[4,15,128,256]{3,2,1,0:T(8,128)S(1)} custom-call(f32[46]{0:T(128)S(1)} %constant_dynamic-update-slice_fusion.scalars, f32[8,128,256]{2,1,0:T(8,128)S(1)} %bitcast.13, f32[8,128,256]{2,1,0:T(8,128)} %collective-permute-done.2.across, f32[8,128,256]{2,1,0:T(8,128)S(1)} %collective-permute-done.1.beside, ...), custom_call_target="tpu_custom_call" | custom-call | flops 1000 | bytes 1000 | tf_op jit(solution)/shard_map/pallas_call | solution.py:325
  69.4 5.7 %shard_map.54.part = f32[4,5,128,256]{3,2,1,0:T(8,128)S(1)} custom-call(f32[46]{0:T(128)S(1)} %constant_dynamic-update-slice_fusion.scalars, f32[6,128,256]{2,1,0:T(8,128)} %collective-permute-done.5.halo_a, f32[6,128,256]{2,1,0:T(8,128)} %collective-permute-done.6.across_a, f32[4,128,256]{2,1,0:T(8,128)} %collective-permute-done.7.halo_b, ...), custom_call_target="tpu_custom_call" | custom-call | flops 1000 | bytes 1000 | tf_op jit(solution)/shard_map/pallas_call | solution.py:325
  75.2 1.7 %collective-permute-done.9.far = f32[3,128,256]{2,1,0:T(8,128)S(1)} collective-permute-done((f32[3,128,256]{2,1,0:T(8,128)S(1)}, f32[3,128,256]{2,1,0:T(8,128)S(1)}, u32[]{:S(2)}, u32[]{:S(2)}) %collective-permute-start.9) | collective-permute-done | bytes 393248 | tf_op jit(solution)/shard_map/ppermute | solution.py:355
  76.9 3.9 %shard_map.55 = (f32[9,128,256]{2,1,0:T(8,128)S(1)}, f32[9,128,256]{2,1,0:T(8,128)S(1)}) custom-call(f32[46]{0:T(128)S(1)} %constant_dynamic-update-slice_fusion.scalars, f32[8,128,256]{2,1,0:T(8,128)S(1)} %bitcast.16, f32[4,128,256]{2,1,0:T(8,128)S(1)} %collective-permute-done.3.halo_start, f32[5,128,256]{2,1,0:T(8,128)S(1)} %collective-permute-done.4.near, ...), custom_call_target="tpu_custom_call" | custom-call | flops 1000 | bytes 1000 | tf_op jit(solution)/shard_map/pallas_call | solution.py:325
  81.0 2.7 %collective-permute-done.11.other = f32[9,128,256]{2,1,0:T(8,128)S(1)} collective-permute-done((f32[9,128,256]{2,1,0:T(8,128)S(1)}, f32[9,128,256]{2,1,0:T(8,128)S(1)}, u32[]{:S(2)}, u32[]{:S(2)}) %collective-permute-start.11) | collective-permute-done | bytes 1179680 | tf_op jit(solution)/shard_map/ppermute | solution.py:355
  83.7 2.0 %shard_map.56 = (f32[8,128,256]{2,1,0:T(8,128)}, f32[8,128,256]{2,1,0:T(8,128)}) custom-call(f32[46]{0:T(128)S(1)} %constant_dynamic-update-slice_fusion.scalars, f32[9,128,256]{2,1,0:T(8,128)S(1)} %get-tuple-element.41.mine, f32[9,128,256]{2,1,0:T(8,128)S(1)} %collective-permute-done.11.other), custom_call_target="tpu_custom_call" | custom-call | flops 1000 | bytes 1000 | tf_op jit(solution)/shard_map/pallas_call | solution.py:325
  (24 shorter events, 2.2 us)
Async XLA Ops:
  0.6 3.8 %collective-permute-start.1 = (f32[8,128,256]{2,1,0:T(8,128)}, f32[8,128,256]{2,1,0:T(8,128)S(1)}, u32[]{:S(2)}, u32[]{:S(2)}) collective-permute-start(f32[8,128,256]{2,1,0:T(8,128)} %bitcast.8), channel_id=1, source_target_pairs={{0,2},{2,0},{4,6},{6,4},{1,3},{3,1},{5,7},{7,5},{8,10},{10,8},{12,... | collective-permute-start | bytes 3145736 | tf_op jit(solution)/shard_map/ppermute | solution.py:355
  1.1 26.6 %collective-permute-start.2 = (f32[8,128,256]{2,1,0:T(8,128)}, f32[8,128,256]{2,1,0:T(8,128)}, u32[]{:S(2)}, u32[]{:S(2)}) collective-permute-start(f32[8,128,256]{2,1,0:T(8,128)} %bitcast.9), channel_id=1, source_target_pairs={{0,4},{2,6},{4,0},{6,2},{1,5},{3,7},{5,1},{7,3},{8,12},{10,14},{12... | collective-permute-start | bytes 3145736 | tf_op jit(solution)/shard_map/ppermute | solution.py:352
  4.4 1.2 %copy-start = (f32[1,1,8,128,256]{4,3,2,1,0:T(8,128)S(1)}, f32[1,1,8,128,256]{4,3,2,1,0:T(8,128)}, u32[]{:S(2)}) copy-start(f32[1,1,8,128,256]{4,3,2,1,0:T(8,128)} %param.8) | copy-start | bytes 3145732
  5.6 1.2 %copy-start.2 = (f32[1,8,128,256]{3,2,1,0:T(8,128)S(1)}, f32[1,8,128,256]{3,2,1,0:T(8,128)}, u32[]{:S(2)}) copy-start(f32[1,8,128,256]{3,2,1,0:T(8,128)} %param.7) | copy-start | bytes 3145732
  6.9 31.0 %copy-start.1 = (f32[1,1,8,128,256]{4,3,2,1,0:T(8,128)S(1)}, f32[1,1,8,128,256]{4,3,2,1,0:T(8,128)}, u32[]{:S(2)}) copy-start(f32[1,1,8,128,256]{4,3,2,1,0:T(8,128)} %param.8) | copy-start | bytes 3145732
  6.9 31.0 %copy-start.3 = (f32[1,8,128,256]{3,2,1,0:T(8,128)S(1)}, f32[1,8,128,256]{3,2,1,0:T(8,128)}, u32[]{:S(2)}) copy-start(f32[1,8,128,256]{3,2,1,0:T(8,128)} %param.7) | copy-start | bytes 3145732
  8.3 0.8 copy-start.4
  9.1 22.6 %collective-permute-start.5 = (f32[6,128,256]{2,1,0:T(8,128)S(1)}, f32[6,128,256]{2,1,0:T(8,128)}, u32[]{:S(2)}, u32[]{:S(2)}) collective-permute-start(f32[6,128,256]{2,1,0:T(8,128)S(1)} %get-tuple-element.33), channel_id=1, source_target_pairs={{0,8},{1,9},{2,26},{3,27},{4,12},{5,13},{6,30},{7,31},{8,16},{9,17... | collective-permute-start | bytes 2359304 | tf_op jit(solution)/shard_map/ppermute | solution.py:370
  11.3 33.3 %collective-permute-start.7 = (f32[4,128,256]{2,1,0:T(8,128)}, f32[4,128,256]{2,1,0:T(8,128)}, u32[]{:S(2)}, u32[]{:S(2)}) collective-permute-start(f32[4,128,256]{2,1,0:T(8,128)} %get-tuple-element.38), channel_id=1, source_target_pairs={{0,8},{1,9},{2,26},{3,27},{4,12},{5,13},{6,30},{7,31},{8,16},{9,17... | collective-permute-start | bytes 1572872 | tf_op jit(solution)/shard_map/ppermute | solution.py:370
  31.7 29.1 %collective-permute-start.6 = (f32[6,128,256]{2,1,0:T(8,128)}, f32[6,128,256]{2,1,0:T(8,128)}, u32[]{:S(2)}, u32[]{:S(2)}) collective-permute-start(f32[6,128,256]{2,1,0:T(8,128)} %collective-permute-done.5.halo_a), channel_id=1, source_target_pairs={{0,4},{2,6},{4,0},{6,2},{1,5},{3,7},{5,1},{7,3},{8,12},{10,14},{12... | collective-permute-start | bytes 2359304 | tf_op jit(solution)/shard_map/ppermute | solution.py:352
  34.8 3.1 %collective-permute-start = (f32[8,128,256]{2,1,0:T(8,128)}, f32[8,128,256]{2,1,0:T(8,128)}, u32[]{:S(2)}, u32[]{:S(2)}) collective-permute-start(f32[8,128,256]{2,1,0:T(8,128)} %param.3), channel_id=1, source_target_pairs={{0,2},{2,0},{4,6},{6,4},{1,3},{3,1},{5,7},{7,5},{8,10},{10,8},{12,... | collective-permute-start | bytes 3145736 | tf_op jit(solution)/shard_map/cond/branch_1_fun/ppermute | solution.py:355
  37.9 8.6 %copy-start.5 = (f32[4,128,256]{2,1,0:T(8,128)S(1)}, f32[4,128,256]{2,1,0:T(8,128)}, u32[]{:S(2)}) copy-start(f32[4,128,256]{2,1,0:T(8,128)} %copy-done.4) | copy-start | bytes 1572868
  41.1 34.0 %collective-permute-start.4 = (f32[5,128,256]{2,1,0:T(8,128)S(1)}, f32[5,128,256]{2,1,0:T(8,128)S(1)}, u32[]{:S(2)}, u32[]{:S(2)}) collective-permute-start(f32[5,128,256]{2,1,0:T(8,128)S(1)} %get-tuple-element.36), channel_id=1, source_target_pairs={{0,1},{2,3},{4,5},{6,7},{8,9},{10,11},{12,13},{14,15},{16,17},{18,... | collective-permute-start | bytes 1966088 | tf_op jit(solution)/shard_map/ppermute | solution.py:370
  44.6 24.8 %collective-permute-start.8 = (f32[4,128,256]{2,1,0:T(8,128)}, f32[4,128,256]{2,1,0:T(8,128)S(1)}, u32[]{:S(2)}, u32[]{:S(2)}) collective-permute-start(f32[4,128,256]{2,1,0:T(8,128)} %collective-permute-done.7.halo_b), channel_id=1, source_target_pairs={{0,4},{2,6},{4,0},{6,2},{1,5},{3,7},{5,1},{7,3},{8,12},{10,14},{12... | collective-permute-start | bytes 1572872 | tf_op jit(solution)/shard_map/ppermute | solution.py:352
  45.2 30.1 %collective-permute-start.10 = (f32[5,128,256]{2,1,0:T(8,128)S(1)}, f32[5,128,256]{2,1,0:T(8,128)S(1)}, u32[]{:S(2)}, u32[]{:S(2)}) collective-permute-start(f32[5,128,256]{2,1,0:T(8,128)S(1)} %get-tuple-element.40), channel_id=1, source_target_pairs={{0,9},{2,27},{4,13},{6,31},{8,17},{10,3},{12,21},{14,7},{16,25},{1... | collective-permute-start | bytes 1966088 | tf_op jit(solution)/shard_map/ppermute | solution.py:370
  46.5 28.7 %collective-permute-start.3 = (f32[4,128,256]{2,1,0:T(8,128)S(1)}, f32[4,128,256]{2,1,0:T(8,128)S(1)}, u32[]{:S(2)}, u32[]{:S(2)}) collective-permute-start(f32[4,128,256]{2,1,0:T(8,128)S(1)} %copy-done.5), channel_id=1, source_target_pairs={{0,8},{2,26},{4,12},{6,30},{8,16},{10,2},{12,20},{14,6},{16,24},{1... | collective-permute-start | bytes 1572872 | tf_op jit(solution)/shard_map/ppermute | solution.py:370
  75.1 1.8 %collective-permute-start.9 = (f32[3,128,256]{2,1,0:T(8,128)S(1)}, f32[3,128,256]{2,1,0:T(8,128)S(1)}, u32[]{:S(2)}, u32[]{:S(2)}) collective-permute-start(f32[3,128,256]{2,1,0:T(8,128)S(1)} %slice.16), channel_id=1, source_target_pairs={{0,2},{2,0},{4,6},{6,4},{1,3},{3,1},{5,7},{7,5},{8,10},{10,8},{12,... | collective-permute-start | bytes 1179656 | tf_op jit(solution)/shard_map/ppermute | solution.py:355
  80.8 2.9 %collective-permute-start.11 = (f32[9,128,256]{2,1,0:T(8,128)S(1)}, f32[9,128,256]{2,1,0:T(8,128)S(1)}, u32[]{:S(2)}, u32[]{:S(2)}) collective-permute-start(f32[9,128,256]{2,1,0:T(8,128)S(1)} %get-tuple-element.42), channel_id=1, source_target_pairs={{0,2},{2,0},{4,6},{6,4},{1,3},{3,1},{5,7},{7,5},{8,10},{10,8},{12,... | collective-permute-start | bytes 3538952 | tf_op jit(solution)/shard_map/ppermute | solution.py:355

commit v4 on v3

v4 whole, which is shorter than its diff:
```python
import functools

import jax
import jax.numpy as jnp
import numpy as np
from jax import lax
from jax.experimental import pallas as pl
from jax.experimental.pallas import tpu as pltpu
from jax.sharding import PartitionSpec as P

NODES = 4
PASSES = 4

time_step = 0.25
diffusion = 4.0
reaction = 1.0

F32 = jnp.float32

OUTER = 5
SLAB = 8
HALF = 4


def collocation(count):
    points = [-0.8611363115940526, -0.3399810435848563, 0.3399810435848563, 0.8611363115940526]
    raw_weights = [0.3478548451374538, 0.6521451548625461, 0.6521451548625461, 0.3478548451374538]
    node_times = [(point + 1.0) / 2.0 for point in points]
    quadrature = [[0.0 for column in range(count)] for target in range(count)]
    for source in range(count):
        coeffs = [1.0]
        scaling = 1.0
        for other in range(count):
            if other != source:
                other_time = node_times[other]
                shifted = [0.0] + coeffs
                for power in range(len(coeffs)):
                    shifted[power] = shifted[power] - other_time * coeffs[power]
                coeffs = shifted
                scaling = scaling * (node_times[source] - other_time)
        for target in range(count):
            target_time = node_times[target]
            integral = 0.0
            for power in range(len(coeffs)):
                integral = integral + coeffs[power] * target_time ** (power + 1) / (power + 1)
            quadrature[target][source] = integral / scaling
    return (node_times, quadrature, [weight / 2.0 for weight in raw_weights])


LIN, CUB, WEIGHT, MIX, SCALE, FIRST, CORE, COUNT = 0, 16, 32, 36, 40, 44, 45, 46


def scalar_table():
    times, quad, weights = collocation(NODES)
    table = np.zeros((NODES, COUNT), np.float64)
    for node in range(NODES):
        order = [node, node ^ 2, node ^ 1, node ^ 3]
        for place, target in enumerate(order):
            implicit = time_step * diffusion * times[target]
            scale = 1.0 / (1.0 + 6.0 * implicit)
            for index, source in enumerate(order):
                lin = time_step * diffusion * quad[target][source] - (implicit if source == target else 0.0)
                table[node, LIN + 4 * place + index] = scale * lin
                table[node, CUB + 4 * place + index] = scale * time_step * reaction * quad[target][source]
            table[node, WEIGHT + place] = weights[target]
            table[node, MIX + place] = scale * implicit
            table[node, SCALE + place] = scale
        table[node, CORE] = node & 1
    return table.astype(np.float32)


class Plane:
    def __init__(self, ref, *index):
        self.ref, self.index = ref, index

    def rows(self, first, count):
        return self.ref[(*self.index, pl.ds(first, count))]

    def put(self, first, value):
        self.ref[(*self.index, pl.ds(first, value.shape[0]))] = value


def flat_sum(plane, first, count):
    whole = plane.ref.shape[-2]
    centre = plane.rows(first, count)
    above, below = plane.rows((first - 8) % whole, 8), plane.rows((first + count) % whole, 8)
    longer = jnp.concatenate([above, centre, below], axis=0)
    vertical = pltpu.roll(longer, 1, 0)[8 : 8 + count] + pltpu.roll(longer, count + 15, 0)[8 : 8 + count]
    columns = centre.shape[1]
    return vertical + (pltpu.roll(centre, 1, 1) + pltpu.roll(centre, columns - 1, 1)), centre


def around(outside, plane, inside, first, count):
    flat, centre = flat_sum(plane, first, count)
    return (outside.rows(first, count) + inside.rows(first, count)) + flat, centre


def chunks(plane, count):
    return range(0, plane.ref.shape[-2], count)


def mixed(scalars, base, planes):
    own, across, beside, corner = (scalars[base + index] * plane for index, plane in enumerate(planes))
    return (own + across) + (beside + corner)


def cubed(state):
    return state - state * state * state


def counter(scalars):
    upper = (scalars[CORE] > 0.5).astype(jnp.int32)
    base, sign = upper * (SLAB - 1), 1 - 2 * upper
    return lambda place: base + sign * (place - OUTER)


def send_kernel(scalars, own, beside, halo_a, halo_b):
    plane = counter(scalars)
    for number, source in enumerate((own, beside)):
        for index in range(3):
            halo_a[index + 3 * number] = source[plane(10 + index)]
        for index in range(2):
            halo_b[index + 2 * number] = source[plane(8 + index)]


def end_kernel(scalars, own, across, beside, corner, start, near, away, total):
    plane = counter(scalars)
    sources = (own, across, beside, corner)
    weighted = [Plane(total, index) for index in range(SLAB + 2)]
    for first in chunks(weighted[0], 32):
        nothing = jnp.zeros_like(weighted[0].rows(first, 32))
        weighted[0].put(first, nothing)
        weighted[SLAB + 1].put(first, nothing)
        for index in range(SLAB):
            here = plane(index + OUTER)
            weighted[index + 1].put(first, mixed(scalars, WEIGHT, [Plane(source, here).rows(first, 32) for source in sources]))
    for index in range(SLAB):
        here = plane(index + OUTER)
        out = Plane(near, index + 1) if index < HALF else Plane(away, index - HALF)
        for first in chunks(out, 32):
            local = mixed(scalars, WEIGHT, [cubed(Plane(source, here).rows(first, 32)) for source in sources])
            nearby, centre = around(*weighted[index : index + 3], first, 32)
            force = diffusion * (nearby - 6.0 * centre) + reaction * local
            out.put(first, Plane(start, here).rows(first, 32) + time_step * force)
    near[0] = (time_step * diffusion) * total[1]
    away[HALF] = (time_step * diffusion) * total[SLAB]


NAMES = ("g", "x1", "x2", "x3", "x4")
STAGES = [
    {"g": range(6, 12), "x1": range(6, 12), "x2": range(7, 11), "x3": range(8, 10), "x4": ()},
    {"g": range(3, 6), "x1": range(3, 6), "x2": range(4, 7), "x3": range(5, 8), "x4": range(6, 9)},
    {"g": range(1, 3), "x1": range(1, 3), "x2": range(2, 4), "x3": range(3, 5), "x4": range(4, 6)},
]
KEPT = [
    {"g": (6, 7, 8), "x1": (6, 7), "x2": (7, 8), "x3": (8, 9), "x4": ()},
    {"g": (3, 4, 5), "x1": (3, 4), "x2": (4, 5), "x3": (5, 6), "x4": (6, 7, 8)},
    {"g": (), "x1": (), "x2": (), "x3": (), "x4": (4, 5)},
]


def kept_keys(stage):
    return [(name, place) for name in NAMES for place in KEPT[stage][name]]


def spare_keys(stage):
    return [(name, place) for name in NAMES for place in STAGES[stage][name] if place not in KEPT[stage][name]]


def run_stage(stage, scalars, state, old, out, spare):
    where = {}
    for ref, keys in ((old, kept_keys(stage - 1) if stage else []), (out, kept_keys(stage)), (spare, spare_keys(stage))):
        where.update({key: (ref, index) for index, key in enumerate(keys)})

    def plane(name, target, place):
        ref, index = where[name, place]
        return Plane(ref, target, index)

    targets = range(NODES)
    for place in STAGES[stage]["g"]:
        sources = [[state(source, place + by) for by in (-1, 0, 1)] for source in range(NODES)]
        for first in chunks(sources[0][0], 16):
            nearby, centre = zip(*(around(*planes, first, 16) for planes in sources))
            spread_ = [value - 6.0 * middle for value, middle in zip(nearby, centre)]
            local = [cubed(middle) for middle in centre]
            for target in targets:
                value = mixed(scalars, LIN + 4 * target, spread_) + mixed(scalars, CUB + 4 * target, local)
                plane("g", target, place).put(first, value)
                plane("x1", target, place).put(first, value + scalars[MIX + target] * nearby[target])
    for name, before in (("x2", "x1"), ("x3", "x2"), ("x4", "x3")):
        for place in STAGES[stage][name]:
            for target in targets:
                planes = [plane(before, target, place + by) for by in (-1, 0, 1)]
                base, sink = plane("g", target, place), plane(name, target, place)
                for first in chunks(sink, 32):
                    nearby, _ = around(*planes, first, 32)
                    sink.put(first, base.rows(first, 32) + scalars[MIX + target] * nearby)


def first_kernel(scalars, own, across, beside, corner, out, spare):
    plane = counter(scalars)
    sources = (own, across, beside, corner)
    run_stage(0, scalars, lambda source, place: Plane(sources[source], plane(place)), None, out, spare)


def halo_state(halo, halo_across, first, count):
    def state(source, place):
        ref = (halo, halo_across, halo, halo_across)[source]
        return Plane(ref, (count if source >= 2 else 0) + place - first)

    return state


def second_kernel(scalars, own, across, beside, corner, halo_a, across_a, kept, out, spare):
    plane = counter(scalars)
    sources = (own, across, beside, corner)
    outer = halo_state(halo_a, across_a, 2, 3)

    def state(source, place):
        return outer(source, place) if place < OUTER else Plane(sources[source], plane(place))

    run_stage(1, scalars, state, kept, out, spare)


def third_kernel(scalars, halo_a, across_a, halo_b, across_b, kept, out, spare):
    inner, outer = halo_state(halo_a, across_a, 2, 3), halo_state(halo_b, across_b, 0, 2)

    def state(source, place):
        return outer(source, place) if place < 2 else inner(source, place)

    run_stage(2, scalars, state, kept, out, spare)


def last_kernel(scalars, start, halo_start, near, far, away, kept, part, mine, swap, begin, once, twice, last, total):
    plane = counter(scalars)
    begin_first = scalars[FIRST]
    back = (scalars[CORE] > 0.5).astype(jnp.int32)
    for place in range(1, 5):
        begin[place] = halo_start[place - 1 + back * (5 - 2 * place)] + away[place - 1]
    begin[4] = begin[4] + near[0]
    begin[5] = (begin_first * start[plane(5)] + near[1]) + away[4]
    for place in range(6, 9):
        begin[place] = begin_first * start[plane(place)] + near[place - 4]
    for place in range(9, 12):
        begin[place] = begin_first * start[plane(place)] + far[11 - place]

    def around_place(ref, place, first, count):
        return around(*(Plane(ref, place + by) for by in (-1, 0, 1)), first, count)

    for source, sink, places in ((begin, once, range(2, 11)), (once, twice, range(3, 10))):
        for place in places:
            out = Plane(sink, place)
            for first in chunks(out, 32):
                out.put(first, around_place(source, place, first, 32)[0])
    kept_x4 = {key: index for index, key in enumerate(kept_keys(1))}
    for place in range(4, 9):
        for first in chunks(Plane(total, 0), 16):
            thrice, two = around_place(twice, place, first, 16)
            zero, one = Plane(begin, place).rows(first, 16), Plane(once, place).rows(first, 16)
            values = []
            for target in range(NODES):
                mix = scalars[MIX + target]
                rest = Plane(part, target, place - 4) if place < 6 else Plane(kept, target, kept_x4["x4", place])
                value = scalars[SCALE + target] * (zero + mix * (one + mix * (two + mix * thrice)))
                values.append(rest.rows(first, 16) + value)
                Plane(last, target, place - 4).put(first, values[-1])
            Plane(total, place - 4).put(first, mixed(scalars, WEIGHT, values))
    total[5] = jnp.zeros_like(total[5])
    for place in range(OUTER, OUTER + HALF):
        index = place - 4
        for first in chunks(Plane(total, 0), 16):
            states = [Plane(last, target, index).rows(first, 16) for target in range(NODES)]
            local = mixed(scalars, WEIGHT, [cubed(state) for state in states])
            nearby, centre = around_place(total, index, first, 16)
            force = diffusion * (nearby - 6.0 * centre) + reaction * local
            value = Plane(begin, place).rows(first, 16) + time_step * force
            for sink, state in ((mine, states[0]), (swap, states[2])):
                Plane(sink, index - 1).put(first, state)
                Plane(sink, index - 1 + HALF).put(first, value)
    mine[2 * HALF] = total[HALF]
    swap[2 * HALF] = total[HALF]


def join_kernel(scalars, mine, other, state, end):
    plane = counter(scalars)
    for index in range(HALF):
        near, far = plane(OUTER + index), plane(OUTER + SLAB - 1 - index)
        state[near] = mine[index]
        state[far] = other[index]
        own, others = mine[HALF + index], other[HALF + index]
        if index == HALF - 1:
            own = own + (time_step * diffusion) * other[2 * HALF]
            others = others + (time_step * diffusion) * mine[2 * HALF]
        end[near] = own
        end[far] = others


def call(kernel, scalars, operands, outs, scratch, limit):
    return pl.pallas_call(
        kernel,
        out_shape=[jax.ShapeDtypeStruct(shape, F32) for shape in outs],
        in_specs=[pl.BlockSpec(memory_space=pltpu.SMEM)] + [pl.BlockSpec(memory_space=pltpu.VMEM)] * len(operands),
        out_specs=[pl.BlockSpec(memory_space=pltpu.VMEM)] * len(outs),
        scratch_shapes=[pltpu.VMEM(shape, F32) for shape in scratch],
        compiler_params=pltpu.CompilerParams(vmem_limit_bytes=limit << 20),
        cost_estimate=pl.CostEstimate(flops=1000, bytes_accessed=1000, transcendentals=0),
    )(scalars, *operands)


def on_device(start_old, nodes_old):
    slabs, slices = lax.axis_size("space"), lax.axis_size("tm")
    node_index = lax.axis_index("node")
    slice_index = lax.axis_index("tm")
    state, start = nodes_old[0, 0], start_old[0]
    slab, rows, columns = state.shape
    scalars = jnp.asarray(scalar_table())[node_index]
    scalars = scalars.at[FIRST].set((slice_index == 0).astype(F32))

    def after(array, other):
        return lax.optimization_barrier((array, other))[0]

    def planes(*lead):
        return (*lead, rows, columns)

    def across(array):
        return lax.ppermute(array, "node", [(node, node ^ 2) for node in range(NODES)])

    def beside(array):
        return lax.ppermute(array, "node", [(node, node ^ 1) for node in range(NODES)])

    always = scalars[WEIGHT] > 0.0

    def swapped(array):
        return lax.cond(always, beside, lambda array: array, array)

    def device(slab_, node, slice_):
        return ((slab_ % slabs) * NODES + node) * slices + slice_

    def spread(array, steps, by):
        pairs = [
            (device(slab_, node, here), device(slab_ + by[node % 2], node, there))
            for slab_ in range(slabs) for node in range(NODES) for here, there in steps
        ]
        return lax.ppermute(array, ("space", "node", "tm"), pairs)

    same = [(slice_, slice_) for slice_ in range(slices)]
    onward = [(slice_, slice_ + 1) for slice_ in range(slices - 1)]

    beside_state = beside(state)
    across_state = across(state)
    send_a, send_b = call(send_kernel, scalars, [state, beside_state], [planes(6), planes(4)], [], 16)
    halo_a = spread(send_a, same, (1, -1))
    halo_b = spread(send_b, same, (1, -1))
    corner_state = swapped(after(across_state, send_a))
    sources = [state, across_state, beside_state, corner_state]
    first_start = lax.dynamic_slice_in_dim(start, HALF * (1 - lax.rem(node_index, 2)), HALF, axis=0)
    passing_start = spread(first_start, [(0, 1)], (0, 0))
    send_near, send_away = call(
        end_kernel, scalars, [*sources, after(start, passing_start)], [planes(5), planes(5)], [planes(slab + 2)], 16
    )
    near = spread(send_near, onward, (0, 0))
    away = spread(send_away, onward, (1, -1))
    across_a = across(after(halo_a, corner_state))
    halo_start = spread(passing_start, [(1, 0)], (1, -1))

    def stage(index, kernel, operands, limit):
        shapes = [planes(NODES, len(keys)) for keys in (kept_keys(index), spare_keys(index))]
        return call(kernel, scalars, operands, shapes[:1], shapes[1:], limit)[0]

    kept = stage(0, first_kernel, sources, 24)
    across_b = across(halo_b)
    kept = stage(1, second_kernel, [*sources, halo_a, across_a, kept], 24)
    part = stage(2, third_kernel, [halo_a, across_a, halo_b, across_b, kept], 24)
    far = beside(after(near, part)[2:])
    mine, swap = call(
        last_kernel, scalars, [start, halo_start, near, far, away, kept, part], [planes(2 * HALF + 1)] * 2,
        [planes(12), planes(11), planes(10), planes(NODES, 5), planes(6)], 24,
    )
    state_new, end_new = call(join_kernel, scalars, [mine, beside(swap)], [planes(slab)] * 2, [], 16)
    return (state_new[None, None], end_new[None])


def solution(mesh):
    return jax.shard_map(
        on_device,
        mesh=mesh,
        in_specs=(P("tm", "space", None, None), P("tm", "node", "space", None, None)),
        out_specs=(P("tm", "node", "space", None, None), P("tm", "space", None, None)),
        check_vma=False,
    )
```

time: 86.1 us -> 78.7 us (0.914)
  waiting for transfers between devices: 26.3 us -> 20.7 us
  Pallas kernels: 34.4 us -> 29.2 us
  starting transfers between devices: 18.9 us -> 22.8 us
    pallas_call x7, Pallas kernels: 34.4 us -> 29.2 us  [call(): pl.pallas_call(kernel, out_shape=[jax.ShapeDtypeStruct(shape, F32) for sh...]
    ppermute x3, waiting for transfers between devices: 14.9 us -> 10.9 us  [across(): lax.ppermute(array, 'node', [(node, node ^ 2) for node in range(NODES)])]
    ppermute x5 -> x6, starting transfers between devices: 13.1 us -> 15.1 us  [spread(): return lax.ppermute(array, ('space', 'node', 'tm'), pairs)]
    unnamed x12 -> x8, local copies, waits for them, and re-layouts: 3.25 us -> 2.03 us
    ppermute x4, starting transfers between devices: 0.86 us -> 1.92 us  [beside(): lax.ppermute(array, 'node', [(node, node ^ 1) for node in range(NODES)])]
    ppermute x5 -> x6, waiting for transfers between devices: 3.96 us -> 3.02 us  [spread(): return lax.ppermute(array, ('space', 'node', 'tm'), pairs)]
    ppermute x3, starting transfers between devices: 4.91 us -> 5.82 us  [across(): lax.ppermute(array, 'node', [(node, node ^ 2) for node in range(NODES)])]
  transfers between devices with their start and end apart: 12 -> 13, of which waited for: 5 -> 7; matrix products, arithmetic and copies ran while one was open for 2% -> 3% of each run, Pallas kernels for 33% -> 30%
where the time goes in v4:
time: 78.7 us; the launch traced here: 78.1 us
  Pallas kernels  29.2 us (37%)
  starting transfers between devices  22.8 us (29%)
  waiting for transfers between devices  20.7 us (26%)
  local copies, waits for them, and re-layouts  4.14 us (5%)
  between operations  1.27 us (2%)
    pallas_call x7, Pallas kernels, call(): pl.pallas_call(kernel, out_shape=[jax.ShapeDtypeStruct(shape, F32) for sh...  29.2 us
    ppermute x6, starting transfers between devices, spread(): return lax.ppermute(array, ('space', 'node', 'tm'), pairs)  15.1 us
    ppermute x3, waiting for transfers between devices, across(): lax.ppermute(array, 'node', [(node, node ^ 2) for node in range(NODES)])  10.9 us
    ppermute x4, waiting for transfers between devices, beside(): lax.ppermute(array, 'node', [(node, node ^ 1) for node in range(NODES)])  6.82 us
    ppermute x3, starting transfers between devices, across(): lax.ppermute(array, 'node', [(node, node ^ 2) for node in range(NODES)])  5.82 us
    ppermute x6, waiting for transfers between devices, spread(): return lax.ppermute(array, ('space', 'node', 'tm'), pairs)  3.02 us
    unnamed x8, local copies, waits for them, and re-layouts  2.03 us
    ppermute x4, starting transfers between devices, beside(): lax.ppermute(array, 'node', [(node, node ^ 1) for node in range(NODES)])  1.92 us
  transfers between devices with their start and end apart: 13, of which 7 were waited for; matrix products, arithmetic and copies ran while one was open for 3% of the time, Pallas kernels for 30%

profile of v4, /device:TPU:0, one launch (start us, length us, event | category | flops | bytes accessed | tf_op | source)
XLA Modules:
  0.0 78.1 jit_solution(12385699676396650863)
XLA Ops:
  1.1 2.6 %collective-permute-start.3 = (f32[8,128,256]{2,1,0:T(8,128)}, f32[8,128,256]{2,1,0:T(8,128)}, u32[]{:S(2)}, u32[]{:S(2)}) collective-permute-start(f32[8,128,256]{2,1,0:T(8,128)} %bitcast.11), channel_id=1, source_target_pairs={{0,4},{2,6},{4,0},{6,2},{1,5},{3,7},{5,1},{7,3},{8,12},{10,14},{12... | collective-permute-start | bytes 3145736 | tf_op jit(solution)/shard_map/ppermute | solution.py:326
  4.4 1.2 %copy-done = f32[1,1,8,128,256]{4,3,2,1,0:T(8,128)S(1)} copy-done((f32[1,1,8,128,256]{4,3,2,1,0:T(8,128)S(1)}, f32[1,1,8,128,256]{4,3,2,1,0:T(8,128)}, u32[]{:S(2)}) %copy-start) | copy-done | bytes 1048600
  5.7 1.5 %shard_map.50 = (f32[6,128,256]{2,1,0:T(8,128)}, f32[4,128,256]{2,1,0:T(8,128)S(1)}) custom-call(f32[46]{0:T(128)S(1)} %constant_dynamic-update-slice_fusion.scalars, f32[8,128,256]{2,1,0:T(8,128)S(1)} %bitcast.12, f32[8,128,256]{2,1,0:T(8,128)S(1)} %collective-permute-done.4.beside), custom_call_target="tpu_custom_call" | custom-call | flops 1000 | bytes 1000 | tf_op jit(solution)/shard_map/pallas_call | solution.py:299
  8.0 2.2 %collective-permute-start.6 = (f32[6,128,256]{2,1,0:T(8,128)}, f32[6,128,256]{2,1,0:T(8,128)}, u32[]{:S(2)}, u32[]{:S(2)}) collective-permute-start(f32[6,128,256]{2,1,0:T(8,128)} %get-tuple-element.31), channel_id=1, source_target_pairs={{0,8},{1,9},{2,26},{3,27},{4,12},{5,13},{6,30},{7,31},{8,16},{9,17... | collective-permute-start | bytes 2359304 | tf_op jit(solution)/shard_map/ppermute | solution.py:344
  11.0 4.3 %collective-permute-start.1 = (f32[4,128,256]{2,1,0:T(8,128)}, f32[4,128,256]{2,1,0:T(8,128)}, u32[]{:S(2)}, u32[]{:S(2)}) collective-permute-start(f32[4,128,256]{2,1,0:T(8,128)} %dynamic-slice_bitcast_fusion), channel_id=1, source_target_pairs={{0,1},{2,3},{4,5},{6,7},{8,9},{10,11},{12,13},{14,15},{16,17},{18,... | collective-permute-start | bytes 1572872 | tf_op jit(solution)/shard_map/ppermute | solution.py:344
  15.3 1.6 %collective-permute-start.8 = (f32[4,128,256]{2,1,0:T(8,128)}, f32[4,128,256]{2,1,0:T(8,128)}, u32[]{:S(2)}, u32[]{:S(2)}) collective-permute-start(f32[4,128,256]{2,1,0:T(8,128)} %copy-done.3), channel_id=1, source_target_pairs={{0,8},{1,9},{2,26},{3,27},{4,12},{5,13},{6,30},{7,31},{8,16},{9,17... | collective-permute-start | bytes 1572872 | tf_op jit(solution)/shard_map/ppermute | solution.py:344
  18.0 9.8 %collective-permute-done.3.across = f32[8,128,256]{2,1,0:T(8,128)} collective-permute-done((f32[8,128,256]{2,1,0:T(8,128)}, f32[8,128,256]{2,1,0:T(8,128)}, u32[]{:S(2)}, u32[]{:S(2)}) %collective-permute-start.3) | collective-permute-done | bytes 1048608 | tf_op jit(solution)/shard_map/ppermute | solution.py:326
  27.8 3.0 %conditional.1 = (f32[8,128,256]{2,1,0:T(8,128)}) conditional(s32[]{:T(128)} %bitcast.5, f32[8,128,256]{2,1,0:T(8,128)} %collective-permute-done.3.across, f32[8,128,256]{2,1,0:T(8,128)} %collective-permute-done.3.across), branch_computations={%region_0.0_spmd, %region_1.0_spmd} | conditional | bytes 4194352 | solution.py:334
  27.8 3.0 %collective-permute-done = f32[8,128,256]{2,1,0:T(8,128)} collective-permute-done((f32[8,128,256]{2,1,0:T(8,128)}, f32[8,128,256]{2,1,0:T(8,128)}, u32[]{:S(2)}, u32[]{:S(2)}) %collective-permute-start) | collective-permute-done | bytes 1048608 | tf_op jit(solution)/shard_map/cond/branch_1_fun/ppermute | solution.py:329
  30.8 1.8 %collective-permute-start.7 = (f32[6,128,256]{2,1,0:T(8,128)}, f32[6,128,256]{2,1,0:T(8,128)S(1)}, u32[]{:S(2)}, u32[]{:S(2)}) collective-permute-start(f32[6,128,256]{2,1,0:T(8,128)} %collective-permute-done.6.halo_a), channel_id=1, source_target_pairs={{0,4},{2,6},{4,0},{6,2},{1,5},{3,7},{5,1},{7,3},{8,12},{10,14},{12... | collective-permute-start | bytes 2359304 | tf_op jit(solution)/shard_map/ppermute | solution.py:326
  32.6 3.1 %shard_map.51 = (f32[5,128,256]{2,1,0:T(8,128)S(1)}, f32[5,128,256]{2,1,0:T(8,128)S(1)}) custom-call(f32[46]{0:T(128)S(1)} %constant_dynamic-update-slice_fusion.scalars, f32[8,128,256]{2,1,0:T(8,128)S(1)} %bitcast.13, f32[8,128,256]{2,1,0:T(8,128)} %collective-permute-done.3.across, f32[8,128,256]{2,1,0:T(8,128)S(1)} %collective-permute-done.4.beside, ...), custom_call_target="tpu_custom_call" | custom-call | flops 1000 | bytes 1000 | tf_op jit(solution)/shard_map/pallas_call | solution.py:299
  35.7 3.5 %collective-permute-start.5 = (f32[5,128,256]{2,1,0:T(8,128)S(1)}, f32[5,128,256]{2,1,0:T(8,128)S(1)}, u32[]{:S(2)}, u32[]{:S(2)}) collective-permute-start(f32[5,128,256]{2,1,0:T(8,128)S(1)} %get-tuple-element.34), channel_id=1, source_target_pairs={{0,1},{2,3},{4,5},{6,7},{8,9},{10,11},{12,13},{14,15},{16,17},{18,... | collective-permute-start | bytes 1966088 | tf_op jit(solution)/shard_map/ppermute | solution.py:344
  39.2 2.6 %collective-permute-done.8.halo_b = f32[4,128,256]{2,1,0:T(8,128)} collective-permute-done((f32[4,128,256]{2,1,0:T(8,128)}, f32[4,128,256]{2,1,0:T(8,128)}, u32[]{:S(2)}, u32[]{:S(2)}) %collective-permute-start.8) | collective-permute-done | bytes 524320 | tf_op jit(solution)/shard_map/ppermute | solution.py:344
  41.7 1.5 %collective-permute-start.9 = (f32[4,128,256]{2,1,0:T(8,128)}, f32[4,128,256]{2,1,0:T(8,128)S(1)}, u32[]{:S(2)}, u32[]{:S(2)}) collective-permute-start(f32[4,128,256]{2,1,0:T(8,128)} %collective-permute-done.8.halo_b), channel_id=1, source_target_pairs={{0,4},{2,6},{4,0},{6,2},{1,5},{3,7},{5,1},{7,3},{8,12},{10,14},{12... | collective-permute-start | bytes 1572872 | tf_op jit(solution)/shard_map/ppermute | solution.py:326
  43.2 2.1 %collective-permute-start.11 = (f32[5,128,256]{2,1,0:T(8,128)S(1)}, f32[5,128,256]{2,1,0:T(8,128)S(1)}, u32[]{:S(2)}, u32[]{:S(2)}) collective-permute-start(f32[5,128,256]{2,1,0:T(8,128)S(1)} %get-tuple-element.38), channel_id=1, source_target_pairs={{0,9},{2,27},{4,13},{6,31},{8,17},{10,3},{12,21},{14,7},{16,25},{1... | collective-permute-start | bytes 1966088 | tf_op jit(solution)/shard_map/ppermute | solution.py:344
  45.3 1.5 %collective-permute-start.2 = (f32[4,128,256]{2,1,0:T(8,128)}, f32[4,128,256]{2,1,0:T(8,128)S(1)}, u32[]{:S(2)}, u32[]{:S(2)}) collective-permute-start(f32[4,128,256]{2,1,0:T(8,128)} %collective-permute-done.1), channel_id=1, source_target_pairs={{1,8},{3,26},{5,12},{7,30},{9,16},{11,2},{13,20},{15,6},{17,24},{1... | collective-permute-start | bytes 1572872 | tf_op jit(solution)/shard_map/ppermute | solution.py:344
  46.8 7.3 %shard_map.52.kept = f32[4,9,128,256]{3,2,1,0:T(8,128)S(1)} custom-call(f32[46]{0:T(128)S(1)} %constant_dynamic-update-slice_fusion.scalars, f32[8,128,256]{2,1,0:T(8,128)S(1)} %bitcast.14, f32[8,128,256]{2,1,0:T(8,128)} %collective-permute-done.3.across, f32[8,128,256]{2,1,0:T(8,128)S(1)} %collective-permute-done.4.beside, ...), custom_call_target="tpu_custom_call" | custom-call | flops 1000 | bytes 1000 | tf_op jit(solution)/shard_map/pallas_call | solution.py:299
  54.1 6.6 %shard_map.53.kept = f32[4,12,128,256]{3,2,1,0:T(8,128)S(1)} custom-call(f32[46]{0:T(128)S(1)} %constant_dynamic-update-slice_fusion.scalars, f32[8,128,256]{2,1,0:T(8,128)S(1)} %bitcast.15, f32[8,128,256]{2,1,0:T(8,128)} %collective-permute-done.3.across, f32[8,128,256]{2,1,0:T(8,128)S(1)} %collective-permute-done.4.beside, ...), custom_call_target="tpu_custom_call" | custom-call | flops 1000 | bytes 1000 | tf_op jit(solution)/shard_map/pallas_call | solution.py:299
  60.7 1.1 %collective-permute-done.9.across_b = f32[4,128,256]{2,1,0:T(8,128)S(1)} collective-permute-done((f32[4,128,256]{2,1,0:T(8,128)}, f32[4,128,256]{2,1,0:T(8,128)S(1)}, u32[]{:S(2)}, u32[]{:S(2)}) %collective-permute-start.9) | collective-permute-done | bytes 524320 | tf_op jit(solution)/shard_map/ppermute | solution.py:326
  61.8 4.9 %shard_map.54.part = f32[4,2,128,256]{3,2,1,0:T(8,128)S(1)} custom-call(f32[46]{0:T(128)S(1)} %constant_dynamic-update-slice_fusion.scalars, f32[6,128,256]{2,1,0:T(8,128)} %collective-permute-done.6.halo_a, f32[6,128,256]{2,1,0:T(8,128)S(1)} %collective-permute-done.7.across_a, f32[4,128,256]{2,1,0:T(8,128)} %collective-permute-done.8.halo_b, ...), custom_call_target="tpu_custom_call" | custom-call | flops 1000 | bytes 1000 | tf_op jit(solution)/shard_map/pallas_call | solution.py:299
  68.2 1.3 %collective-permute-done.10.far = f32[3,128,256]{2,1,0:T(8,128)S(1)} collective-permute-done((f32[3,128,256]{2,1,0:T(8,128)S(1)}, f32[3,128,256]{2,1,0:T(8,128)S(1)}, u32[]{:S(2)}, u32[]{:S(2)}) %collective-permute-start.10) | collective-permute-done | bytes 393248 | tf_op jit(solution)/shard_map/ppermute | solution.py:329
  69.5 3.7 %shard_map.55 = (f32[9,128,256]{2,1,0:T(8,128)S(1)}, f32[9,128,256]{2,1,0:T(8,128)S(1)}) custom-call(f32[46]{0:T(128)S(1)} %constant_dynamic-update-slice_fusion.scalars, f32[8,128,256]{2,1,0:T(8,128)S(1)} %bitcast.17, f32[4,128,256]{2,1,0:T(8,128)S(1)} %collective-permute-done.2.halo_start, f32[5,128,256]{2,1,0:T(8,128)S(1)} %collective-permute-done.5.near, ...), custom_call_target="tpu_custom_call" | custom-call | flops 1000 | bytes 1000 | tf_op jit(solution)/shard_map/pallas_call | solution.py:299
  73.7 2.5 %collective-permute-done.12.other = f32[9,128,256]{2,1,0:T(8,128)S(1)} collective-permute-done((f32[9,128,256]{2,1,0:T(8,128)S(1)}, f32[9,128,256]{2,1,0:T(8,128)S(1)}, u32[]{:S(2)}, u32[]{:S(2)}) %collective-permute-start.12) | collective-permute-done | bytes 1179680 | tf_op jit(solution)/shard_map/ppermute | solution.py:329
  76.1 2.0 %shard_map.56 = (f32[8,128,256]{2,1,0:T(8,128)}, f32[8,128,256]{2,1,0:T(8,128)}) custom-call(f32[46]{0:T(128)S(1)} %constant_dynamic-update-slice_fusion.scalars, f32[9,128,256]{2,1,0:T(8,128)S(1)} %get-tuple-element.39.mine, f32[9,128,256]{2,1,0:T(8,128)S(1)} %collective-permute-done.12.other), custom_call_target="tpu_custom_call" | custom-call | flops 1000 | bytes 1000 | tf_op jit(solution)/shard_map/pallas_call | solution.py:299
  (23 shorter events, 5.3 us)
Async XLA Ops:
  0.6 3.8 %collective-permute-start.4 = (f32[8,128,256]{2,1,0:T(8,128)}, f32[8,128,256]{2,1,0:T(8,128)S(1)}, u32[]{:S(2)}, u32[]{:S(2)}) collective-permute-start(f32[8,128,256]{2,1,0:T(8,128)} %bitcast.10), channel_id=1, source_target_pairs={{0,2},{2,0},{4,6},{6,4},{1,3},{3,1},{5,7},{7,5},{8,10},{10,8},{12,... | collective-permute-start | bytes 3145736 | tf_op jit(solution)/shard_map/ppermute | solution.py:329
  1.1 26.6 %collective-permute-start.3 = (f32[8,128,256]{2,1,0:T(8,128)}, f32[8,128,256]{2,1,0:T(8,128)}, u32[]{:S(2)}, u32[]{:S(2)}) collective-permute-start(f32[8,128,256]{2,1,0:T(8,128)} %bitcast.11), channel_id=1, source_target_pairs={{0,4},{2,6},{4,0},{6,2},{1,5},{3,7},{5,1},{7,3},{8,12},{10,14},{12... | collective-permute-start | bytes 3145736 | tf_op jit(solution)/shard_map/ppermute | solution.py:326
  4.4 1.2 %copy-start = (f32[1,1,8,128,256]{4,3,2,1,0:T(8,128)S(1)}, f32[1,1,8,128,256]{4,3,2,1,0:T(8,128)}, u32[]{:S(2)}) copy-start(f32[1,1,8,128,256]{4,3,2,1,0:T(8,128)} %param.8) | copy-start | bytes 3145732
  5.6 4.5 %copy-start.2 = (f32[1,8,128,256]{3,2,1,0:T(8,128)S(1)}, f32[1,8,128,256]{3,2,1,0:T(8,128)}, u32[]{:S(2)}) copy-start(f32[1,8,128,256]{3,2,1,0:T(8,128)} %param.7) | copy-start | bytes 3145732
  7.2 0.8 %copy-start.3 = (f32[4,128,256]{2,1,0:T(8,128)}, f32[4,128,256]{2,1,0:T(8,128)S(1)}, u32[]{:S(2)}) copy-start(f32[4,128,256]{2,1,0:T(8,128)S(1)} %get-tuple-element.36) | copy-start | bytes 1572868
  8.0 22.8 %collective-permute-start.6 = (f32[6,128,256]{2,1,0:T(8,128)}, f32[6,128,256]{2,1,0:T(8,128)}, u32[]{:S(2)}, u32[]{:S(2)}) collective-permute-start(f32[6,128,256]{2,1,0:T(8,128)} %get-tuple-element.31), channel_id=1, source_target_pairs={{0,8},{1,9},{2,26},{3,27},{4,12},{5,13},{6,30},{7,31},{8,16},{9,17... | collective-permute-start | bytes 2359304 | tf_op jit(solution)/shard_map/ppermute | solution.py:344
  11.0 21.6 %copy-start.1 = (f32[1,1,8,128,256]{4,3,2,1,0:T(8,128)S(1)}, f32[1,1,8,128,256]{4,3,2,1,0:T(8,128)}, u32[]{:S(2)}) copy-start(f32[1,1,8,128,256]{4,3,2,1,0:T(8,128)} %param.8) | copy-start | bytes 3145732
  11.0 21.6 %collective-permute-start.1 = (f32[4,128,256]{2,1,0:T(8,128)}, f32[4,128,256]{2,1,0:T(8,128)}, u32[]{:S(2)}, u32[]{:S(2)}) collective-permute-start(f32[4,128,256]{2,1,0:T(8,128)} %dynamic-slice_bitcast_fusion), channel_id=1, source_target_pairs={{0,1},{2,3},{4,5},{6,7},{8,9},{10,11},{12,13},{14,15},{16,17},{18,... | collective-permute-start | bytes 1572872 | tf_op jit(solution)/shard_map/ppermute | solution.py:344
  15.3 26.4 %collective-permute-start.8 = (f32[4,128,256]{2,1,0:T(8,128)}, f32[4,128,256]{2,1,0:T(8,128)}, u32[]{:S(2)}, u32[]{:S(2)}) collective-permute-start(f32[4,128,256]{2,1,0:T(8,128)} %copy-done.3), channel_id=1, source_target_pairs={{0,8},{1,9},{2,26},{3,27},{4,12},{5,13},{6,30},{7,31},{8,16},{9,17... | collective-permute-start | bytes 1572872 | tf_op jit(solution)/shard_map/ppermute | solution.py:344
  27.8 3.0 %collective-permute-start = (f32[8,128,256]{2,1,0:T(8,128)}, f32[8,128,256]{2,1,0:T(8,128)}, u32[]{:S(2)}, u32[]{:S(2)}) collective-permute-start(f32[8,128,256]{2,1,0:T(8,128)} %param.3), channel_id=1, source_target_pairs={{0,2},{2,0},{4,6},{6,4},{1,3},{3,1},{5,7},{7,5},{8,10},{10,8},{12,... | collective-permute-start | bytes 3145736 | tf_op jit(solution)/shard_map/cond/branch_1_fun/ppermute | solution.py:329
  30.8 23.3 %collective-permute-start.7 = (f32[6,128,256]{2,1,0:T(8,128)}, f32[6,128,256]{2,1,0:T(8,128)S(1)}, u32[]{:S(2)}, u32[]{:S(2)}) collective-permute-start(f32[6,128,256]{2,1,0:T(8,128)} %collective-permute-done.6.halo_a), channel_id=1, source_target_pairs={{0,4},{2,6},{4,0},{6,2},{1,5},{3,7},{5,1},{7,3},{8,12},{10,14},{12... | collective-permute-start | bytes 2359304 | tf_op jit(solution)/shard_map/ppermute | solution.py:326
  35.7 31.5 %collective-permute-start.5 = (f32[5,128,256]{2,1,0:T(8,128)S(1)}, f32[5,128,256]{2,1,0:T(8,128)S(1)}, u32[]{:S(2)}, u32[]{:S(2)}) collective-permute-start(f32[5,128,256]{2,1,0:T(8,128)S(1)} %get-tuple-element.34), channel_id=1, source_target_pairs={{0,1},{2,3},{4,5},{6,7},{8,9},{10,11},{12,13},{14,15},{16,17},{18,... | collective-permute-start | bytes 1966088 | tf_op jit(solution)/shard_map/ppermute | solution.py:344
  41.7 20.1 %collective-permute-start.9 = (f32[4,128,256]{2,1,0:T(8,128)}, f32[4,128,256]{2,1,0:T(8,128)S(1)}, u32[]{:S(2)}, u32[]{:S(2)}) collective-permute-start(f32[4,128,256]{2,1,0:T(8,128)} %collective-permute-done.8.halo_b), channel_id=1, source_target_pairs={{0,4},{2,6},{4,0},{6,2},{1,5},{3,7},{5,1},{7,3},{8,12},{10,14},{12... | collective-permute-start | bytes 1572872 | tf_op jit(solution)/shard_map/ppermute | solution.py:326
  43.2 24.9 %collective-permute-start.11 = (f32[5,128,256]{2,1,0:T(8,128)S(1)}, f32[5,128,256]{2,1,0:T(8,128)S(1)}, u32[]{:S(2)}, u32[]{:S(2)}) collective-permute-start(f32[5,128,256]{2,1,0:T(8,128)S(1)} %get-tuple-element.38), channel_id=1, source_target_pairs={{0,9},{2,27},{4,13},{6,31},{8,17},{10,3},{12,21},{14,7},{16,25},{1... | collective-permute-start | bytes 1966088 | tf_op jit(solution)/shard_map/ppermute | solution.py:344
  45.3 22.9 %collective-permute-start.2 = (f32[4,128,256]{2,1,0:T(8,128)}, f32[4,128,256]{2,1,0:T(8,128)S(1)}, u32[]{:S(2)}, u32[]{:S(2)}) collective-permute-start(f32[4,128,256]{2,1,0:T(8,128)} %collective-permute-done.1), channel_id=1, source_target_pairs={{1,8},{3,26},{5,12},{7,30},{9,16},{11,2},{13,20},{15,6},{17,24},{1... | collective-permute-start | bytes 1572872 | tf_op jit(solution)/shard_map/ppermute | solution.py:344
  67.2 2.3 %collective-permute-start.10 = (f32[3,128,256]{2,1,0:T(8,128)S(1)}, f32[3,128,256]{2,1,0:T(8,128)S(1)}, u32[]{:S(2)}, u32[]{:S(2)}) collective-permute-start(f32[3,128,256]{2,1,0:T(8,128)S(1)} %slice.16), channel_id=1, source_target_pairs={{0,2},{2,0},{4,6},{6,4},{1,3},{3,1},{5,7},{7,5},{8,10},{10,8},{12,... | collective-permute-start | bytes 1179656 | tf_op jit(solution)/shard_map/ppermute | solution.py:329
  73.2 2.9 %collective-permute-start.12 = (f32[9,128,256]{2,1,0:T(8,128)S(1)}, f32[9,128,256]{2,1,0:T(8,128)S(1)}, u32[]{:S(2)}, u32[]{:S(2)}) collective-permute-start(f32[9,128,256]{2,1,0:T(8,128)S(1)} %get-tuple-element.40), channel_id=1, source_target_pairs={{0,2},{2,0},{4,6},{6,4},{1,3},{3,1},{5,7},{7,5},{8,10},{10,8},{12,... | collective-permute-start | bytes 3538952 | tf_op jit(solution)/shard_map/ppermute | solution.py:329

commit v5 on v4

--- a/solution.py
+++ b/solution.py
@@ -20,6 +20,7 @@
 OUTER = 5
 SLAB = 8
 HALF = 4
+RIGHT_ROWS, PASS_ROWS = 16, 32
 
 
 def collocation(count):
@@ -123,27 +124,28 @@
             halo_b[index + 2 * number] = source[plane(8 + index)]
 
 
-def end_kernel(scalars, own, across, beside, corner, start, near, away, total):
+def end_kernel(scalars, own, across, beside, corner, start, out, total):
     plane = counter(scalars)
     sources = (own, across, beside, corner)
-    weighted = [Plane(total, index) for index in range(SLAB + 2)]
+    weighted = [Plane(total, index) for index in range(HALF + 2)]
+
+    def states(place, first):
+        return [Plane(source, plane(place)).rows(first, 32) for source in sources]
+
     for first in chunks(weighted[0], 32):
-        nothing = jnp.zeros_like(weighted[0].rows(first, 32))
-        weighted[0].put(first, nothing)
-        weighted[SLAB + 1].put(first, nothing)
-        for index in range(SLAB):
-            here = plane(index + OUTER)
-            weighted[index + 1].put(first, mixed(scalars, WEIGHT, [Plane(source, here).rows(first, 32) for source in sources]))
-    for index in range(SLAB):
-        here = plane(index + OUTER)
-        out = Plane(near, index + 1) if index < HALF else Plane(away, index - HALF)
-        for first in chunks(out, 32):
-            local = mixed(scalars, WEIGHT, [cubed(Plane(source, here).rows(first, 32)) for source in sources])
-            nearby, centre = around(*weighted[index : index + 3], first, 32)
+        weighted[0].put(first, jnp.zeros_like(weighted[0].rows(first, 32)))
+        for index in range(1, HALF + 2):
+            value = mixed(scalars, WEIGHT, states(index + 4, first))
+            weighted[index].put(first, value)
+            if index == 1:
+                Plane(out, 0).put(first, (time_step * diffusion) * value)
+    for index in range(1, HALF + 1):
+        place = index + 4
+        for first in chunks(weighted[0], 32):
+            local = mixed(scalars, WEIGHT, [cubed(state) for state in states(place, first)])
+            nearby, centre = around(*weighted[index - 1 : index + 2], first, 32)
             force = diffusion * (nearby - 6.0 * centre) + reaction * local
-            out.put(first, Plane(start, here).rows(first, 32) + time_step * force)
-    near[0] = (time_step * diffusion) * total[1]
-    away[HALF] = (time_step * diffusion) * total[SLAB]
+            Plane(out, index).put(first, Plane(start, plane(place)).rows(first, 32) + time_step * force)
 
 
 NAMES = ("g", "x1", "x2", "x3", "x4")
@@ -179,8 +181,8 @@
     targets = range(NODES)
     for place in STAGES[stage]["g"]:
         sources = [[state(source, place + by) for by in (-1, 0, 1)] for source in range(NODES)]
-        for first in chunks(sources[0][0], 16):
-            nearby, centre = zip(*(around(*planes, first, 16) for planes in sources))
+        for first in chunks(sources[0][0], RIGHT_ROWS):
+            nearby, centre = zip(*(around(*planes, first, RIGHT_ROWS) for planes in sources))
             spread_ = [value - 6.0 * middle for value, middle in zip(nearby, centre)]
             local = [cubed(middle) for middle in centre]
             for target in targets:
@@ -192,9 +194,9 @@
             for target in targets:
                 planes = [plane(before, target, place + by) for by in (-1, 0, 1)]
                 base, sink = plane("g", target, place), plane(name, target, place)
-                for first in chunks(sink, 32):
-                    nearby, _ = around(*planes, first, 32)
-                    sink.put(first, base.rows(first, 32) + scalars[MIX + target] * nearby)
+                for first in chunks(sink, PASS_ROWS):
+                    nearby, _ = around(*planes, first, PASS_ROWS)
+                    sink.put(first, base.rows(first, PASS_ROWS) + scalars[MIX + target] * nearby)
 
 
 def first_kernel(scalars, own, across, beside, corner, out, spare):
@@ -236,9 +238,9 @@
     begin_first = scalars[FIRST]
     back = (scalars[CORE] > 0.5).astype(jnp.int32)
     for place in range(1, 5):
-        begin[place] = halo_start[place - 1 + back * (5 - 2 * place)] + away[place - 1]
+        begin[place] = halo_start[place - 1 + back * (5 - 2 * place)] + away[5 - place]
     begin[4] = begin[4] + near[0]
-    begin[5] = (begin_first * start[plane(5)] + near[1]) + away[4]
+    begin[5] = (begin_first * start[plane(5)] + near[1]) + away[0]
     for place in range(6, 9):
         begin[place] = begin_first * start[plane(place)] + near[place - 4]
     for place in range(9, 12):
@@ -336,9 +338,9 @@
     def device(slab_, node, slice_):
         return ((slab_ % slabs) * NODES + node) * slices + slice_
 
-    def spread(array, steps, by):
+    def spread(array, steps, by, flip=0):
         pairs = [
-            (device(slab_, node, here), device(slab_ + by[node % 2], node, there))
+            (device(slab_, node, here), device(slab_ + by[node % 2], node ^ flip, there))
             for slab_ in range(slabs) for node in range(NODES) for here, there in steps
         ]
         return lax.ppermute(array, ("space", "node", "tm"), pairs)
@@ -355,11 +357,11 @@
     sources = [state, across_state, beside_state, corner_state]
     first_start = lax.dynamic_slice_in_dim(start, HALF * (1 - lax.rem(node_index, 2)), HALF, axis=0)
     passing_start = spread(first_start, [(0, 1)], (0, 0))
-    send_near, send_away = call(
-        end_kernel, scalars, [*sources, after(start, passing_start)], [planes(5), planes(5)], [planes(slab + 2)], 16
+    (send_end,) = call(
+        end_kernel, scalars, [*sources, after(start, passing_start)], [planes(5)], [planes(HALF + 2)], 16
     )
-    near = spread(send_near, onward, (0, 0))
-    away = spread(send_away, onward, (1, -1))
+    near = spread(send_end, onward, (0, 0))
+    away = spread(send_end, onward, (-1, 1), 1)
     across_a = across(after(halo_a, corner_state))
     halo_start = spread(passing_start, [(1, 0)], (1, -1))
 
@@ -368,7 +370,7 @@
         return call(kernel, scalars, operands, shapes[:1], shapes[1:], limit)[0]
 
     kept = stage(0, first_kernel, sources, 24)
-    across_b = across(halo_b)
+    across_b = across(after(halo_b, kept))
     kept = stage(1, second_kernel, [*sources, halo_a, across_a, kept], 24)
     part = stage(2, third_kernel, [halo_a, across_a, halo_b, across_b, kept], 24)
     far = beside(after(near, part)[2:])

time: 78.7 us -> 77.3 us (0.982)
  Pallas kernels: 29.2 us -> 28.2 us
    ppermute x3, waiting for transfers between devices: 10.9 us -> 13.5 us  [across(): lax.ppermute(array, 'node', [(node, node ^ 2) for node in range(NODES)])]
    ppermute x6, waiting for transfers between devices: 3.02 us -> 1.47 us  [spread(): return lax.ppermute(array, ('space', 'node', 'tm'), pairs)]
    ppermute x6, starting transfers between devices: 15.1 us -> 16.5 us  [spread(): return lax.ppermute(array, ('space', 'node', 'tm'), pairs)]
    ppermute x4, starting transfers between devices: 1.92 us -> 0.79 us  [beside(): lax.ppermute(array, 'node', [(node, node ^ 1) for node in range(NODES)])]
    pallas_call x7, Pallas kernels: 29.2 us -> 28.2 us  [call(): pl.pallas_call(kernel, out_shape=[jax.ShapeDtypeStruct(shape, F32) for sh...]
    ppermute x3, starting transfers between devices: 5.82 us -> 4.92 us  [across(): lax.ppermute(array, 'node', [(node, node ^ 2) for node in range(NODES)])]
    ppermute x4, waiting for transfers between devices: 6.82 us -> 5.97 us  [beside(): lax.ppermute(array, 'node', [(node, node ^ 1) for node in range(NODES)])]
  transfers between devices with their start and end apart: 13 -> 13, of which waited for: 7 -> 7; matrix products, arithmetic and copies ran while one was open for 3% -> 3% of each run, Pallas kernels for 30% -> 29%
where the time goes in v5:
time: 77.3 us; the launch traced here: 77 us
  Pallas kernels  28.2 us (36%)
  starting transfers between devices  22.2 us (29%)
  waiting for transfers between devices  20.9 us (27%)
  local copies, waits for them, and re-layouts  4.25 us (5%)
  between operations  1.38 us (2%)
    pallas_call x7, Pallas kernels, call(): pl.pallas_call(kernel, out_shape=[jax.ShapeDtypeStruct(shape, F32) for sh...  28.2 us
    ppermute x6, starting transfers between devices, spread(): return lax.ppermute(array, ('space', 'node', 'tm'), pairs)  16.5 us
    ppermute x3, waiting for transfers between devices, across(): lax.ppermute(array, 'node', [(node, node ^ 2) for node in range(NODES)])  13.5 us
    ppermute x4, waiting for transfers between devices, beside(): lax.ppermute(array, 'node', [(node, node ^ 1) for node in range(NODES)])  5.97 us
    ppermute x3, starting transfers between devices, across(): lax.ppermute(array, 'node', [(node, node ^ 2) for node in range(NODES)])  4.92 us
    unnamed x8, local copies, waits for them, and re-layouts  2.04 us
  transfers between devices with their start and end apart: 13, of which 7 were waited for; matrix products, arithmetic and copies ran while one was open for 3% of the time, Pallas kernels for 29%

profile of v5, /device:TPU:0, one launch (start us, length us, event | category | flops | bytes accessed | tf_op | source)
XLA Modules:
  0.0 77.0 jit_solution(8163225702001823303)
XLA Ops:
  1.1 2.6 %collective-permute-start.3 = (f32[8,128,256]{2,1,0:T(8,128)}, f32[8,128,256]{2,1,0:T(8,128)}, u32[]{:S(2)}, u32[]{:S(2)}) collective-permute-start(f32[8,128,256]{2,1,0:T(8,128)} %bitcast.11), channel_id=1, source_target_pairs={{0,4},{2,6},{4,0},{6,2},{1,5},{3,7},{5,1},{7,3},{8,12},{10,14},{12... | collective-permute-start | bytes 3145736 | tf_op jit(solution)/shard_map/ppermute | solution.py:328
  4.4 1.2 %copy-done = f32[1,1,8,128,256]{4,3,2,1,0:T(8,128)S(1)} copy-done((f32[1,1,8,128,256]{4,3,2,1,0:T(8,128)S(1)}, f32[1,1,8,128,256]{4,3,2,1,0:T(8,128)}, u32[]{:S(2)}) %copy-start) | copy-done | bytes 1048600
  5.7 1.5 %shard_map.50 = (f32[6,128,256]{2,1,0:T(8,128)}, f32[4,128,256]{2,1,0:T(8,128)S(1)}) custom-call(f32[46]{0:T(128)S(1)} %constant_dynamic-update-slice_fusion.scalars, f32[8,128,256]{2,1,0:T(8,128)S(1)} %bitcast.12, f32[8,128,256]{2,1,0:T(8,128)S(1)} %collective-permute-done.4.beside), custom_call_target="tpu_custom_call" | custom-call | flops 1000 | bytes 1000 | tf_op jit(solution)/shard_map/pallas_call | solution.py:301
  7.2 0.8 %copy-done.3 = f32[4,128,256]{2,1,0:T(8,128)} copy-done((f32[4,128,256]{2,1,0:T(8,128)}, f32[4,128,256]{2,1,0:T(8,128)S(1)}, u32[]{:S(2)}) %copy-start.3) | copy-done | bytes 524312
  8.0 2.2 %collective-permute-start.6 = (f32[6,128,256]{2,1,0:T(8,128)}, f32[6,128,256]{2,1,0:T(8,128)}, u32[]{:S(2)}, u32[]{:S(2)}) collective-permute-start(f32[6,128,256]{2,1,0:T(8,128)} %get-tuple-element.30), channel_id=1, source_target_pairs={{0,8},{1,9},{2,26},{3,27},{4,12},{5,13},{6,30},{7,31},{8,16},{9,17... | collective-permute-start | bytes 2359304 | tf_op jit(solution)/shard_map/ppermute | solution.py:346
  10.2 0.8 %dynamic-slice_bitcast_fusion = f32[4,128,256]{2,1,0:T(8,128)} fusion(f32[1,8,128,256]{3,2,1,0:T(8,128)S(1)} %copy-done.2, s32[]{:T(128)S(6)} %select_n.7), kind=kLoop, calls=%fused_computation | loop fusion | bytes 1048580 | tf_op jit(solution)/shard_map/dynamic_slice | solution.py:358
  11.0 4.3 %collective-permute-start.1 = (f32[4,128,256]{2,1,0:T(8,128)}, f32[4,128,256]{2,1,0:T(8,128)}, u32[]{:S(2)}, u32[]{:S(2)}) collective-permute-start(f32[4,128,256]{2,1,0:T(8,128)} %dynamic-slice_bitcast_fusion), channel_id=1, source_target_pairs={{0,1},{2,3},{4,5},{6,7},{8,9},{10,11},{12,13},{14,15},{16,17},{18,... | collective-permute-start | bytes 1572872 | tf_op jit(solution)/shard_map/ppermute | solution.py:346
  15.3 1.6 %collective-permute-start.8 = (f32[4,128,256]{2,1,0:T(8,128)}, f32[4,128,256]{2,1,0:T(8,128)}, u32[]{:S(2)}, u32[]{:S(2)}) collective-permute-start(f32[4,128,256]{2,1,0:T(8,128)} %copy-done.3), channel_id=1, source_target_pairs={{0,8},{1,9},{2,26},{3,27},{4,12},{5,13},{6,30},{7,31},{8,16},{9,17... | collective-permute-start | bytes 1572872 | tf_op jit(solution)/shard_map/ppermute | solution.py:346
  18.2 9.6 %collective-permute-done.3.across = f32[8,128,256]{2,1,0:T(8,128)} collective-permute-done((f32[8,128,256]{2,1,0:T(8,128)}, f32[8,128,256]{2,1,0:T(8,128)}, u32[]{:S(2)}, u32[]{:S(2)}) %collective-permute-start.3) | collective-permute-done | bytes 1048608 | tf_op jit(solution)/shard_map/ppermute | solution.py:328
  27.8 3.0 %conditional.1 = (f32[8,128,256]{2,1,0:T(8,128)}) conditional(s32[]{:T(128)} %bitcast.5, f32[8,128,256]{2,1,0:T(8,128)} %collective-permute-done.3.across, f32[8,128,256]{2,1,0:T(8,128)} %collective-permute-done.3.across), branch_computations={%region_0.0_spmd, %region_1.0_spmd} | conditional | bytes 4194352 | solution.py:336
  27.8 3.0 %collective-permute-done = f32[8,128,256]{2,1,0:T(8,128)} collective-permute-done((f32[8,128,256]{2,1,0:T(8,128)}, f32[8,128,256]{2,1,0:T(8,128)}, u32[]{:S(2)}, u32[]{:S(2)}) %collective-permute-start) | collective-permute-done | bytes 1048608 | tf_op jit(solution)/shard_map/cond/branch_1_fun/ppermute | solution.py:331
  30.8 1.8 %collective-permute-start.7 = (f32[6,128,256]{2,1,0:T(8,128)}, f32[6,128,256]{2,1,0:T(8,128)S(1)}, u32[]{:S(2)}, u32[]{:S(2)}) collective-permute-start(f32[6,128,256]{2,1,0:T(8,128)} %collective-permute-done.6.halo_a), channel_id=1, source_target_pairs={{0,4},{2,6},{4,0},{6,2},{1,5},{3,7},{5,1},{7,3},{8,12},{10,14},{12... | collective-permute-start | bytes 2359304 | tf_op jit(solution)/shard_map/ppermute | solution.py:328
  32.6 2.4 %shard_map.51 = f32[5,128,256]{2,1,0:T(8,128)S(1)} custom-call(f32[46]{0:T(128)S(1)} %constant_dynamic-update-slice_fusion.scalars, f32[8,128,256]{2,1,0:T(8,128)S(1)} %bitcast.13, f32[8,128,256]{2,1,0:T(8,128)} %collective-permute-done.3.across, f32[8,128,256]{2,1,0:T(8,128)S(1)} %collective-permute-done.4.beside, f32[8,128,256]{2,1,0:T(8,128)} %get-tuple-element.41.corner, ...), custom_call_target="tpu_custom_call" | custom-call | flops 1000 | bytes 1000 | tf_op jit(solution)/shard_map/pallas_call | solution.py:301
  34.9 3.5 %collective-permute-start.5 = (f32[5,128,256]{2,1,0:T(8,128)S(1)}, f32[5,128,256]{2,1,0:T(8,128)S(1)}, u32[]{:S(2)}, u32[]{:S(2)}) collective-permute-start(f32[5,128,256]{2,1,0:T(8,128)S(1)} %shard_map.51), channel_id=1, source_target_pairs={{0,1},{2,3},{4,5},{6,7},{8,9},{10,11},{12,13},{14,15},{16,17},{18,... | collective-permute-start | bytes 1966088 | tf_op jit(solution)/shard_map/ppermute | solution.py:346
  38.4 7.3 %shard_map.52.kept = f32[4,9,128,256]{3,2,1,0:T(8,128)S(1)} custom-call(f32[46]{0:T(128)S(1)} %constant_dynamic-update-slice_fusion.scalars, f32[8,128,256]{2,1,0:T(8,128)S(1)} %bitcast.14, f32[8,128,256]{2,1,0:T(8,128)} %collective-permute-done.3.across, f32[8,128,256]{2,1,0:T(8,128)S(1)} %collective-permute-done.4.beside, ...), custom_call_target="tpu_custom_call" | custom-call | flops 1000 | bytes 1000 | tf_op jit(solution)/shard_map/pallas_call | solution.py:301
  46.3 3.5 %collective-permute-start.11 = (f32[5,128,256]{2,1,0:T(8,128)S(1)}, f32[5,128,256]{2,1,0:T(8,128)S(1)}, u32[]{:S(2)}, u32[]{:S(2)}) collective-permute-start(f32[5,128,256]{2,1,0:T(8,128)S(1)} %shard_map.51), channel_id=1, source_target_pairs={{0,27},{2,9},{4,31},{6,13},{8,3},{10,17},{12,7},{14,21},{16,11},{1... | collective-permute-start | bytes 1966088 | tf_op jit(solution)/shard_map/ppermute | solution.py:346
  49.8 1.5 %collective-permute-start.2 = (f32[4,128,256]{2,1,0:T(8,128)}, f32[4,128,256]{2,1,0:T(8,128)S(1)}, u32[]{:S(2)}, u32[]{:S(2)}) collective-permute-start(f32[4,128,256]{2,1,0:T(8,128)} %collective-permute-done.1), channel_id=1, source_target_pairs={{1,8},{3,26},{5,12},{7,30},{9,16},{11,2},{13,20},{15,6},{17,24},{1... | collective-permute-start | bytes 1572872 | tf_op jit(solution)/shard_map/ppermute | solution.py:346
  51.4 6.6 %shard_map.53.kept = f32[4,12,128,256]{3,2,1,0:T(8,128)S(1)} custom-call(f32[46]{0:T(128)S(1)} %constant_dynamic-update-slice_fusion.scalars, f32[8,128,256]{2,1,0:T(8,128)S(1)} %bitcast.15, f32[8,128,256]{2,1,0:T(8,128)} %collective-permute-done.3.across, f32[8,128,256]{2,1,0:T(8,128)S(1)} %collective-permute-done.4.beside, ...), custom_call_target="tpu_custom_call" | custom-call | flops 1000 | bytes 1000 | tf_op jit(solution)/shard_map/pallas_call | solution.py:301
  58.0 3.8 %collective-permute-done.9.across_b = f32[4,128,256]{2,1,0:T(8,128)S(1)} collective-permute-done((f32[4,128,256]{2,1,0:T(8,128)}, f32[4,128,256]{2,1,0:T(8,128)S(1)}, u32[]{:S(2)}, u32[]{:S(2)}) %collective-permute-start.9) | collective-permute-done | bytes 524320 | tf_op jit(solution)/shard_map/ppermute | solution.py:328
  61.8 4.7 %shard_map.54.part = f32[4,2,128,256]{3,2,1,0:T(8,128)S(1)} custom-call(f32[46]{0:T(128)S(1)} %constant_dynamic-update-slice_fusion.scalars, f32[6,128,256]{2,1,0:T(8,128)} %collective-permute-done.6.halo_a, f32[6,128,256]{2,1,0:T(8,128)S(1)} %collective-permute-done.7.across_a, f32[4,128,256]{2,1,0:T(8,128)} %collective-permute-done.8.halo_b, ...), custom_call_target="tpu_custom_call" | custom-call | flops 1000 | bytes 1000 | tf_op jit(solution)/shard_map/pallas_call | solution.py:301
  66.6 1.4 %collective-permute-done.2.halo_start = f32[4,128,256]{2,1,0:T(8,128)S(1)} collective-permute-done((f32[4,128,256]{2,1,0:T(8,128)}, f32[4,128,256]{2,1,0:T(8,128)S(1)}, u32[]{:S(2)}, u32[]{:S(2)}) %collective-permute-start.2) | collective-permute-done | bytes 524320 | tf_op jit(solution)/shard_map/ppermute | solution.py:346
  68.3 3.7 %shard_map.55 = (f32[9,128,256]{2,1,0:T(8,128)S(1)}, f32[9,128,256]{2,1,0:T(8,128)S(1)}) custom-call(f32[46]{0:T(128)S(1)} %constant_dynamic-update-slice_fusion.scalars, f32[8,128,256]{2,1,0:T(8,128)S(1)} %bitcast.17, f32[4,128,256]{2,1,0:T(8,128)S(1)} %collective-permute-done.2.halo_start, f32[5,128,256]{2,1,0:T(8,128)S(1)} %collective-permute-done.5.near, ...), custom_call_target="tpu_custom_call" | custom-call | flops 1000 | bytes 1000 | tf_op jit(solution)/shard_map/pallas_call | solution.py:301
  72.2 2.7 %collective-permute-done.12.other = f32[9,128,256]{2,1,0:T(8,128)S(1)} collective-permute-done((f32[9,128,256]{2,1,0:T(8,128)S(1)}, f32[9,128,256]{2,1,0:T(8,128)S(1)}, u32[]{:S(2)}, u32[]{:S(2)}) %collective-permute-start.12) | collective-permute-done | bytes 1179680 | tf_op jit(solution)/shard_map/ppermute | solution.py:331
  75.0 2.0 %shard_map.56 = (f32[8,128,256]{2,1,0:T(8,128)}, f32[8,128,256]{2,1,0:T(8,128)}) custom-call(f32[46]{0:T(128)S(1)} %constant_dynamic-update-slice_fusion.scalars, f32[9,128,256]{2,1,0:T(8,128)S(1)} %get-tuple-element.37.mine, f32[9,128,256]{2,1,0:T(8,128)S(1)} %collective-permute-done.12.other), custom_call_target="tpu_custom_call" | custom-call | flops 1000 | bytes 1000 | tf_op jit(solution)/shard_map/pallas_call | solution.py:301
  (23 shorter events, 3.1 us)
Async XLA Ops:
  0.6 3.8 %collective-permute-start.4 = (f32[8,128,256]{2,1,0:T(8,128)}, f32[8,128,256]{2,1,0:T(8,128)S(1)}, u32[]{:S(2)}, u32[]{:S(2)}) collective-permute-start(f32[8,128,256]{2,1,0:T(8,128)} %bitcast.10), channel_id=1, source_target_pairs={{0,2},{2,0},{4,6},{6,4},{1,3},{3,1},{5,7},{7,5},{8,10},{10,8},{12,... | collective-permute-start | bytes 3145736 | tf_op jit(solution)/shard_map/ppermute | solution.py:331
  1.1 26.6 %collective-permute-start.3 = (f32[8,128,256]{2,1,0:T(8,128)}, f32[8,128,256]{2,1,0:T(8,128)}, u32[]{:S(2)}, u32[]{:S(2)}) collective-permute-start(f32[8,128,256]{2,1,0:T(8,128)} %bitcast.11), channel_id=1, source_target_pairs={{0,4},{2,6},{4,0},{6,2},{1,5},{3,7},{5,1},{7,3},{8,12},{10,14},{12... | collective-permute-start | bytes 3145736 | tf_op jit(solution)/shard_map/ppermute | solution.py:328
  4.4 1.2 %copy-start = (f32[1,1,8,128,256]{4,3,2,1,0:T(8,128)S(1)}, f32[1,1,8,128,256]{4,3,2,1,0:T(8,128)}, u32[]{:S(2)}) copy-start(f32[1,1,8,128,256]{4,3,2,1,0:T(8,128)} %param.8) | copy-start | bytes 3145732
  5.6 4.5 %copy-start.2 = (f32[1,8,128,256]{3,2,1,0:T(8,128)S(1)}, f32[1,8,128,256]{3,2,1,0:T(8,128)}, u32[]{:S(2)}) copy-start(f32[1,8,128,256]{3,2,1,0:T(8,128)} %param.7) | copy-start | bytes 3145732
  7.2 0.8 %copy-start.3 = (f32[4,128,256]{2,1,0:T(8,128)}, f32[4,128,256]{2,1,0:T(8,128)S(1)}, u32[]{:S(2)}) copy-start(f32[4,128,256]{2,1,0:T(8,128)S(1)} %get-tuple-element.34) | copy-start | bytes 1572868
  8.0 22.8 %collective-permute-start.6 = (f32[6,128,256]{2,1,0:T(8,128)}, f32[6,128,256]{2,1,0:T(8,128)}, u32[]{:S(2)}, u32[]{:S(2)}) collective-permute-start(f32[6,128,256]{2,1,0:T(8,128)} %get-tuple-element.30), channel_id=1, source_target_pairs={{0,8},{1,9},{2,26},{3,27},{4,12},{5,13},{6,30},{7,31},{8,16},{9,17... | collective-permute-start | bytes 2359304 | tf_op jit(solution)/shard_map/ppermute | solution.py:346
  11.0 21.6 %copy-start.1 = (f32[1,1,8,128,256]{4,3,2,1,0:T(8,128)S(1)}, f32[1,1,8,128,256]{4,3,2,1,0:T(8,128)}, u32[]{:S(2)}) copy-start(f32[1,1,8,128,256]{4,3,2,1,0:T(8,128)} %param.8) | copy-start | bytes 3145732
  11.0 21.6 %collective-permute-start.1 = (f32[4,128,256]{2,1,0:T(8,128)}, f32[4,128,256]{2,1,0:T(8,128)}, u32[]{:S(2)}, u32[]{:S(2)}) collective-permute-start(f32[4,128,256]{2,1,0:T(8,128)} %dynamic-slice_bitcast_fusion), channel_id=1, source_target_pairs={{0,1},{2,3},{4,5},{6,7},{8,9},{10,11},{12,13},{14,15},{16,17},{18,... | collective-permute-start | bytes 1572872 | tf_op jit(solution)/shard_map/ppermute | solution.py:346
  15.3 30.4 %collective-permute-start.8 = (f32[4,128,256]{2,1,0:T(8,128)}, f32[4,128,256]{2,1,0:T(8,128)}, u32[]{:S(2)}, u32[]{:S(2)}) collective-permute-start(f32[4,128,256]{2,1,0:T(8,128)} %copy-done.3), channel_id=1, source_target_pairs={{0,8},{1,9},{2,26},{3,27},{4,12},{5,13},{6,30},{7,31},{8,16},{9,17... | collective-permute-start | bytes 1572872 | tf_op jit(solution)/shard_map/ppermute | solution.py:346
  27.8 3.0 %collective-permute-start = (f32[8,128,256]{2,1,0:T(8,128)}, f32[8,128,256]{2,1,0:T(8,128)}, u32[]{:S(2)}, u32[]{:S(2)}) collective-permute-start(f32[8,128,256]{2,1,0:T(8,128)} %param.3), channel_id=1, source_target_pairs={{0,2},{2,0},{4,6},{6,4},{1,3},{3,1},{5,7},{7,5},{8,10},{10,8},{12,... | collective-permute-start | bytes 3145736 | tf_op jit(solution)/shard_map/cond/branch_1_fun/ppermute | solution.py:331
  30.8 20.6 %collective-permute-start.7 = (f32[6,128,256]{2,1,0:T(8,128)}, f32[6,128,256]{2,1,0:T(8,128)S(1)}, u32[]{:S(2)}, u32[]{:S(2)}) collective-permute-start(f32[6,128,256]{2,1,0:T(8,128)} %collective-permute-done.6.halo_a), channel_id=1, source_target_pairs={{0,4},{2,6},{4,0},{6,2},{1,5},{3,7},{5,1},{7,3},{8,12},{10,14},{12... | collective-permute-start | bytes 2359304 | tf_op jit(solution)/shard_map/ppermute | solution.py:328
  34.9 31.6 %collective-permute-start.5 = (f32[5,128,256]{2,1,0:T(8,128)S(1)}, f32[5,128,256]{2,1,0:T(8,128)S(1)}, u32[]{:S(2)}, u32[]{:S(2)}) collective-permute-start(f32[5,128,256]{2,1,0:T(8,128)S(1)} %shard_map.51), channel_id=1, source_target_pairs={{0,1},{2,3},{4,5},{6,7},{8,9},{10,11},{12,13},{14,15},{16,17},{18,... | collective-permute-start | bytes 1966088 | tf_op jit(solution)/shard_map/ppermute | solution.py:346
  45.7 16.1 %collective-permute-start.9 = (f32[4,128,256]{2,1,0:T(8,128)}, f32[4,128,256]{2,1,0:T(8,128)S(1)}, u32[]{:S(2)}, u32[]{:S(2)}) collective-permute-start(f32[4,128,256]{2,1,0:T(8,128)} %collective-permute-done.8.halo_b), channel_id=1, source_target_pairs={{0,4},{2,6},{4,0},{6,2},{1,5},{3,7},{5,1},{7,3},{8,12},{10,14},{12... | collective-permute-start | bytes 1572872 | tf_op jit(solution)/shard_map/ppermute | solution.py:328
  46.3 21.7 %collective-permute-start.11 = (f32[5,128,256]{2,1,0:T(8,128)S(1)}, f32[5,128,256]{2,1,0:T(8,128)S(1)}, u32[]{:S(2)}, u32[]{:S(2)}) collective-permute-start(f32[5,128,256]{2,1,0:T(8,128)S(1)} %shard_map.51), channel_id=1, source_target_pairs={{0,27},{2,9},{4,31},{6,13},{8,3},{10,17},{12,7},{14,21},{16,11},{1... | collective-permute-start | bytes 1966088 | tf_op jit(solution)/shard_map/ppermute | solution.py:346
  49.8 18.2 %collective-permute-start.2 = (f32[4,128,256]{2,1,0:T(8,128)}, f32[4,128,256]{2,1,0:T(8,128)S(1)}, u32[]{:S(2)}, u32[]{:S(2)}) collective-permute-start(f32[4,128,256]{2,1,0:T(8,128)} %collective-permute-done.1), channel_id=1, source_target_pairs={{1,8},{3,26},{5,12},{7,30},{9,16},{11,2},{13,20},{15,6},{17,24},{1... | collective-permute-start | bytes 1572872 | tf_op jit(solution)/shard_map/ppermute | solution.py:346
  66.5 1.8 %collective-permute-start.10 = (f32[3,128,256]{2,1,0:T(8,128)S(1)}, f32[3,128,256]{2,1,0:T(8,128)S(1)}, u32[]{:S(2)}, u32[]{:S(2)}) collective-permute-start(f32[3,128,256]{2,1,0:T(8,128)S(1)} %slice.16), channel_id=1, source_target_pairs={{0,2},{2,0},{4,6},{6,4},{1,3},{3,1},{5,7},{7,5},{8,10},{10,8},{12,... | collective-permute-start | bytes 1179656 | tf_op jit(solution)/shard_map/ppermute | solution.py:331
  72.0 2.9 %collective-permute-start.12 = (f32[9,128,256]{2,1,0:T(8,128)S(1)}, f32[9,128,256]{2,1,0:T(8,128)S(1)}, u32[]{:S(2)}, u32[]{:S(2)}) collective-permute-start(f32[9,128,256]{2,1,0:T(8,128)S(1)} %get-tuple-element.38), channel_id=1, source_target_pairs={{0,2},{2,0},{4,6},{6,4},{1,3},{3,1},{5,7},{7,5},{8,10},{10,8},{12,... | collective-permute-start | bytes 3538952 | tf_op jit(solution)/shard_map/ppermute | solution.py:331

commit v6 on v5

--- a/solution.py
+++ b/solution.py
@@ -233,7 +233,18 @@
     run_stage(2, scalars, state, kept, out, spare)
 
 
-def last_kernel(scalars, start, halo_start, near, far, away, kept, part, mine, swap, begin, once, twice, last, total):
+def around_place(ref, place, first, count):
+    return around(*(Plane(ref, place + by) for by in (-1, 0, 1)), first, count)
+
+
+def raise_power(source, sink, places):
+    for place in places:
+        out = Plane(sink, place)
+        for first in chunks(out, 32):
+            out.put(first, around_place(source, place, first, 32)[0])
+
+
+def begin_kernel(scalars, start, halo_start, near, away, begin, once, twice):
     plane = counter(scalars)
     begin_first = scalars[FIRST]
     back = (scalars[CORE] > 0.5).astype(jnp.int32)
@@ -243,22 +254,36 @@
     begin[5] = (begin_first * start[plane(5)] + near[1]) + away[0]
     for place in range(6, 9):
         begin[place] = begin_first * start[plane(place)] + near[place - 4]
+    raise_power(begin, once, range(2, 8))
+    raise_power(once, twice, range(3, 7))
+
+
+def last_kernel(
+    scalars, start, far, begin_near, once_near, twice_near, kept, part, mine, swap, begin, once, twice, last, total
+):
+    plane = counter(scalars)
+    begin_first = scalars[FIRST]
     for place in range(9, 12):
         begin[place] = begin_first * start[plane(place)] + far[11 - place]
 
-    def around_place(ref, place, first, count):
-        return around(*(Plane(ref, place + by) for by in (-1, 0, 1)), first, count)
-
-    for source, sink, places in ((begin, once, range(2, 11)), (once, twice, range(3, 10))):
+    def at(place, near, own, split):
+        return Plane(near if place < split else own, place)
+
+    def raised(near_source, source, split, sink, places):
         for place in places:
+            planes = [at(place + by, near_source, source, split) for by in (-1, 0, 1)]
             out = Plane(sink, place)
             for first in chunks(out, 32):
-                out.put(first, around_place(source, place, first, 32)[0])
+                out.put(first, around(*planes, first, 32)[0])
+
+    raised(begin_near, begin, 9, once, range(8, 11))
+    raised(once_near, once, 8, twice, range(7, 10))
     kept_x4 = {key: index for index, key in enumerate(kept_keys(1))}
     for place in range(4, 9):
+        planes = [at(place + by, twice_near, twice, 7) for by in (-1, 0, 1)]
         for first in chunks(Plane(total, 0), 16):
-            thrice, two = around_place(twice, place, first, 16)
-            zero, one = Plane(begin, place).rows(first, 16), Plane(once, place).rows(first, 16)
+            thrice, two = around(*planes, first, 16)
+            zero, one = Plane(begin_near, place).rows(first, 16), at(place, once_near, once, 8).rows(first, 16)
             values = []
             for target in range(NODES):
                 mix = scalars[MIX + target]
@@ -275,24 +300,22 @@
             local = mixed(scalars, WEIGHT, [cubed(state) for state in states])
             nearby, centre = around_place(total, index, first, 16)
             force = diffusion * (nearby - 6.0 * centre) + reaction * local
-            value = Plane(begin, place).rows(first, 16) + time_step * force
-            for sink, state in ((mine, states[0]), (swap, states[2])):
-                Plane(sink, index - 1).put(first, state)
-                Plane(sink, index - 1 + HALF).put(first, value)
-    mine[2 * HALF] = total[HALF]
+            Plane(mine, index - 1).put(first, states[0])
+            Plane(swap, index - 1).put(first, states[2])
+            Plane(swap, index - 1 + HALF).put(first, Plane(begin_near, place).rows(first, 16) + time_step * force)
     swap[2 * HALF] = total[HALF]
 
 
-def join_kernel(scalars, mine, other, state, end):
+def join_kernel(scalars, mine, swap, other, state, end):
     plane = counter(scalars)
     for index in range(HALF):
         near, far = plane(OUTER + index), plane(OUTER + SLAB - 1 - index)
         state[near] = mine[index]
         state[far] = other[index]
-        own, others = mine[HALF + index], other[HALF + index]
+        own, others = swap[HALF + index], other[HALF + index]
         if index == HALF - 1:
             own = own + (time_step * diffusion) * other[2 * HALF]
-            others = others + (time_step * diffusion) * mine[2 * HALF]
+            others = others + (time_step * diffusion) * swap[2 * HALF]
         end[near] = own
         end[far] = others
 
@@ -374,11 +397,12 @@
     kept = stage(1, second_kernel, [*sources, halo_a, across_a, kept], 24)
     part = stage(2, third_kernel, [halo_a, across_a, halo_b, across_b, kept], 24)
     far = beside(after(near, part)[2:])
+    begun = call(begin_kernel, scalars, [start, halo_start, near, away], [planes(9), planes(8), planes(7)], [], 16)
     mine, swap = call(
-        last_kernel, scalars, [start, halo_start, near, far, away, kept, part], [planes(2 * HALF + 1)] * 2,
+        last_kernel, scalars, [start, far, *begun, kept, part], [planes(HALF), planes(2 * HALF + 1)],
         [planes(12), planes(11), planes(10), planes(NODES, 5), planes(6)], 24,
     )
-    state_new, end_new = call(join_kernel, scalars, [mine, beside(swap)], [planes(slab)] * 2, [], 16)
+    state_new, end_new = call(join_kernel, scalars, [mine, swap, beside(swap)], [planes(slab)] * 2, [], 16)
     return (state_new[None, None], end_new[None])
 
 

time: 77.3 us -> 77.7 us (level)
    pallas_call x7 -> x8, Pallas kernels: 28.2 us -> 28.7 us  [call(): pl.pallas_call(kernel, out_shape=[jax.ShapeDtypeStruct(shape, F32) for sh...]
  transfers between devices with their start and end apart: 13 -> 13, of which waited for: 7 -> 6; matrix products, arithmetic and copies ran while one was open for 3% -> 3% of each run, Pallas kernels for 29% -> 31%
where the time goes in v6:
time: 77.7 us; the launch traced here: 77.3 us
  Pallas kernels  28.7 us (37%)
  starting transfers between devices  22.1 us (28%)
  waiting for transfers between devices  21 us (27%)
  local copies, waits for them, and re-layouts  4.14 us (5%)
  between operations  1.32 us (2%)
    pallas_call x8, Pallas kernels, call(): pl.pallas_call(kernel, out_shape=[jax.ShapeDtypeStruct(shape, F32) for sh...  28.7 us
    ppermute x6, starting transfers between devices, spread(): return lax.ppermute(array, ('space', 'node', 'tm'), pairs)  16.5 us
    ppermute x3, waiting for transfers between devices, across(): lax.ppermute(array, 'node', [(node, node ^ 2) for node in range(NODES)])  13.7 us
    ppermute x4, waiting for transfers between devices, beside(): lax.ppermute(array, 'node', [(node, node ^ 1) for node in range(NODES)])  5.84 us
    ppermute x3, starting transfers between devices, across(): lax.ppermute(array, 'node', [(node, node ^ 2) for node in range(NODES)])  4.92 us
    unnamed x8, local copies, waits for them, and re-layouts  2.03 us
  transfers between devices with their start and end apart: 13, of which 6 were waited for; matrix products, arithmetic and copies ran while one was open for 3% of the time, Pallas kernels for 31%

profile of v6, /device:TPU:0, one launch (start us, length us, event | category | flops | bytes accessed | tf_op | source)
XLA Modules:
  0.0 77.3 jit_solution(7268062575684960725)
XLA Ops:
  1.1 2.6 %collective-permute-start.1 = (f32[8,128,256]{2,1,0:T(8,128)}, f32[8,128,256]{2,1,0:T(8,128)}, u32[]{:S(2)}, u32[]{:S(2)}) collective-permute-start(f32[8,128,256]{2,1,0:T(8,128)} %bitcast.11), channel_id=1, source_target_pairs={{0,4},{2,6},{4,0},{6,2},{1,5},{3,7},{5,1},{7,3},{8,12},{10,14},{12... | collective-permute-start | bytes 3145736 | tf_op jit(solution)/shard_map/ppermute | solution.py:351
  4.4 1.2 %copy-done = f32[1,1,8,128,256]{4,3,2,1,0:T(8,128)S(1)} copy-done((f32[1,1,8,128,256]{4,3,2,1,0:T(8,128)S(1)}, f32[1,1,8,128,256]{4,3,2,1,0:T(8,128)}, u32[]{:S(2)}) %copy-start) | copy-done | bytes 1048600
  5.7 1.5 %shard_map.50 = (f32[6,128,256]{2,1,0:T(8,128)}, f32[4,128,256]{2,1,0:T(8,128)S(1)}) custom-call(f32[46]{0:T(128)S(1)} %constant_dynamic-update-slice_fusion.scalars, f32[8,128,256]{2,1,0:T(8,128)S(1)} %bitcast.12, f32[8,128,256]{2,1,0:T(8,128)S(1)} %collective-permute-done.2.beside), custom_call_target="tpu_custom_call" | custom-call | flops 1000 | bytes 1000 | tf_op jit(solution)/shard_map/pallas_call | solution.py:324
  8.0 2.2 %collective-permute-start.5 = (f32[6,128,256]{2,1,0:T(8,128)}, f32[6,128,256]{2,1,0:T(8,128)}, u32[]{:S(2)}, u32[]{:S(2)}) collective-permute-start(f32[6,128,256]{2,1,0:T(8,128)} %get-tuple-element.33), channel_id=1, source_target_pairs={{0,8},{1,9},{2,26},{3,27},{4,12},{5,13},{6,30},{7,31},{8,16},{9,17... | collective-permute-start | bytes 2359304 | tf_op jit(solution)/shard_map/ppermute | solution.py:369
  10.1 0.8 %dynamic-slice_bitcast_fusion = f32[4,128,256]{2,1,0:T(8,128)} fusion(f32[1,8,128,256]{3,2,1,0:T(8,128)S(1)} %copy-done.2, s32[]{:T(128)S(6)} %select_n.7), kind=kLoop, calls=%fused_computation | loop fusion | bytes 1048580 | tf_op jit(solution)/shard_map/dynamic_slice | solution.py:381
  11.0 4.3 %collective-permute-start.3 = (f32[4,128,256]{2,1,0:T(8,128)}, f32[4,128,256]{2,1,0:T(8,128)}, u32[]{:S(2)}, u32[]{:S(2)}) collective-permute-start(f32[4,128,256]{2,1,0:T(8,128)} %dynamic-slice_bitcast_fusion), channel_id=1, source_target_pairs={{0,1},{2,3},{4,5},{6,7},{8,9},{10,11},{12,13},{14,15},{16,17},{18,... | collective-permute-start | bytes 1572872 | tf_op jit(solution)/shard_map/ppermute | solution.py:369
  15.3 1.6 %collective-permute-start.7 = (f32[4,128,256]{2,1,0:T(8,128)}, f32[4,128,256]{2,1,0:T(8,128)}, u32[]{:S(2)}, u32[]{:S(2)}) collective-permute-start(f32[4,128,256]{2,1,0:T(8,128)} %copy-done.3), channel_id=1, source_target_pairs={{0,8},{1,9},{2,26},{3,27},{4,12},{5,13},{6,30},{7,31},{8,16},{9,17... | collective-permute-start | bytes 1572872 | tf_op jit(solution)/shard_map/ppermute | solution.py:369
  18.0 9.8 %collective-permute-done.1.across = f32[8,128,256]{2,1,0:T(8,128)} collective-permute-done((f32[8,128,256]{2,1,0:T(8,128)}, f32[8,128,256]{2,1,0:T(8,128)}, u32[]{:S(2)}, u32[]{:S(2)}) %collective-permute-start.1) | collective-permute-done | bytes 1048608 | tf_op jit(solution)/shard_map/ppermute | solution.py:351
  27.8 3.0 %conditional.1 = (f32[8,128,256]{2,1,0:T(8,128)}) conditional(s32[]{:T(128)} %bitcast.4, f32[8,128,256]{2,1,0:T(8,128)} %collective-permute-done.1.across, f32[8,128,256]{2,1,0:T(8,128)} %collective-permute-done.1.across), branch_computations={%region_0.0_spmd, %region_1.0_spmd} | conditional | bytes 4194352 | solution.py:359
  27.8 3.0 %collective-permute-done = f32[8,128,256]{2,1,0:T(8,128)} collective-permute-done((f32[8,128,256]{2,1,0:T(8,128)}, f32[8,128,256]{2,1,0:T(8,128)}, u32[]{:S(2)}, u32[]{:S(2)}) %collective-permute-start) | collective-permute-done | bytes 1048608 | tf_op jit(solution)/shard_map/cond/branch_1_fun/ppermute | solution.py:354
  30.8 1.8 %collective-permute-start.6 = (f32[6,128,256]{2,1,0:T(8,128)}, f32[6,128,256]{2,1,0:T(8,128)S(1)}, u32[]{:S(2)}, u32[]{:S(2)}) collective-permute-start(f32[6,128,256]{2,1,0:T(8,128)} %collective-permute-done.5.halo_a), channel_id=1, source_target_pairs={{0,4},{2,6},{4,0},{6,2},{1,5},{3,7},{5,1},{7,3},{8,12},{10,14},{12... | collective-permute-start | bytes 2359304 | tf_op jit(solution)/shard_map/ppermute | solution.py:351
  32.6 2.4 %shard_map.51 = f32[5,128,256]{2,1,0:T(8,128)S(1)} custom-call(f32[46]{0:T(128)S(1)} %constant_dynamic-update-slice_fusion.scalars, f32[8,128,256]{2,1,0:T(8,128)S(1)} %bitcast.13, f32[8,128,256]{2,1,0:T(8,128)} %collective-permute-done.1.across, f32[8,128,256]{2,1,0:T(8,128)S(1)} %collective-permute-done.2.beside, f32[8,128,256]{2,1,0:T(8,128)} %get-tuple-element.47.corner, ...), custom_call_target="tpu_custom_call" | custom-call | flops 1000 | bytes 1000 | tf_op jit(solution)/shard_map/pallas_call | solution.py:324
  34.9 3.5 %collective-permute-start.4 = (f32[5,128,256]{2,1,0:T(8,128)S(1)}, f32[5,128,256]{2,1,0:T(8,128)S(1)}, u32[]{:S(2)}, u32[]{:S(2)}) collective-permute-start(f32[5,128,256]{2,1,0:T(8,128)S(1)} %shard_map.51), channel_id=1, source_target_pairs={{0,1},{2,3},{4,5},{6,7},{8,9},{10,11},{12,13},{14,15},{16,17},{18,... | collective-permute-start | bytes 1966088 | tf_op jit(solution)/shard_map/ppermute | solution.py:369
  38.4 7.3 %shard_map.52.kept = f32[4,9,128,256]{3,2,1,0:T(8,128)S(1)} custom-call(f32[46]{0:T(128)S(1)} %constant_dynamic-update-slice_fusion.scalars, f32[8,128,256]{2,1,0:T(8,128)S(1)} %bitcast.14, f32[8,128,256]{2,1,0:T(8,128)} %collective-permute-done.1.across, f32[8,128,256]{2,1,0:T(8,128)S(1)} %collective-permute-done.2.beside, ...), custom_call_target="tpu_custom_call" | custom-call | flops 1000 | bytes 1000 | tf_op jit(solution)/shard_map/pallas_call | solution.py:324
  46.3 3.5 %collective-permute-start.11 = (f32[5,128,256]{2,1,0:T(8,128)S(1)}, f32[5,128,256]{2,1,0:T(8,128)S(1)}, u32[]{:S(2)}, u32[]{:S(2)}) collective-permute-start(f32[5,128,256]{2,1,0:T(8,128)S(1)} %shard_map.51), channel_id=1, source_target_pairs={{0,27},{2,9},{4,31},{6,13},{8,3},{10,17},{12,7},{14,21},{16,11},{1... | collective-permute-start | bytes 1966088 | tf_op jit(solution)/shard_map/ppermute | solution.py:369
  49.8 1.5 %collective-permute-start.10 = (f32[4,128,256]{2,1,0:T(8,128)}, f32[4,128,256]{2,1,0:T(8,128)S(1)}, u32[]{:S(2)}, u32[]{:S(2)}) collective-permute-start(f32[4,128,256]{2,1,0:T(8,128)} %collective-permute-done.3), channel_id=1, source_target_pairs={{1,8},{3,26},{5,12},{7,30},{9,16},{11,2},{13,20},{15,6},{17,24},{1... | collective-permute-start | bytes 1572872 | tf_op jit(solution)/shard_map/ppermute | solution.py:369
  51.4 6.6 %shard_map.53.kept = f32[4,12,128,256]{3,2,1,0:T(8,128)S(1)} custom-call(f32[46]{0:T(128)S(1)} %constant_dynamic-update-slice_fusion.scalars, f32[8,128,256]{2,1,0:T(8,128)S(1)} %bitcast.15, f32[8,128,256]{2,1,0:T(8,128)} %collective-permute-done.1.across, f32[8,128,256]{2,1,0:T(8,128)S(1)} %collective-permute-done.2.beside, ...), custom_call_target="tpu_custom_call" | custom-call | flops 1000 | bytes 1000 | tf_op jit(solution)/shard_map/pallas_call | solution.py:324
  58.0 3.8 %collective-permute-done.8.across_b = f32[4,128,256]{2,1,0:T(8,128)S(1)} collective-permute-done((f32[4,128,256]{2,1,0:T(8,128)}, f32[4,128,256]{2,1,0:T(8,128)S(1)}, u32[]{:S(2)}, u32[]{:S(2)}) %collective-permute-start.8) | collective-permute-done | bytes 524320 | tf_op jit(solution)/shard_map/ppermute | solution.py:351
  61.8 4.7 %shard_map.54.part = f32[4,2,128,256]{3,2,1,0:T(8,128)S(1)} custom-call(f32[46]{0:T(128)S(1)} %constant_dynamic-update-slice_fusion.scalars, f32[6,128,256]{2,1,0:T(8,128)} %collective-permute-done.5.halo_a, f32[6,128,256]{2,1,0:T(8,128)S(1)} %collective-permute-done.6.across_a, f32[4,128,256]{2,1,0:T(8,128)} %collective-permute-done.7.halo_b, ...), custom_call_target="tpu_custom_call" | custom-call | flops 1000 | bytes 1000 | tf_op jit(solution)/shard_map/pallas_call | solution.py:324
  66.6 1.4 %collective-permute-done.10.halo_start = f32[4,128,256]{2,1,0:T(8,128)S(1)} collective-permute-done((f32[4,128,256]{2,1,0:T(8,128)}, f32[4,128,256]{2,1,0:T(8,128)S(1)}, u32[]{:S(2)}, u32[]{:S(2)}) %collective-permute-start.10) | collective-permute-done | bytes 524320 | tf_op jit(solution)/shard_map/ppermute | solution.py:369
  68.1 1.3 %shard_map.55 = (f32[9,128,256]{2,1,0:T(8,128)S(1)}, f32[8,128,256]{2,1,0:T(8,128)S(1)}, f32[7,128,256]{2,1,0:T(8,128)S(1)}) custom-call(f32[46]{0:T(128)S(1)} %constant_dynamic-update-slice_fusion.scalars, f32[8,128,256]{2,1,0:T(8,128)S(1)} %bitcast.17, f32[4,128,256]{2,1,0:T(8,128)S(1)} %collective-permute-done.10.halo_start, ...), custom_call_target="tpu_custom_call" | custom-call | flops 1000 | bytes 1000 | tf_op jit(solution)/shard_map/pallas_call | solution.py:324
  69.4 3.0 %shard_map.56 = (f32[4,128,256]{2,1,0:T(8,128)S(1)}, f32[9,128,256]{2,1,0:T(8,128)S(1)}) custom-call(f32[46]{0:T(128)S(1)} %constant_dynamic-update-slice_fusion.scalars, f32[8,128,256]{2,1,0:T(8,128)S(1)} %bitcast.18, f32[3,128,256]{2,1,0:T(8,128)S(1)} %collective-permute-done.9.far, f32[9,128,256]{2,1,0:T(8,128)S(1)} %get-tuple-element.40.begin_near, ...), custom_call_target="tpu_custom_call" | custom-call | flops 1000 | bytes 1000 | tf_op jit(solution)/shard_map/pallas_call | solution.py:324
  72.5 2.8 %collective-permute-done.12.other = f32[9,128,256]{2,1,0:T(8,128)S(1)} collective-permute-done((f32[9,128,256]{2,1,0:T(8,128)S(1)}, f32[9,128,256]{2,1,0:T(8,128)S(1)}, u32[]{:S(2)}, u32[]{:S(2)}) %collective-permute-start.12) | collective-permute-done | bytes 1179680 | tf_op jit(solution)/shard_map/ppermute | solution.py:354
  75.3 2.0 %shard_map.57 = (f32[8,128,256]{2,1,0:T(8,128)}, f32[8,128,256]{2,1,0:T(8,128)}) custom-call(f32[46]{0:T(128)S(1)} %constant_dynamic-update-slice_fusion.scalars, f32[4,128,256]{2,1,0:T(8,128)S(1)} %get-tuple-element.43.mine, f32[9,128,256]{2,1,0:T(8,128)S(1)} %get-tuple-element.44.swap, f32[9,128,256]{2,1,0:T(8,128)S(1)} %collective-permute-done.12.other), custom_call_target="tpu_custom_call" | custom-call | flops 1000 | bytes 1000 | tf_op jit(solution)/shard_map/pallas_call | solution.py:324
  (24 shorter events, 3.5 us)
Async XLA Ops:
  0.6 3.8 %collective-permute-start.2 = (f32[8,128,256]{2,1,0:T(8,128)}, f32[8,128,256]{2,1,0:T(8,128)S(1)}, u32[]{:S(2)}, u32[]{:S(2)}) collective-permute-start(f32[8,128,256]{2,1,0:T(8,128)} %bitcast.10), channel_id=1, source_target_pairs={{0,2},{2,0},{4,6},{6,4},{1,3},{3,1},{5,7},{7,5},{8,10},{10,8},{12,... | collective-permute-start | bytes 3145736 | tf_op jit(solution)/shard_map/ppermute | solution.py:354
  1.1 26.6 %collective-permute-start.1 = (f32[8,128,256]{2,1,0:T(8,128)}, f32[8,128,256]{2,1,0:T(8,128)}, u32[]{:S(2)}, u32[]{:S(2)}) collective-permute-start(f32[8,128,256]{2,1,0:T(8,128)} %bitcast.11), channel_id=1, source_target_pairs={{0,4},{2,6},{4,0},{6,2},{1,5},{3,7},{5,1},{7,3},{8,12},{10,14},{12... | collective-permute-start | bytes 3145736 | tf_op jit(solution)/shard_map/ppermute | solution.py:351
  4.4 1.2 %copy-start = (f32[1,1,8,128,256]{4,3,2,1,0:T(8,128)S(1)}, f32[1,1,8,128,256]{4,3,2,1,0:T(8,128)}, u32[]{:S(2)}) copy-start(f32[1,1,8,128,256]{4,3,2,1,0:T(8,128)} %param.8) | copy-start | bytes 3145732
  5.6 4.5 %copy-start.2 = (f32[1,8,128,256]{3,2,1,0:T(8,128)S(1)}, f32[1,8,128,256]{3,2,1,0:T(8,128)}, u32[]{:S(2)}) copy-start(f32[1,8,128,256]{3,2,1,0:T(8,128)} %param.7) | copy-start | bytes 3145732
  7.2 0.8 %copy-start.3 = (f32[4,128,256]{2,1,0:T(8,128)}, f32[4,128,256]{2,1,0:T(8,128)S(1)}, u32[]{:S(2)}) copy-start(f32[4,128,256]{2,1,0:T(8,128)S(1)} %get-tuple-element.37) | copy-start | bytes 1572868
  8.0 22.8 %collective-permute-start.5 = (f32[6,128,256]{2,1,0:T(8,128)}, f32[6,128,256]{2,1,0:T(8,128)}, u32[]{:S(2)}, u32[]{:S(2)}) collective-permute-start(f32[6,128,256]{2,1,0:T(8,128)} %get-tuple-element.33), channel_id=1, source_target_pairs={{0,8},{1,9},{2,26},{3,27},{4,12},{5,13},{6,30},{7,31},{8,16},{9,17... | collective-permute-start | bytes 2359304 | tf_op jit(solution)/shard_map/ppermute | solution.py:369
  11.0 21.6 %copy-start.1 = (f32[1,1,8,128,256]{4,3,2,1,0:T(8,128)S(1)}, f32[1,1,8,128,256]{4,3,2,1,0:T(8,128)}, u32[]{:S(2)}) copy-start(f32[1,1,8,128,256]{4,3,2,1,0:T(8,128)} %param.8) | copy-start | bytes 3145732
  11.0 21.6 %collective-permute-start.3 = (f32[4,128,256]{2,1,0:T(8,128)}, f32[4,128,256]{2,1,0:T(8,128)}, u32[]{:S(2)}, u32[]{:S(2)}) collective-permute-start(f32[4,128,256]{2,1,0:T(8,128)} %dynamic-slice_bitcast_fusion), channel_id=1, source_target_pairs={{0,1},{2,3},{4,5},{6,7},{8,9},{10,11},{12,13},{14,15},{16,17},{18,... | collective-permute-start | bytes 1572872 | tf_op jit(solution)/shard_map/ppermute | solution.py:369
  15.3 30.4 %collective-permute-start.7 = (f32[4,128,256]{2,1,0:T(8,128)}, f32[4,128,256]{2,1,0:T(8,128)}, u32[]{:S(2)}, u32[]{:S(2)}) collective-permute-start(f32[4,128,256]{2,1,0:T(8,128)} %copy-done.3), channel_id=1, source_target_pairs={{0,8},{1,9},{2,26},{3,27},{4,12},{5,13},{6,30},{7,31},{8,16},{9,17... | collective-permute-start | bytes 1572872 | tf_op jit(solution)/shard_map/ppermute | solution.py:369
  27.8 3.0 %collective-permute-start = (f32[8,128,256]{2,1,0:T(8,128)}, f32[8,128,256]{2,1,0:T(8,128)}, u32[]{:S(2)}, u32[]{:S(2)}) collective-permute-start(f32[8,128,256]{2,1,0:T(8,128)} %param.3), channel_id=1, source_target_pairs={{0,2},{2,0},{4,6},{6,4},{1,3},{3,1},{5,7},{7,5},{8,10},{10,8},{12,... | collective-permute-start | bytes 3145736 | tf_op jit(solution)/shard_map/cond/branch_1_fun/ppermute | solution.py:354
  30.8 20.6 %collective-permute-start.6 = (f32[6,128,256]{2,1,0:T(8,128)}, f32[6,128,256]{2,1,0:T(8,128)S(1)}, u32[]{:S(2)}, u32[]{:S(2)}) collective-permute-start(f32[6,128,256]{2,1,0:T(8,128)} %collective-permute-done.5.halo_a), channel_id=1, source_target_pairs={{0,4},{2,6},{4,0},{6,2},{1,5},{3,7},{5,1},{7,3},{8,12},{10,14},{12... | collective-permute-start | bytes 2359304 | tf_op jit(solution)/shard_map/ppermute | solution.py:351
  34.9 31.6 %collective-permute-start.4 = (f32[5,128,256]{2,1,0:T(8,128)S(1)}, f32[5,128,256]{2,1,0:T(8,128)S(1)}, u32[]{:S(2)}, u32[]{:S(2)}) collective-permute-start(f32[5,128,256]{2,1,0:T(8,128)S(1)} %shard_map.51), channel_id=1, source_target_pairs={{0,1},{2,3},{4,5},{6,7},{8,9},{10,11},{12,13},{14,15},{16,17},{18,... | collective-permute-start | bytes 1966088 | tf_op jit(solution)/shard_map/ppermute | solution.py:369
  45.7 16.1 %collective-permute-start.8 = (f32[4,128,256]{2,1,0:T(8,128)}, f32[4,128,256]{2,1,0:T(8,128)S(1)}, u32[]{:S(2)}, u32[]{:S(2)}) collective-permute-start(f32[4,128,256]{2,1,0:T(8,128)} %collective-permute-done.7.halo_b), channel_id=1, source_target_pairs={{0,4},{2,6},{4,0},{6,2},{1,5},{3,7},{5,1},{7,3},{8,12},{10,14},{12... | collective-permute-start | bytes 1572872 | tf_op jit(solution)/shard_map/ppermute | solution.py:351
  46.3 21.7 %collective-permute-start.11 = (f32[5,128,256]{2,1,0:T(8,128)S(1)}, f32[5,128,256]{2,1,0:T(8,128)S(1)}, u32[]{:S(2)}, u32[]{:S(2)}) collective-permute-start(f32[5,128,256]{2,1,0:T(8,128)S(1)} %shard_map.51), channel_id=1, source_target_pairs={{0,27},{2,9},{4,31},{6,13},{8,3},{10,17},{12,7},{14,21},{16,11},{1... | collective-permute-start | bytes 1966088 | tf_op jit(solution)/shard_map/ppermute | solution.py:369
  49.8 18.2 %collective-permute-start.10 = (f32[4,128,256]{2,1,0:T(8,128)}, f32[4,128,256]{2,1,0:T(8,128)S(1)}, u32[]{:S(2)}, u32[]{:S(2)}) collective-permute-start(f32[4,128,256]{2,1,0:T(8,128)} %collective-permute-done.3), channel_id=1, source_target_pairs={{1,8},{3,26},{5,12},{7,30},{9,16},{11,2},{13,20},{15,6},{17,24},{1... | collective-permute-start | bytes 1572872 | tf_op jit(solution)/shard_map/ppermute | solution.py:369
  66.5 2.8 %collective-permute-start.9 = (f32[3,128,256]{2,1,0:T(8,128)S(1)}, f32[3,128,256]{2,1,0:T(8,128)S(1)}, u32[]{:S(2)}, u32[]{:S(2)}) collective-permute-start(f32[3,128,256]{2,1,0:T(8,128)S(1)} %slice.16), channel_id=1, source_target_pairs={{0,2},{2,0},{4,6},{6,4},{1,3},{3,1},{5,7},{7,5},{8,10},{10,8},{12,... | collective-permute-start | bytes 1179656 | tf_op jit(solution)/shard_map/ppermute | solution.py:354
  72.4 2.9 %collective-permute-start.12 = (f32[9,128,256]{2,1,0:T(8,128)S(1)}, f32[9,128,256]{2,1,0:T(8,128)S(1)}, u32[]{:S(2)}, u32[]{:S(2)}) collective-permute-start(f32[9,128,256]{2,1,0:T(8,128)S(1)} %get-tuple-element.44.swap), channel_id=1, source_target_pairs={{0,2},{2,0},{4,6},{6,4},{1,3},{3,1},{5,7},{7,5},{8,10},{10,8},{12,... | collective-permute-start | bytes 3538952 | tf_op jit(solution)/shard_map/ppermute | solution.py:354

commit v7 on v6

--- a/solution.py
+++ b/solution.py
@@ -263,6 +263,7 @@
 ):
     plane = counter(scalars)
     begin_first = scalars[FIRST]
+    back = (scalars[CORE] > 0.5).astype(jnp.int32)
     for place in range(9, 12):
         begin[place] = begin_first * start[plane(place)] + far[11 - place]
 
@@ -295,29 +296,73 @@
     total[5] = jnp.zeros_like(total[5])
     for place in range(OUTER, OUTER + HALF):
         index = place - 4
+        order = index - 1 + back * (HALF + 1 - 2 * index)
         for first in chunks(Plane(total, 0), 16):
             states = [Plane(last, target, index).rows(first, 16) for target in range(NODES)]
             local = mixed(scalars, WEIGHT, [cubed(state) for state in states])
             nearby, centre = around_place(total, index, first, 16)
             force = diffusion * (nearby - 6.0 * centre) + reaction * local
-            Plane(mine, index - 1).put(first, states[0])
-            Plane(swap, index - 1).put(first, states[2])
-            Plane(swap, index - 1 + HALF).put(first, Plane(begin_near, place).rows(first, 16) + time_step * force)
+            Plane(mine, order).put(first, states[0])
+            Plane(swap, order).put(first, states[2])
+            Plane(swap, order + HALF).put(first, Plane(begin_near, place).rows(first, 16) + time_step * force)
     swap[2 * HALF] = total[HALF]
 
 
-def join_kernel(scalars, mine, swap, other, state, end):
-    plane = counter(scalars)
-    for index in range(HALF):
-        near, far = plane(OUTER + index), plane(OUTER + SLAB - 1 - index)
-        state[near] = mine[index]
-        state[far] = other[index]
-        own, others = swap[HALF + index], other[HALF + index]
-        if index == HALF - 1:
-            own = own + (time_step * diffusion) * other[2 * HALF]
-            others = others + (time_step * diffusion) * swap[2 * HALF]
-        end[near] = own
-        end[far] = others
+def finished(copies):
+    for copy in copies:
+        copy.start()
+    for copy in copies:
+        copy.wait()
+
+
+def own_half_kernel(scalars, mine, swap, state, end, sems):
+    upper = (scalars[CORE] > 0.5).astype(jnp.int32)
+    base = HALF * upper
+    inner = pl.ds(HALF + upper, HALF - 1)
+    finished([
+        pltpu.make_async_copy(mine, state.at[pl.ds(base, HALF)], sems.at[0]),
+        pltpu.make_async_copy(swap.at[inner], end.at[pl.ds(base + upper, HALF - 1)], sems.at[1]),
+    ])
+
+
+def other_half_kernel(scalars, swap, other, state_before, end_before, state, end, cut, sems):
+    upper = (scalars[CORE] > 0.5).astype(jnp.int32)
+    base, base_other = HALF * upper, HALF * (1 - upper)
+    edge, edge_other = (HALF - 1) * (1 - upper), (HALF - 1) * upper
+    inner = pl.ds(HALF + 1 - upper, HALF - 1)
+    halves = [
+        pltpu.make_async_copy(other.at[pl.ds(0, HALF)], state.at[pl.ds(base_other, HALF)], sems.at[0]),
+        pltpu.make_async_copy(other.at[inner], end.at[pl.ds(base_other + 1 - upper, HALF - 1)], sems.at[1]),
+    ]
+    for copy in halves:
+        copy.start()
+    cut[0] = swap[HALF + edge] + (time_step * diffusion) * other[2 * HALF]
+    cut[1] = other[HALF + edge_other] + (time_step * diffusion) * swap[2 * HALF]
+    finished([
+        pltpu.make_async_copy(cut.at[0], end.at[base + edge], sems.at[2]),
+        pltpu.make_async_copy(cut.at[1], end.at[base_other + edge_other], sems.at[3]),
+    ])
+    for copy in halves:
+        copy.wait()
+
+
+def join_call(scalars, mine, swap, other, shape):
+    def placed(kernel, operands, before, scratch, sems):
+        vmem, anywhere = pl.BlockSpec(memory_space=pltpu.VMEM), pl.BlockSpec(memory_space=pl.ANY)
+        first = 1 + len(operands)
+        return pl.pallas_call(
+            kernel,
+            out_shape=[jax.ShapeDtypeStruct(shape, F32)] * 2,
+            in_specs=[pl.BlockSpec(memory_space=pltpu.SMEM)] + [vmem] * len(operands) + [anywhere] * len(before),
+            out_specs=[anywhere] * 2,
+            input_output_aliases={first + index: index for index in range(len(before))},
+            scratch_shapes=[*scratch, pltpu.SemaphoreType.DMA((sems,))],
+            compiler_params=pltpu.CompilerParams(vmem_limit_bytes=16 << 20),
+            cost_estimate=pl.CostEstimate(flops=1000, bytes_accessed=1000, transcendentals=0),
+        )(scalars, *operands, *before)
+
+    halves = placed(own_half_kernel, [mine, swap], [], [], 2)
+    return placed(other_half_kernel, [swap, other], halves, [pltpu.VMEM((2, *shape[1:]), F32)], 4)
 
 
 def call(kernel, scalars, operands, outs, scratch, limit):
@@ -402,7 +447,7 @@
         last_kernel, scalars, [start, far, *begun, kept, part], [planes(HALF), planes(2 * HALF + 1)],
         [planes(12), planes(11), planes(10), planes(NODES, 5), planes(6)], 24,
     )
-    state_new, end_new = call(join_kernel, scalars, [mine, swap, beside(swap)], [planes(slab)] * 2, [], 16)
+    state_new, end_new = join_call(scalars, mine, swap, beside(swap), planes(slab))
     return (state_new[None, None], end_new[None])
 
 

time: 77.7 us -> 77.4 us (level)
  waiting for transfers between devices: 21 us -> 19.9 us
    pallas_call x0 -> x2, Pallas kernels: none -> 3.06 us  [placed(): pl.pallas_call(kernel, out_shape=[jax.ShapeDtypeStruct(shape, F32)] * 2,...]
    pallas_call x8 -> x7, Pallas kernels: 28.7 us -> 26.1 us  [call(): pl.pallas_call(kernel, out_shape=[jax.ShapeDtypeStruct(shape, F32) for sh...]
    ppermute x4, waiting for transfers between devices: 5.84 us -> 4.35 us  [beside(): lax.ppermute(array, 'node', [(node, node ^ 1) for node in range(NODES)])]
  transfers between devices with their start and end apart: 13 -> 13, of which waited for: 6 -> 7; matrix products, arithmetic and copies ran while one was open for 3% -> 3% of each run, Pallas kernels for 31% -> 32%
where the time goes in v7:
time: 77.4 us; the launch traced here: 77 us
  Pallas kernels  29.2 us (38%)
  starting transfers between devices  22.1 us (29%)
  waiting for transfers between devices  19.9 us (26%)
  local copies, waits for them, and re-layouts  4.23 us (5%)
  between operations  1.59 us (2%)
    pallas_call x7, Pallas kernels, call(): pl.pallas_call(kernel, out_shape=[jax.ShapeDtypeStruct(shape, F32) for sh...  26.1 us
    ppermute x6, starting transfers between devices, spread(): return lax.ppermute(array, ('space', 'node', 'tm'), pairs)  16.5 us
    ppermute x3, waiting for transfers between devices, across(): lax.ppermute(array, 'node', [(node, node ^ 2) for node in range(NODES)])  13.9 us
    ppermute x3, starting transfers between devices, across(): lax.ppermute(array, 'node', [(node, node ^ 2) for node in range(NODES)])  4.92 us
    ppermute x4, waiting for transfers between devices, beside(): lax.ppermute(array, 'node', [(node, node ^ 1) for node in range(NODES)])  4.35 us
    pallas_call x2, Pallas kernels, placed(): pl.pallas_call(kernel, out_shape=[jax.ShapeDtypeStruct(shape, F32)] * 2,...  3.06 us
    unnamed x8, local copies, waits for them, and re-layouts  2.03 us
    ppermute x6, waiting for transfers between devices, spread(): return lax.ppermute(array, ('space', 'node', 'tm'), pairs)  1.67 us
  transfers between devices with their start and end apart: 13, of which 7 were waited for; matrix products, arithmetic and copies ran while one was open for 3% of the time, Pallas kernels for 32%

profile of v7, /device:TPU:0, one launch (start us, length us, event | category | flops | bytes accessed | tf_op | source)
XLA Modules:
  0.0 77.0 jit_solution(13837357160583502460)
XLA Ops:
  1.1 2.6 %collective-permute-start.1 = (f32[8,128,256]{2,1,0:T(8,128)}, f32[8,128,256]{2,1,0:T(8,128)}, u32[]{:S(2)}, u32[]{:S(2)}) collective-permute-start(f32[8,128,256]{2,1,0:T(8,128)} %bitcast.11), channel_id=1, source_target_pairs={{0,4},{2,6},{4,0},{6,2},{1,5},{3,7},{5,1},{7,3},{8,12},{10,14},{12... | collective-permute-start | bytes 3145736 | tf_op jit(solution)/shard_map/ppermute | solution.py:396
  4.4 1.2 %copy-done = f32[1,1,8,128,256]{4,3,2,1,0:T(8,128)S(1)} copy-done((f32[1,1,8,128,256]{4,3,2,1,0:T(8,128)S(1)}, f32[1,1,8,128,256]{4,3,2,1,0:T(8,128)}, u32[]{:S(2)}) %copy-start) | copy-done | bytes 1048600
  5.7 1.5 %shard_map.50 = (f32[6,128,256]{2,1,0:T(8,128)}, f32[4,128,256]{2,1,0:T(8,128)S(1)}) custom-call(f32[46]{0:T(128)S(1)} %constant_dynamic-update-slice_fusion.scalars, f32[8,128,256]{2,1,0:T(8,128)S(1)} %bitcast.12, f32[8,128,256]{2,1,0:T(8,128)S(1)} %collective-permute-done.2.beside), custom_call_target="tpu_custom_call" | custom-call | flops 1000 | bytes 1000 | tf_op jit(solution)/shard_map/pallas_call | solution.py:369
  8.0 2.2 %collective-permute-start.5 = (f32[6,128,256]{2,1,0:T(8,128)}, f32[6,128,256]{2,1,0:T(8,128)}, u32[]{:S(2)}, u32[]{:S(2)}) collective-permute-start(f32[6,128,256]{2,1,0:T(8,128)} %get-tuple-element.35), channel_id=1, source_target_pairs={{0,8},{1,9},{2,26},{3,27},{4,12},{5,13},{6,30},{7,31},{8,16},{9,17... | collective-permute-start | bytes 2359304 | tf_op jit(solution)/shard_map/ppermute | solution.py:414
  11.0 4.3 %collective-permute-start.3 = (f32[4,128,256]{2,1,0:T(8,128)}, f32[4,128,256]{2,1,0:T(8,128)}, u32[]{:S(2)}, u32[]{:S(2)}) collective-permute-start(f32[4,128,256]{2,1,0:T(8,128)} %dynamic-slice_bitcast_fusion), channel_id=1, source_target_pairs={{0,1},{2,3},{4,5},{6,7},{8,9},{10,11},{12,13},{14,15},{16,17},{18,... | collective-permute-start | bytes 1572872 | tf_op jit(solution)/shard_map/ppermute | solution.py:414
  15.3 1.6 %collective-permute-start.7 = (f32[4,128,256]{2,1,0:T(8,128)}, f32[4,128,256]{2,1,0:T(8,128)}, u32[]{:S(2)}, u32[]{:S(2)}) collective-permute-start(f32[4,128,256]{2,1,0:T(8,128)} %copy-done.3), channel_id=1, source_target_pairs={{0,8},{1,9},{2,26},{3,27},{4,12},{5,13},{6,30},{7,31},{8,16},{9,17... | collective-permute-start | bytes 1572872 | tf_op jit(solution)/shard_map/ppermute | solution.py:414
  18.2 9.6 %collective-permute-done.1.across = f32[8,128,256]{2,1,0:T(8,128)} collective-permute-done((f32[8,128,256]{2,1,0:T(8,128)}, f32[8,128,256]{2,1,0:T(8,128)}, u32[]{:S(2)}, u32[]{:S(2)}) %collective-permute-start.1) | collective-permute-done | bytes 1048608 | tf_op jit(solution)/shard_map/ppermute | solution.py:396
  27.8 3.0 %conditional.1 = (f32[8,128,256]{2,1,0:T(8,128)}) conditional(s32[]{:T(128)} %bitcast.4, f32[8,128,256]{2,1,0:T(8,128)} %collective-permute-done.1.across, f32[8,128,256]{2,1,0:T(8,128)} %collective-permute-done.1.across), branch_computations={%region_0.0_spmd, %region_1.0_spmd} | conditional | bytes 4194352 | solution.py:404
  27.8 3.0 %collective-permute-done = f32[8,128,256]{2,1,0:T(8,128)} collective-permute-done((f32[8,128,256]{2,1,0:T(8,128)}, f32[8,128,256]{2,1,0:T(8,128)}, u32[]{:S(2)}, u32[]{:S(2)}) %collective-permute-start) | collective-permute-done | bytes 1048608 | tf_op jit(solution)/shard_map/cond/branch_1_fun/ppermute | solution.py:399
  30.8 1.8 %collective-permute-start.6 = (f32[6,128,256]{2,1,0:T(8,128)}, f32[6,128,256]{2,1,0:T(8,128)S(1)}, u32[]{:S(2)}, u32[]{:S(2)}) collective-permute-start(f32[6,128,256]{2,1,0:T(8,128)} %collective-permute-done.5.halo_a), channel_id=1, source_target_pairs={{0,4},{2,6},{4,0},{6,2},{1,5},{3,7},{5,1},{7,3},{8,12},{10,14},{12... | collective-permute-start | bytes 2359304 | tf_op jit(solution)/shard_map/ppermute | solution.py:396
  32.6 2.4 %shard_map.51 = f32[5,128,256]{2,1,0:T(8,128)S(1)} custom-call(f32[46]{0:T(128)S(1)} %constant_dynamic-update-slice_fusion.scalars, f32[8,128,256]{2,1,0:T(8,128)S(1)} %bitcast.13, f32[8,128,256]{2,1,0:T(8,128)} %collective-permute-done.1.across, f32[8,128,256]{2,1,0:T(8,128)S(1)} %collective-permute-done.2.beside, f32[8,128,256]{2,1,0:T(8,128)} %get-tuple-element.51.corner, ...), custom_call_target="tpu_custom_call" | custom-call | flops 1000 | bytes 1000 | tf_op jit(solution)/shard_map/pallas_call | solution.py:369
  35.0 3.5 %collective-permute-start.4 = (f32[5,128,256]{2,1,0:T(8,128)S(1)}, f32[5,128,256]{2,1,0:T(8,128)S(1)}, u32[]{:S(2)}, u32[]{:S(2)}) collective-permute-start(f32[5,128,256]{2,1,0:T(8,128)S(1)} %shard_map.51), channel_id=1, source_target_pairs={{0,1},{2,3},{4,5},{6,7},{8,9},{10,11},{12,13},{14,15},{16,17},{18,... | collective-permute-start | bytes 1966088 | tf_op jit(solution)/shard_map/ppermute | solution.py:414
  38.4 7.2 %shard_map.52.kept = f32[4,9,128,256]{3,2,1,0:T(8,128)S(1)} custom-call(f32[46]{0:T(128)S(1)} %constant_dynamic-update-slice_fusion.scalars, f32[8,128,256]{2,1,0:T(8,128)S(1)} %bitcast.14, f32[8,128,256]{2,1,0:T(8,128)} %collective-permute-done.1.across, f32[8,128,256]{2,1,0:T(8,128)S(1)} %collective-permute-done.2.beside, ...), custom_call_target="tpu_custom_call" | custom-call | flops 1000 | bytes 1000 | tf_op jit(solution)/shard_map/pallas_call | solution.py:369
  46.2 3.5 %collective-permute-start.11 = (f32[5,128,256]{2,1,0:T(8,128)S(1)}, f32[5,128,256]{2,1,0:T(8,128)S(1)}, u32[]{:S(2)}, u32[]{:S(2)}) collective-permute-start(f32[5,128,256]{2,1,0:T(8,128)S(1)} %shard_map.51), channel_id=1, source_target_pairs={{0,27},{2,9},{4,31},{6,13},{8,3},{10,17},{12,7},{14,21},{16,11},{1... | collective-permute-start | bytes 1966088 | tf_op jit(solution)/shard_map/ppermute | solution.py:414
  49.7 1.5 %collective-permute-start.10 = (f32[4,128,256]{2,1,0:T(8,128)}, f32[4,128,256]{2,1,0:T(8,128)S(1)}, u32[]{:S(2)}, u32[]{:S(2)}) collective-permute-start(f32[4,128,256]{2,1,0:T(8,128)} %collective-permute-done.3), channel_id=1, source_target_pairs={{1,8},{3,26},{5,12},{7,30},{9,16},{11,2},{13,20},{15,6},{17,24},{1... | collective-permute-start | bytes 1572872 | tf_op jit(solution)/shard_map/ppermute | solution.py:414
  51.4 6.3 %shard_map.53.kept = f32[4,12,128,256]{3,2,1,0:T(8,128)S(1)} custom-call(f32[46]{0:T(128)S(1)} %constant_dynamic-update-slice_fusion.scalars, f32[8,128,256]{2,1,0:T(8,128)S(1)} %bitcast.15, f32[8,128,256]{2,1,0:T(8,128)} %collective-permute-done.1.across, f32[8,128,256]{2,1,0:T(8,128)S(1)} %collective-permute-done.2.beside, ...), custom_call_target="tpu_custom_call" | custom-call | flops 1000 | bytes 1000 | tf_op jit(solution)/shard_map/pallas_call | solution.py:369
  57.7 4.1 %collective-permute-done.8.across_b = f32[4,128,256]{2,1,0:T(8,128)S(1)} collective-permute-done((f32[4,128,256]{2,1,0:T(8,128)}, f32[4,128,256]{2,1,0:T(8,128)S(1)}, u32[]{:S(2)}, u32[]{:S(2)}) %collective-permute-start.8) | collective-permute-done | bytes 524320 | tf_op jit(solution)/shard_map/ppermute | solution.py:396
  61.8 4.3 %shard_map.54.part = f32[4,2,128,256]{3,2,1,0:T(8,128)S(1)} custom-call(f32[46]{0:T(128)S(1)} %constant_dynamic-update-slice_fusion.scalars, f32[6,128,256]{2,1,0:T(8,128)} %collective-permute-done.5.halo_a, f32[6,128,256]{2,1,0:T(8,128)S(1)} %collective-permute-done.6.across_a, f32[4,128,256]{2,1,0:T(8,128)} %collective-permute-done.7.halo_b, ...), custom_call_target="tpu_custom_call" | custom-call | flops 1000 | bytes 1000 | tf_op jit(solution)/shard_map/pallas_call | solution.py:369
  66.5 1.4 %collective-permute-done.10.halo_start = f32[4,128,256]{2,1,0:T(8,128)S(1)} collective-permute-done((f32[4,128,256]{2,1,0:T(8,128)}, f32[4,128,256]{2,1,0:T(8,128)S(1)}, u32[]{:S(2)}, u32[]{:S(2)}) %collective-permute-start.10) | collective-permute-done | bytes 524320 | tf_op jit(solution)/shard_map/ppermute | solution.py:414
  68.0 1.3 %shard_map.55 = (f32[9,128,256]{2,1,0:T(8,128)S(1)}, f32[8,128,256]{2,1,0:T(8,128)S(1)}, f32[7,128,256]{2,1,0:T(8,128)S(1)}) custom-call(f32[46]{0:T(128)S(1)} %constant_dynamic-update-slice_fusion.scalars, f32[8,128,256]{2,1,0:T(8,128)S(1)} %bitcast.17, f32[4,128,256]{2,1,0:T(8,128)S(1)} %collective-permute-done.10.halo_start, ...), custom_call_target="tpu_custom_call" | custom-call | flops 1000 | bytes 1000 | tf_op jit(solution)/shard_map/pallas_call | solution.py:369
  69.3 3.0 %shard_map.56 = (f32[4,128,256]{2,1,0:T(8,128)S(1)}, f32[9,128,256]{2,1,0:T(8,128)S(1)}) custom-call(f32[46]{0:T(128)S(1)} %constant_dynamic-update-slice_fusion.scalars, f32[8,128,256]{2,1,0:T(8,128)S(1)} %bitcast.18, f32[3,128,256]{2,1,0:T(8,128)S(1)} %collective-permute-done.9.far, f32[9,128,256]{2,1,0:T(8,128)S(1)} %get-tuple-element.42.begin_near, ...), custom_call_target="tpu_custom_call" | custom-call | flops 1000 | bytes 1000 | tf_op jit(solution)/shard_map/pallas_call | solution.py:369
  72.4 1.5 %shard_map.57 = (f32[8,128,256]{2,1,0:T(8,128)}, f32[8,128,256]{2,1,0:T(8,128)}) custom-call(f32[46]{0:T(128)S(1)} %constant_dynamic-update-slice_fusion.scalars, f32[4,128,256]{2,1,0:T(8,128)S(1)} %get-tuple-element.46.mine, f32[9,128,256]{2,1,0:T(8,128)S(1)} %get-tuple-element.45.swap), custom_call_target="tpu_custom_call" | custom-call | flops 1000 | bytes 1000 | tf_op jit(solution)/shard_map/pallas_call | solution.py:353
  73.9 1.3 %collective-permute-done.12.other = f32[9,128,256]{2,1,0:T(8,128)S(1)} collective-permute-done((f32[9,128,256]{2,1,0:T(8,128)S(1)}, f32[9,128,256]{2,1,0:T(8,128)S(1)}, u32[]{:S(2)}, u32[]{:S(2)}) %collective-permute-start.12) | collective-permute-done | bytes 1179680 | tf_op jit(solution)/shard_map/ppermute | solution.py:399
  75.2 1.6 %shard_map.58 = (f32[8,128,256]{2,1,0:T(8,128)}, f32[8,128,256]{2,1,0:T(8,128)}) custom-call(f32[46]{0:T(128)S(1)} %constant_dynamic-update-slice_fusion.scalars, f32[9,128,256]{2,1,0:T(8,128)S(1)} %get-tuple-element.45.swap, f32[9,128,256]{2,1,0:T(8,128)S(1)} %collective-permute-done.12.other, ...), custom_call_target="tpu_custom_call", output_to_operand_aliasing={{0}: (3, {}), {1}: (4, {})} | custom-call | flops 1000 | bytes 1000 | tf_op jit(solution)/shard_map/pallas_call | solution.py:353
  (25 shorter events, 4.7 us)
Async XLA Ops:
  0.6 3.8 %collective-permute-start.2 = (f32[8,128,256]{2,1,0:T(8,128)}, f32[8,128,256]{2,1,0:T(8,128)S(1)}, u32[]{:S(2)}, u32[]{:S(2)}) collective-permute-start(f32[8,128,256]{2,1,0:T(8,128)} %bitcast.10), channel_id=1, source_target_pairs={{0,2},{2,0},{4,6},{6,4},{1,3},{3,1},{5,7},{7,5},{8,10},{10,8},{12,... | collective-permute-start | bytes 3145736 | tf_op jit(solution)/shard_map/ppermute | solution.py:399
  1.1 26.6 %collective-permute-start.1 = (f32[8,128,256]{2,1,0:T(8,128)}, f32[8,128,256]{2,1,0:T(8,128)}, u32[]{:S(2)}, u32[]{:S(2)}) collective-permute-start(f32[8,128,256]{2,1,0:T(8,128)} %bitcast.11), channel_id=1, source_target_pairs={{0,4},{2,6},{4,0},{6,2},{1,5},{3,7},{5,1},{7,3},{8,12},{10,14},{12... | collective-permute-start | bytes 3145736 | tf_op jit(solution)/shard_map/ppermute | solution.py:396
  4.4 1.2 %copy-start = (f32[1,1,8,128,256]{4,3,2,1,0:T(8,128)S(1)}, f32[1,1,8,128,256]{4,3,2,1,0:T(8,128)}, u32[]{:S(2)}) copy-start(f32[1,1,8,128,256]{4,3,2,1,0:T(8,128)} %param.8) | copy-start | bytes 3145732
  5.6 4.5 %copy-start.2 = (f32[1,8,128,256]{3,2,1,0:T(8,128)S(1)}, f32[1,8,128,256]{3,2,1,0:T(8,128)}, u32[]{:S(2)}) copy-start(f32[1,8,128,256]{3,2,1,0:T(8,128)} %param.7) | copy-start | bytes 3145732
  7.2 0.8 %copy-start.3 = (f32[4,128,256]{2,1,0:T(8,128)}, f32[4,128,256]{2,1,0:T(8,128)S(1)}, u32[]{:S(2)}) copy-start(f32[4,128,256]{2,1,0:T(8,128)S(1)} %get-tuple-element.39) | copy-start | bytes 1572868
  8.0 22.8 %collective-permute-start.5 = (f32[6,128,256]{2,1,0:T(8,128)}, f32[6,128,256]{2,1,0:T(8,128)}, u32[]{:S(2)}, u32[]{:S(2)}) collective-permute-start(f32[6,128,256]{2,1,0:T(8,128)} %get-tuple-element.35), channel_id=1, source_target_pairs={{0,8},{1,9},{2,26},{3,27},{4,12},{5,13},{6,30},{7,31},{8,16},{9,17... | collective-permute-start | bytes 2359304 | tf_op jit(solution)/shard_map/ppermute | solution.py:414
  11.0 21.6 %copy-start.1 = (f32[1,1,8,128,256]{4,3,2,1,0:T(8,128)S(1)}, f32[1,1,8,128,256]{4,3,2,1,0:T(8,128)}, u32[]{:S(2)}) copy-start(f32[1,1,8,128,256]{4,3,2,1,0:T(8,128)} %param.8) | copy-start | bytes 3145732
  11.0 21.6 %collective-permute-start.3 = (f32[4,128,256]{2,1,0:T(8,128)}, f32[4,128,256]{2,1,0:T(8,128)}, u32[]{:S(2)}, u32[]{:S(2)}) collective-permute-start(f32[4,128,256]{2,1,0:T(8,128)} %dynamic-slice_bitcast_fusion), channel_id=1, source_target_pairs={{0,1},{2,3},{4,5},{6,7},{8,9},{10,11},{12,13},{14,15},{16,17},{18,... | collective-permute-start | bytes 1572872 | tf_op jit(solution)/shard_map/ppermute | solution.py:414
  15.3 30.3 %collective-permute-start.7 = (f32[4,128,256]{2,1,0:T(8,128)}, f32[4,128,256]{2,1,0:T(8,128)}, u32[]{:S(2)}, u32[]{:S(2)}) collective-permute-start(f32[4,128,256]{2,1,0:T(8,128)} %copy-done.3), channel_id=1, source_target_pairs={{0,8},{1,9},{2,26},{3,27},{4,12},{5,13},{6,30},{7,31},{8,16},{9,17... | collective-permute-start | bytes 1572872 | tf_op jit(solution)/shard_map/ppermute | solution.py:414
  27.8 3.0 %collective-permute-start = (f32[8,128,256]{2,1,0:T(8,128)}, f32[8,128,256]{2,1,0:T(8,128)}, u32[]{:S(2)}, u32[]{:S(2)}) collective-permute-start(f32[8,128,256]{2,1,0:T(8,128)} %param.3), channel_id=1, source_target_pairs={{0,2},{2,0},{4,6},{6,4},{1,3},{3,1},{5,7},{7,5},{8,10},{10,8},{12,... | collective-permute-start | bytes 3145736 | tf_op jit(solution)/shard_map/cond/branch_1_fun/ppermute | solution.py:399
  30.8 20.6 %collective-permute-start.6 = (f32[6,128,256]{2,1,0:T(8,128)}, f32[6,128,256]{2,1,0:T(8,128)S(1)}, u32[]{:S(2)}, u32[]{:S(2)}) collective-permute-start(f32[6,128,256]{2,1,0:T(8,128)} %collective-permute-done.5.halo_a), channel_id=1, source_target_pairs={{0,4},{2,6},{4,0},{6,2},{1,5},{3,7},{5,1},{7,3},{8,12},{10,14},{12... | collective-permute-start | bytes 2359304 | tf_op jit(solution)/shard_map/ppermute | solution.py:396
  35.0 31.5 %collective-permute-start.4 = (f32[5,128,256]{2,1,0:T(8,128)S(1)}, f32[5,128,256]{2,1,0:T(8,128)S(1)}, u32[]{:S(2)}, u32[]{:S(2)}) collective-permute-start(f32[5,128,256]{2,1,0:T(8,128)S(1)} %shard_map.51), channel_id=1, source_target_pairs={{0,1},{2,3},{4,5},{6,7},{8,9},{10,11},{12,13},{14,15},{16,17},{18,... | collective-permute-start | bytes 1966088 | tf_op jit(solution)/shard_map/ppermute | solution.py:414
  45.6 16.2 %collective-permute-start.8 = (f32[4,128,256]{2,1,0:T(8,128)}, f32[4,128,256]{2,1,0:T(8,128)S(1)}, u32[]{:S(2)}, u32[]{:S(2)}) collective-permute-start(f32[4,128,256]{2,1,0:T(8,128)} %collective-permute-done.7.halo_b), channel_id=1, source_target_pairs={{0,4},{2,6},{4,0},{6,2},{1,5},{3,7},{5,1},{7,3},{8,12},{10,14},{12... | collective-permute-start | bytes 1572872 | tf_op jit(solution)/shard_map/ppermute | solution.py:396
  46.2 21.7 %collective-permute-start.11 = (f32[5,128,256]{2,1,0:T(8,128)S(1)}, f32[5,128,256]{2,1,0:T(8,128)S(1)}, u32[]{:S(2)}, u32[]{:S(2)}) collective-permute-start(f32[5,128,256]{2,1,0:T(8,128)S(1)} %shard_map.51), channel_id=1, source_target_pairs={{0,27},{2,9},{4,31},{6,13},{8,3},{10,17},{12,7},{14,21},{16,11},{1... | collective-permute-start | bytes 1966088 | tf_op jit(solution)/shard_map/ppermute | solution.py:414
  49.7 18.2 %collective-permute-start.10 = (f32[4,128,256]{2,1,0:T(8,128)}, f32[4,128,256]{2,1,0:T(8,128)S(1)}, u32[]{:S(2)}, u32[]{:S(2)}) collective-permute-start(f32[4,128,256]{2,1,0:T(8,128)} %collective-permute-done.3), channel_id=1, source_target_pairs={{1,8},{3,26},{5,12},{7,30},{9,16},{11,2},{13,20},{15,6},{17,24},{1... | collective-permute-start | bytes 1572872 | tf_op jit(solution)/shard_map/ppermute | solution.py:414
  66.5 2.8 %collective-permute-start.9 = (f32[3,128,256]{2,1,0:T(8,128)S(1)}, f32[3,128,256]{2,1,0:T(8,128)S(1)}, u32[]{:S(2)}, u32[]{:S(2)}) collective-permute-start(f32[3,128,256]{2,1,0:T(8,128)S(1)} %slice.16), channel_id=1, source_target_pairs={{0,2},{2,0},{4,6},{6,4},{1,3},{3,1},{5,7},{7,5},{8,10},{10,8},{12,... | collective-permute-start | bytes 1179656 | tf_op jit(solution)/shard_map/ppermute | solution.py:399
  72.3 2.9 %collective-permute-start.12 = (f32[9,128,256]{2,1,0:T(8,128)S(1)}, f32[9,128,256]{2,1,0:T(8,128)S(1)}, u32[]{:S(2)}, u32[]{:S(2)}) collective-permute-start(f32[9,128,256]{2,1,0:T(8,128)S(1)} %get-tuple-element.45.swap), channel_id=1, source_target_pairs={{0,2},{2,0},{4,6},{6,4},{1,3},{3,1},{5,7},{7,5},{8,10},{10,8},{12,... | collective-permute-start | bytes 3538952 | tf_op jit(solution)/shard_map/ppermute | solution.py:399

commit v8 on v7

--- a/solution.py
+++ b/solution.py
@@ -233,18 +233,7 @@
     run_stage(2, scalars, state, kept, out, spare)
 
 
-def around_place(ref, place, first, count):
-    return around(*(Plane(ref, place + by) for by in (-1, 0, 1)), first, count)
-
-
-def raise_power(source, sink, places):
-    for place in places:
-        out = Plane(sink, place)
-        for first in chunks(out, 32):
-            out.put(first, around_place(source, place, first, 32)[0])
-
-
-def begin_kernel(scalars, start, halo_start, near, away, begin, once, twice):
+def last_kernel(scalars, start, halo_start, near, far, away, kept, part, mine, swap, begin, once, twice, last, total):
     plane = counter(scalars)
     begin_first = scalars[FIRST]
     back = (scalars[CORE] > 0.5).astype(jnp.int32)
@@ -254,37 +243,22 @@
     begin[5] = (begin_first * start[plane(5)] + near[1]) + away[0]
     for place in range(6, 9):
         begin[place] = begin_first * start[plane(place)] + near[place - 4]
-    raise_power(begin, once, range(2, 8))
-    raise_power(once, twice, range(3, 7))
-
-
-def last_kernel(
-    scalars, start, far, begin_near, once_near, twice_near, kept, part, mine, swap, begin, once, twice, last, total
-):
-    plane = counter(scalars)
-    begin_first = scalars[FIRST]
-    back = (scalars[CORE] > 0.5).astype(jnp.int32)
     for place in range(9, 12):
         begin[place] = begin_first * start[plane(place)] + far[11 - place]
 
-    def at(place, near, own, split):
-        return Plane(near if place < split else own, place)
-
-    def raised(near_source, source, split, sink, places):
+    def around_place(ref, place, first, count):
+        return around(*(Plane(ref, place + by) for by in (-1, 0, 1)), first, count)
+
+    for source, sink, places in ((begin, once, range(2, 11)), (once, twice, range(3, 10))):
         for place in places:
-            planes = [at(place + by, near_source, source, split) for by in (-1, 0, 1)]
             out = Plane(sink, place)
             for first in chunks(out, 32):
-                out.put(first, around(*planes, first, 32)[0])
-
-    raised(begin_near, begin, 9, once, range(8, 11))
-    raised(once_near, once, 8, twice, range(7, 10))
+                out.put(first, around_place(source, place, first, 32)[0])
     kept_x4 = {key: index for index, key in enumerate(kept_keys(1))}
     for place in range(4, 9):
-        planes = [at(place + by, twice_near, twice, 7) for by in (-1, 0, 1)]
         for first in chunks(Plane(total, 0), 16):
-            thrice, two = around(*planes, first, 16)
-            zero, one = Plane(begin_near, place).rows(first, 16), at(place, once_near, once, 8).rows(first, 16)
+            thrice, two = around_place(twice, place, first, 16)
+            zero, one = Plane(begin, place).rows(first, 16), Plane(once, place).rows(first, 16)
             values = []
             for target in range(NODES):
                 mix = scalars[MIX + target]
@@ -302,9 +276,10 @@
             local = mixed(scalars, WEIGHT, [cubed(state) for state in states])
             nearby, centre = around_place(total, index, first, 16)
             force = diffusion * (nearby - 6.0 * centre) + reaction * local
+            value = Plane(begin, place).rows(first, 16) + time_step * force
             Plane(mine, order).put(first, states[0])
             Plane(swap, order).put(first, states[2])
-            Plane(swap, order + HALF).put(first, Plane(begin_near, place).rows(first, 16) + time_step * force)
+            Plane(swap, order + HALF).put(first, value)
     swap[2 * HALF] = total[HALF]
 
 
@@ -442,9 +417,8 @@
     kept = stage(1, second_kernel, [*sources, halo_a, across_a, kept], 24)
     part = stage(2, third_kernel, [halo_a, across_a, halo_b, across_b, kept], 24)
     far = beside(after(near, part)[2:])
-    begun = call(begin_kernel, scalars, [start, halo_start, near, away], [planes(9), planes(8), planes(7)], [], 16)
     mine, swap = call(
-        last_kernel, scalars, [start, far, *begun, kept, part], [planes(HALF), planes(2 * HALF + 1)],
+        last_kernel, scalars, [start, halo_start, near, far, away, kept, part], [planes(HALF), planes(2 * HALF + 1)],
         [planes(12), planes(11), planes(10), planes(NODES, 5), planes(6)], 24,
     )
     state_new, end_new = join_call(scalars, mine, swap, beside(swap), planes(slab))

time: 77.4 us -> 77.2 us (level)
  waiting for transfers between devices: 19.9 us -> 18.7 us
  local copies, waits for them, and re-layouts: 4.23 us -> 5.18 us
    ppermute x3, waiting for transfers between devices: 13.9 us -> 12.8 us  [across(): lax.ppermute(array, 'node', [(node, node ^ 2) for node in range(NODES)])]
    dynamic_slice x1, local copies, waits for them, and re-layouts: 0.83 us -> 1.87 us  [on_device(): lax.dynamic_slice_in_dim(start, HALF * (1 - lax.rem(node_index, 2)), HALF...]
    pallas_call x7 -> x6, Pallas kernels: 26.1 us -> 26.3 us  [call(): pl.pallas_call(kernel, out_shape=[jax.ShapeDtypeStruct(shape, F32) for sh...]
  transfers between devices with their start and end apart: 13 -> 13, of which waited for: 7 -> 7; matrix products, arithmetic and copies ran while one was open for 3% -> 4% of each run, Pallas kernels for 32% -> 31%
where the time goes in v8:
time: 77.2 us; the launch traced here: 76.8 us
  Pallas kernels  29.3 us (38%)
  starting transfers between devices  22.1 us (29%)
  waiting for transfers between devices  18.7 us (24%)
  local copies, waits for them, and re-layouts  5.18 us (7%)
  between operations  1.46 us (2%)
    pallas_call x6, Pallas kernels, call(): pl.pallas_call(kernel, out_shape=[jax.ShapeDtypeStruct(shape, F32) for sh...  26.3 us
    ppermute x6, starting transfers between devices, spread(): return lax.ppermute(array, ('space', 'node', 'tm'), pairs)  16.4 us
    ppermute x3, waiting for transfers between devices, across(): lax.ppermute(array, 'node', [(node, node ^ 2) for node in range(NODES)])  12.8 us
    ppermute x3, starting transfers between devices, across(): lax.ppermute(array, 'node', [(node, node ^ 2) for node in range(NODES)])  4.92 us
    ppermute x4, waiting for transfers between devices, beside(): lax.ppermute(array, 'node', [(node, node ^ 1) for node in range(NODES)])  4.48 us
    pallas_call x2, Pallas kernels, placed(): pl.pallas_call(kernel, out_shape=[jax.ShapeDtypeStruct(shape, F32)] * 2,...  3.06 us
    unnamed x8, local copies, waits for them, and re-layouts  2.03 us
    dynamic_slice x1, local copies, waits for them, and re-layouts, on_device(): lax.dynamic_slice_in_dim(start, HALF * (1 - lax.rem(node_index, 2)), HALF...  1.87 us
  transfers between devices with their start and end apart: 13, of which 7 were waited for; matrix products, arithmetic and copies ran while one was open for 4% of the time, Pallas kernels for 31%

profile of v8, /device:TPU:0, one launch (start us, length us, event | category | flops | bytes accessed | tf_op | source)
XLA Modules:
  0.0 76.8 jit_solution(9555605442993209667)
XLA Ops:
  1.1 2.6 %collective-permute-start.3 = (f32[8,128,256]{2,1,0:T(8,128)}, f32[8,128,256]{2,1,0:T(8,128)}, u32[]{:S(2)}, u32[]{:S(2)}) collective-permute-start(f32[8,128,256]{2,1,0:T(8,128)} %bitcast.11), channel_id=1, source_target_pairs={{0,4},{2,6},{4,0},{6,2},{1,5},{3,7},{5,1},{7,3},{8,12},{10,14},{12... | collective-permute-start | bytes 3145736 | tf_op jit(solution)/shard_map/ppermute | solution.py:371
  4.4 1.2 %copy-done = f32[1,1,8,128,256]{4,3,2,1,0:T(8,128)S(1)} copy-done((f32[1,1,8,128,256]{4,3,2,1,0:T(8,128)S(1)}, f32[1,1,8,128,256]{4,3,2,1,0:T(8,128)}, u32[]{:S(2)}) %copy-start) | copy-done | bytes 1048600
  5.7 1.5 %shard_map.50 = (f32[6,128,256]{2,1,0:T(8,128)}, f32[4,128,256]{2,1,0:T(8,128)S(1)}) custom-call(f32[46]{0:T(128)S(1)} %constant_dynamic-update-slice_fusion.scalars, f32[8,128,256]{2,1,0:T(8,128)S(1)} %bitcast.12, f32[8,128,256]{2,1,0:T(8,128)S(1)} %collective-permute-done.4.beside), custom_call_target="tpu_custom_call" | custom-call | flops 1000 | bytes 1000 | tf_op jit(solution)/shard_map/pallas_call | solution.py:344
  8.0 2.2 %collective-permute-start.6 = (f32[6,128,256]{2,1,0:T(8,128)}, f32[6,128,256]{2,1,0:T(8,128)}, u32[]{:S(2)}, u32[]{:S(2)}) collective-permute-start(f32[6,128,256]{2,1,0:T(8,128)} %get-tuple-element.32), channel_id=1, source_target_pairs={{0,8},{1,9},{2,26},{3,27},{4,12},{5,13},{6,30},{7,31},{8,16},{9,17... | collective-permute-start | bytes 2359304 | tf_op jit(solution)/shard_map/ppermute | solution.py:389
  10.1 1.9 %dynamic-slice_bitcast_fusion = f32[4,128,256]{2,1,0:T(8,128)} fusion(f32[1,8,128,256]{3,2,1,0:T(8,128)} %param.7, s32[]{:T(128)S(6)} %select_n.7), kind=kLoop, calls=%fused_computation | loop fusion | bytes 1048580 | tf_op jit(solution)/shard_map/dynamic_slice | solution.py:401
  12.0 4.2 %collective-permute-start.1 = (f32[4,128,256]{2,1,0:T(8,128)}, f32[4,128,256]{2,1,0:T(8,128)}, u32[]{:S(2)}, u32[]{:S(2)}) collective-permute-start(f32[4,128,256]{2,1,0:T(8,128)} %dynamic-slice_bitcast_fusion), channel_id=1, source_target_pairs={{0,1},{2,3},{4,5},{6,7},{8,9},{10,11},{12,13},{14,15},{16,17},{18,... | collective-permute-start | bytes 1572872 | tf_op jit(solution)/shard_map/ppermute | solution.py:389
  16.2 1.6 %collective-permute-start.8 = (f32[4,128,256]{2,1,0:T(8,128)}, f32[4,128,256]{2,1,0:T(8,128)}, u32[]{:S(2)}, u32[]{:S(2)}) collective-permute-start(f32[4,128,256]{2,1,0:T(8,128)} %copy-done.3), channel_id=1, source_target_pairs={{0,8},{1,9},{2,26},{3,27},{4,12},{5,13},{6,30},{7,31},{8,16},{9,17... | collective-permute-start | bytes 1572872 | tf_op jit(solution)/shard_map/ppermute | solution.py:389
  18.9 8.9 %collective-permute-done.3.across = f32[8,128,256]{2,1,0:T(8,128)} collective-permute-done((f32[8,128,256]{2,1,0:T(8,128)}, f32[8,128,256]{2,1,0:T(8,128)}, u32[]{:S(2)}, u32[]{:S(2)}) %collective-permute-start.3) | collective-permute-done | bytes 1048608 | tf_op jit(solution)/shard_map/ppermute | solution.py:371
  27.8 3.0 %conditional.1 = (f32[8,128,256]{2,1,0:T(8,128)}) conditional(s32[]{:T(128)} %bitcast.5, f32[8,128,256]{2,1,0:T(8,128)} %collective-permute-done.3.across, f32[8,128,256]{2,1,0:T(8,128)} %collective-permute-done.3.across), branch_computations={%region_0.0_spmd, %region_1.0_spmd} | conditional | bytes 4194352 | solution.py:379
  27.8 3.0 %collective-permute-done = f32[8,128,256]{2,1,0:T(8,128)} collective-permute-done((f32[8,128,256]{2,1,0:T(8,128)}, f32[8,128,256]{2,1,0:T(8,128)}, u32[]{:S(2)}, u32[]{:S(2)}) %collective-permute-start) | collective-permute-done | bytes 1048608 | tf_op jit(solution)/shard_map/cond/branch_1_fun/ppermute | solution.py:374
  30.8 1.8 %collective-permute-start.7 = (f32[6,128,256]{2,1,0:T(8,128)}, f32[6,128,256]{2,1,0:T(8,128)S(1)}, u32[]{:S(2)}, u32[]{:S(2)}) collective-permute-start(f32[6,128,256]{2,1,0:T(8,128)} %collective-permute-done.6.halo_a), channel_id=1, source_target_pairs={{0,4},{2,6},{4,0},{6,2},{1,5},{3,7},{5,1},{7,3},{8,12},{10,14},{12... | collective-permute-start | bytes 2359304 | tf_op jit(solution)/shard_map/ppermute | solution.py:371
  32.6 2.4 %shard_map.51 = f32[5,128,256]{2,1,0:T(8,128)S(1)} custom-call(f32[46]{0:T(128)S(1)} %constant_dynamic-update-slice_fusion.scalars, f32[8,128,256]{2,1,0:T(8,128)S(1)} %bitcast.13, f32[8,128,256]{2,1,0:T(8,128)} %collective-permute-done.3.across, f32[8,128,256]{2,1,0:T(8,128)S(1)} %collective-permute-done.4.beside, f32[8,128,256]{2,1,0:T(8,128)} %get-tuple-element.45.corner, ...), custom_call_target="tpu_custom_call" | custom-call | flops 1000 | bytes 1000 | tf_op jit(solution)/shard_map/pallas_call | solution.py:344
  34.9 3.5 %collective-permute-start.5 = (f32[5,128,256]{2,1,0:T(8,128)S(1)}, f32[5,128,256]{2,1,0:T(8,128)S(1)}, u32[]{:S(2)}, u32[]{:S(2)}) collective-permute-start(f32[5,128,256]{2,1,0:T(8,128)S(1)} %shard_map.51), channel_id=1, source_target_pairs={{0,1},{2,3},{4,5},{6,7},{8,9},{10,11},{12,13},{14,15},{16,17},{18,... | collective-permute-start | bytes 1966088 | tf_op jit(solution)/shard_map/ppermute | solution.py:389
  38.4 7.3 %shard_map.52.kept = f32[4,9,128,256]{3,2,1,0:T(8,128)S(1)} custom-call(f32[46]{0:T(128)S(1)} %constant_dynamic-update-slice_fusion.scalars, f32[8,128,256]{2,1,0:T(8,128)S(1)} %bitcast.14, f32[8,128,256]{2,1,0:T(8,128)} %collective-permute-done.3.across, f32[8,128,256]{2,1,0:T(8,128)S(1)} %collective-permute-done.4.beside, ...), custom_call_target="tpu_custom_call" | custom-call | flops 1000 | bytes 1000 | tf_op jit(solution)/shard_map/pallas_call | solution.py:344
  46.3 3.5 %collective-permute-start.11 = (f32[5,128,256]{2,1,0:T(8,128)S(1)}, f32[5,128,256]{2,1,0:T(8,128)S(1)}, u32[]{:S(2)}, u32[]{:S(2)}) collective-permute-start(f32[5,128,256]{2,1,0:T(8,128)S(1)} %shard_map.51), channel_id=1, source_target_pairs={{0,27},{2,9},{4,31},{6,13},{8,3},{10,17},{12,7},{14,21},{16,11},{1... | collective-permute-start | bytes 1966088 | tf_op jit(solution)/shard_map/ppermute | solution.py:389
  49.8 1.5 %collective-permute-start.2 = (f32[4,128,256]{2,1,0:T(8,128)}, f32[4,128,256]{2,1,0:T(8,128)S(1)}, u32[]{:S(2)}, u32[]{:S(2)}) collective-permute-start(f32[4,128,256]{2,1,0:T(8,128)} %collective-permute-done.1), channel_id=1, source_target_pairs={{1,8},{3,26},{5,12},{7,30},{9,16},{11,2},{13,20},{15,6},{17,24},{1... | collective-permute-start | bytes 1572872 | tf_op jit(solution)/shard_map/ppermute | solution.py:389
  51.4 6.6 %shard_map.53.kept = f32[4,12,128,256]{3,2,1,0:T(8,128)S(1)} custom-call(f32[46]{0:T(128)S(1)} %constant_dynamic-update-slice_fusion.scalars, f32[8,128,256]{2,1,0:T(8,128)S(1)} %bitcast.15, f32[8,128,256]{2,1,0:T(8,128)} %collective-permute-done.3.across, f32[8,128,256]{2,1,0:T(8,128)S(1)} %collective-permute-done.4.beside, ...), custom_call_target="tpu_custom_call" | custom-call | flops 1000 | bytes 1000 | tf_op jit(solution)/shard_map/pallas_call | solution.py:344
  58.0 3.8 %collective-permute-done.9.across_b = f32[4,128,256]{2,1,0:T(8,128)S(1)} collective-permute-done((f32[4,128,256]{2,1,0:T(8,128)}, f32[4,128,256]{2,1,0:T(8,128)S(1)}, u32[]{:S(2)}, u32[]{:S(2)}) %collective-permute-start.9) | collective-permute-done | bytes 524320 | tf_op jit(solution)/shard_map/ppermute | solution.py:371
  61.8 4.7 %shard_map.54.part = f32[4,2,128,256]{3,2,1,0:T(8,128)S(1)} custom-call(f32[46]{0:T(128)S(1)} %constant_dynamic-update-slice_fusion.scalars, f32[6,128,256]{2,1,0:T(8,128)} %collective-permute-done.6.halo_a, f32[6,128,256]{2,1,0:T(8,128)S(1)} %collective-permute-done.7.across_a, f32[4,128,256]{2,1,0:T(8,128)} %collective-permute-done.8.halo_b, ...), custom_call_target="tpu_custom_call" | custom-call | flops 1000 | bytes 1000 | tf_op jit(solution)/shard_map/pallas_call | solution.py:344
  66.6 1.5 %collective-permute-done.2.halo_start = f32[4,128,256]{2,1,0:T(8,128)S(1)} collective-permute-done((f32[4,128,256]{2,1,0:T(8,128)}, f32[4,128,256]{2,1,0:T(8,128)S(1)}, u32[]{:S(2)}, u32[]{:S(2)}) %collective-permute-start.2) | collective-permute-done | bytes 524320 | tf_op jit(solution)/shard_map/ppermute | solution.py:389
  68.3 3.8 %shard_map.55 = (f32[4,128,256]{2,1,0:T(8,128)S(1)}, f32[9,128,256]{2,1,0:T(8,128)S(1)}) custom-call(f32[46]{0:T(128)S(1)} %constant_dynamic-update-slice_fusion.scalars, f32[8,128,256]{2,1,0:T(8,128)S(1)} %bitcast.17, f32[4,128,256]{2,1,0:T(8,128)S(1)} %collective-permute-done.2.halo_start, f32[5,128,256]{2,1,0:T(8,128)S(1)} %collective-permute-done.5.near, ...), custom_call_target="tpu_custom_call" | custom-call | flops 1000 | bytes 1000 | tf_op jit(solution)/shard_map/pallas_call | solution.py:344
  72.3 1.5 %shard_map.56 = (f32[8,128,256]{2,1,0:T(8,128)}, f32[8,128,256]{2,1,0:T(8,128)}) custom-call(f32[46]{0:T(128)S(1)} %constant_dynamic-update-slice_fusion.scalars, f32[4,128,256]{2,1,0:T(8,128)S(1)} %get-tuple-element.40.mine, f32[9,128,256]{2,1,0:T(8,128)S(1)} %get-tuple-element.39.swap), custom_call_target="tpu_custom_call" | custom-call | flops 1000 | bytes 1000 | tf_op jit(solution)/shard_map/pallas_call | solution.py:328
  73.8 1.2 %collective-permute-done.12.other = f32[9,128,256]{2,1,0:T(8,128)S(1)} collective-permute-done((f32[9,128,256]{2,1,0:T(8,128)S(1)}, f32[9,128,256]{2,1,0:T(8,128)S(1)}, u32[]{:S(2)}, u32[]{:S(2)}) %collective-permute-start.12) | collective-permute-done | bytes 1179680 | tf_op jit(solution)/shard_map/ppermute | solution.py:374
  75.1 1.6 %shard_map.57 = (f32[8,128,256]{2,1,0:T(8,128)}, f32[8,128,256]{2,1,0:T(8,128)}) custom-call(f32[46]{0:T(128)S(1)} %constant_dynamic-update-slice_fusion.scalars, f32[9,128,256]{2,1,0:T(8,128)S(1)} %get-tuple-element.39.swap, f32[9,128,256]{2,1,0:T(8,128)S(1)} %collective-permute-done.12.other, ...), custom_call_target="tpu_custom_call", output_to_operand_aliasing={{0}: (3, {}), {1}: (4, {})} | custom-call | flops 1000 | bytes 1000 | tf_op jit(solution)/shard_map/pallas_call | solution.py:328
  (24 shorter events, 3.8 us)
Async XLA Ops:
  0.6 3.8 %collective-permute-start.4 = (f32[8,128,256]{2,1,0:T(8,128)}, f32[8,128,256]{2,1,0:T(8,128)S(1)}, u32[]{:S(2)}, u32[]{:S(2)}) collective-permute-start(f32[8,128,256]{2,1,0:T(8,128)} %bitcast.10), channel_id=1, source_target_pairs={{0,2},{2,0},{4,6},{6,4},{1,3},{3,1},{5,7},{7,5},{8,10},{10,8},{12,... | collective-permute-start | bytes 3145736 | tf_op jit(solution)/shard_map/ppermute | solution.py:374
  1.1 26.6 %collective-permute-start.3 = (f32[8,128,256]{2,1,0:T(8,128)}, f32[8,128,256]{2,1,0:T(8,128)}, u32[]{:S(2)}, u32[]{:S(2)}) collective-permute-start(f32[8,128,256]{2,1,0:T(8,128)} %bitcast.11), channel_id=1, source_target_pairs={{0,4},{2,6},{4,0},{6,2},{1,5},{3,7},{5,1},{7,3},{8,12},{10,14},{12... | collective-permute-start | bytes 3145736 | tf_op jit(solution)/shard_map/ppermute | solution.py:371
  4.4 1.2 %copy-start = (f32[1,1,8,128,256]{4,3,2,1,0:T(8,128)S(1)}, f32[1,1,8,128,256]{4,3,2,1,0:T(8,128)}, u32[]{:S(2)}) copy-start(f32[1,1,8,128,256]{4,3,2,1,0:T(8,128)} %param.8) | copy-start | bytes 3145732
  5.6 26.9 %copy-start.1 = (f32[1,1,8,128,256]{4,3,2,1,0:T(8,128)S(1)}, f32[1,1,8,128,256]{4,3,2,1,0:T(8,128)}, u32[]{:S(2)}) copy-start(f32[1,1,8,128,256]{4,3,2,1,0:T(8,128)} %param.8) | copy-start | bytes 3145732
  5.7 26.9 %copy-start.2 = (f32[1,8,128,256]{3,2,1,0:T(8,128)S(1)}, f32[1,8,128,256]{3,2,1,0:T(8,128)}, u32[]{:S(2)}) copy-start(f32[1,8,128,256]{3,2,1,0:T(8,128)} %param.7) | copy-start | bytes 3145732
  7.2 0.8 %copy-start.3 = (f32[4,128,256]{2,1,0:T(8,128)}, f32[4,128,256]{2,1,0:T(8,128)S(1)}, u32[]{:S(2)}) copy-start(f32[4,128,256]{2,1,0:T(8,128)S(1)} %get-tuple-element.36) | copy-start | bytes 1572868
  8.0 22.8 %collective-permute-start.6 = (f32[6,128,256]{2,1,0:T(8,128)}, f32[6,128,256]{2,1,0:T(8,128)}, u32[]{:S(2)}, u32[]{:S(2)}) collective-permute-start(f32[6,128,256]{2,1,0:T(8,128)} %get-tuple-element.32), channel_id=1, source_target_pairs={{0,8},{1,9},{2,26},{3,27},{4,12},{5,13},{6,30},{7,31},{8,16},{9,17... | collective-permute-start | bytes 2359304 | tf_op jit(solution)/shard_map/ppermute | solution.py:389
  12.0 20.5 %collective-permute-start.1 = (f32[4,128,256]{2,1,0:T(8,128)}, f32[4,128,256]{2,1,0:T(8,128)}, u32[]{:S(2)}, u32[]{:S(2)}) collective-permute-start(f32[4,128,256]{2,1,0:T(8,128)} %dynamic-slice_bitcast_fusion), channel_id=1, source_target_pairs={{0,1},{2,3},{4,5},{6,7},{8,9},{10,11},{12,13},{14,15},{16,17},{18,... | collective-permute-start | bytes 1572872 | tf_op jit(solution)/shard_map/ppermute | solution.py:389
  16.2 29.5 %collective-permute-start.8 = (f32[4,128,256]{2,1,0:T(8,128)}, f32[4,128,256]{2,1,0:T(8,128)}, u32[]{:S(2)}, u32[]{:S(2)}) collective-permute-start(f32[4,128,256]{2,1,0:T(8,128)} %copy-done.3), channel_id=1, source_target_pairs={{0,8},{1,9},{2,26},{3,27},{4,12},{5,13},{6,30},{7,31},{8,16},{9,17... | collective-permute-start | bytes 1572872 | tf_op jit(solution)/shard_map/ppermute | solution.py:389
  27.8 3.0 %collective-permute-start = (f32[8,128,256]{2,1,0:T(8,128)}, f32[8,128,256]{2,1,0:T(8,128)}, u32[]{:S(2)}, u32[]{:S(2)}) collective-permute-start(f32[8,128,256]{2,1,0:T(8,128)} %param.3), channel_id=1, source_target_pairs={{0,2},{2,0},{4,6},{6,4},{1,3},{3,1},{5,7},{7,5},{8,10},{10,8},{12,... | collective-permute-start | bytes 3145736 | tf_op jit(solution)/shard_map/cond/branch_1_fun/ppermute | solution.py:374
  30.8 20.6 %collective-permute-start.7 = (f32[6,128,256]{2,1,0:T(8,128)}, f32[6,128,256]{2,1,0:T(8,128)S(1)}, u32[]{:S(2)}, u32[]{:S(2)}) collective-permute-start(f32[6,128,256]{2,1,0:T(8,128)} %collective-permute-done.6.halo_a), channel_id=1, source_target_pairs={{0,4},{2,6},{4,0},{6,2},{1,5},{3,7},{5,1},{7,3},{8,12},{10,14},{12... | collective-permute-start | bytes 2359304 | tf_op jit(solution)/shard_map/ppermute | solution.py:371
  34.9 31.6 %collective-permute-start.5 = (f32[5,128,256]{2,1,0:T(8,128)S(1)}, f32[5,128,256]{2,1,0:T(8,128)S(1)}, u32[]{:S(2)}, u32[]{:S(2)}) collective-permute-start(f32[5,128,256]{2,1,0:T(8,128)S(1)} %shard_map.51), channel_id=1, source_target_pairs={{0,1},{2,3},{4,5},{6,7},{8,9},{10,11},{12,13},{14,15},{16,17},{18,... | collective-permute-start | bytes 1966088 | tf_op jit(solution)/shard_map/ppermute | solution.py:389
  45.7 16.1 %collective-permute-start.9 = (f32[4,128,256]{2,1,0:T(8,128)}, f32[4,128,256]{2,1,0:T(8,128)S(1)}, u32[]{:S(2)}, u32[]{:S(2)}) collective-permute-start(f32[4,128,256]{2,1,0:T(8,128)} %collective-permute-done.8.halo_b), channel_id=1, source_target_pairs={{0,4},{2,6},{4,0},{6,2},{1,5},{3,7},{5,1},{7,3},{8,12},{10,14},{12... | collective-permute-start | bytes 1572872 | tf_op jit(solution)/shard_map/ppermute | solution.py:371
  46.3 21.7 %collective-permute-start.11 = (f32[5,128,256]{2,1,0:T(8,128)S(1)}, f32[5,128,256]{2,1,0:T(8,128)S(1)}, u32[]{:S(2)}, u32[]{:S(2)}) collective-permute-start(f32[5,128,256]{2,1,0:T(8,128)S(1)} %shard_map.51), channel_id=1, source_target_pairs={{0,27},{2,9},{4,31},{6,13},{8,3},{10,17},{12,7},{14,21},{16,11},{1... | collective-permute-start | bytes 1966088 | tf_op jit(solution)/shard_map/ppermute | solution.py:389
  49.8 18.2 %collective-permute-start.2 = (f32[4,128,256]{2,1,0:T(8,128)}, f32[4,128,256]{2,1,0:T(8,128)S(1)}, u32[]{:S(2)}, u32[]{:S(2)}) collective-permute-start(f32[4,128,256]{2,1,0:T(8,128)} %collective-permute-done.1), channel_id=1, source_target_pairs={{1,8},{3,26},{5,12},{7,30},{9,16},{11,2},{13,20},{15,6},{17,24},{1... | collective-permute-start | bytes 1572872 | tf_op jit(solution)/shard_map/ppermute | solution.py:389
  66.5 1.8 %collective-permute-start.10 = (f32[3,128,256]{2,1,0:T(8,128)S(1)}, f32[3,128,256]{2,1,0:T(8,128)S(1)}, u32[]{:S(2)}, u32[]{:S(2)}) collective-permute-start(f32[3,128,256]{2,1,0:T(8,128)S(1)} %slice.16), channel_id=1, source_target_pairs={{0,2},{2,0},{4,6},{6,4},{1,3},{3,1},{5,7},{7,5},{8,10},{10,8},{12,... | collective-permute-start | bytes 1179656 | tf_op jit(solution)/shard_map/ppermute | solution.py:374
  72.1 2.9 %collective-permute-start.12 = (f32[9,128,256]{2,1,0:T(8,128)S(1)}, f32[9,128,256]{2,1,0:T(8,128)S(1)}, u32[]{:S(2)}, u32[]{:S(2)}) collective-permute-start(f32[9,128,256]{2,1,0:T(8,128)S(1)} %get-tuple-element.39.swap), channel_id=1, source_target_pairs={{0,2},{2,0},{4,6},{6,4},{1,3},{3,1},{5,7},{7,5},{8,10},{10,8},{12,... | collective-permute-start | bytes 3538952 | tf_op jit(solution)/shard_map/ppermute | solution.py:374

commit v9 on v5

--- a/solution.py
+++ b/solution.py
@@ -124,16 +124,20 @@
             halo_b[index + 2 * number] = source[plane(8 + index)]
 
 
-def end_kernel(scalars, own, across, beside, corner, start, out, total):
+def end_kernel(scalars, own, across, beside, corner_far, start, out, total, corner, sem):
     plane = counter(scalars)
     sources = (own, across, beside, corner)
     weighted = [Plane(total, index) for index in range(HALF + 2)]
+    fetch = pltpu.make_async_copy(corner_far, corner, sem.at[0])
+    fetch.start()
 
     def states(place, first):
         return [Plane(source, plane(place)).rows(first, 32) for source in sources]
 
     for first in chunks(weighted[0], 32):
         weighted[0].put(first, jnp.zeros_like(weighted[0].rows(first, 32)))
+    fetch.wait()
+    for first in chunks(weighted[0], 32):
         for index in range(1, HALF + 2):
             value = mixed(scalars, WEIGHT, states(index + 4, first))
             weighted[index].put(first, value)
@@ -297,13 +301,15 @@
         end[far] = others
 
 
-def call(kernel, scalars, operands, outs, scratch, limit):
+def call(kernel, scalars, operands, outs, scratch, limit, far=None, sems=()):
     return pl.pallas_call(
         kernel,
         out_shape=[jax.ShapeDtypeStruct(shape, F32) for shape in outs],
-        in_specs=[pl.BlockSpec(memory_space=pltpu.SMEM)] + [pl.BlockSpec(memory_space=pltpu.VMEM)] * len(operands),
+        in_specs=[pl.BlockSpec(memory_space=pltpu.SMEM)] + [
+            pl.BlockSpec(memory_space=pl.ANY if index == far else pltpu.VMEM) for index in range(len(operands))
+        ],
         out_specs=[pl.BlockSpec(memory_space=pltpu.VMEM)] * len(outs),
-        scratch_shapes=[pltpu.VMEM(shape, F32) for shape in scratch],
+        scratch_shapes=[pltpu.VMEM(shape, F32) for shape in scratch] + list(sems),
         compiler_params=pltpu.CompilerParams(vmem_limit_bytes=limit << 20),
         cost_estimate=pl.CostEstimate(flops=1000, bytes_accessed=1000, transcendentals=0),
     )(scalars, *operands)
@@ -358,7 +364,8 @@
     first_start = lax.dynamic_slice_in_dim(start, HALF * (1 - lax.rem(node_index, 2)), HALF, axis=0)
     passing_start = spread(first_start, [(0, 1)], (0, 0))
     (send_end,) = call(
-        end_kernel, scalars, [*sources, after(start, passing_start)], [planes(5)], [planes(HALF + 2)], 16
+        end_kernel, scalars, [*sources, after(start, passing_start)], [planes(5)], [planes(HALF + 2), planes(slab)], 16, 3,
+        [pltpu.SemaphoreType.DMA((1,))],
     )
     near = spread(send_end, onward, (0, 0))
     away = spread(send_end, onward, (-1, 1), 1)

time: 77.3 us -> 78.2 us (1.012)
  Pallas kernels: 28.2 us -> 29.1 us
    ppermute x6, waiting for transfers between devices: 1.47 us -> 2.39 us  [spread(): return lax.ppermute(array, ('space', 'node', 'tm'), pairs)]
    ppermute x3, waiting for transfers between devices: 13.5 us -> 12.6 us  [across(): lax.ppermute(array, 'node', [(node, node ^ 2) for node in range(NODES)])]
    pallas_call x7, Pallas kernels: 28.2 us -> 29.1 us  [call(): pl.pallas_call(kernel, out_shape=[jax.ShapeDtypeStruct(shape, F32) for sh...]
  transfers between devices with their start and end apart: 13 -> 13, of which waited for: 7 -> 7; matrix products, arithmetic and copies ran while one was open for 3% -> 3% of each run, Pallas kernels for 29% -> 30%
where the time goes in v9:
time: 78.2 us; the launch traced here: 77.8 us
  Pallas kernels  29.1 us (37%)
  starting transfers between devices  22.2 us (28%)
  waiting for transfers between devices  20.8 us (27%)
  local copies, waits for them, and re-layouts  4.25 us (5%)
  between operations  1.38 us (2%)
    pallas_call x7, Pallas kernels, call(): pl.pallas_call(kernel, out_shape=[jax.ShapeDtypeStruct(shape, F32) for sh...  29.1 us
    ppermute x6, starting transfers between devices, spread(): return lax.ppermute(array, ('space', 'node', 'tm'), pairs)  16.5 us
    ppermute x3, waiting for transfers between devices, across(): lax.ppermute(array, 'node', [(node, node ^ 2) for node in range(NODES)])  12.6 us
    ppermute x4, waiting for transfers between devices, beside(): lax.ppermute(array, 'node', [(node, node ^ 1) for node in range(NODES)])  5.86 us
    ppermute x3, starting transfers between devices, across(): lax.ppermute(array, 'node', [(node, node ^ 2) for node in range(NODES)])  4.92 us
    ppermute x6, waiting for transfers between devices, spread(): return lax.ppermute(array, ('space', 'node', 'tm'), pairs)  2.39 us
    unnamed x8, local copies, waits for them, and re-layouts  2.04 us
  transfers between devices with their start and end apart: 13, of which 7 were waited for; matrix products, arithmetic and copies ran while one was open for 3% of the time, Pallas kernels for 30%

profile of v9, /device:TPU:0, one launch (start us, length us, event | category | flops | bytes accessed | tf_op | source)
XLA Modules:
  0.0 77.8 jit_solution(14411985004999544965)
XLA Ops:
  1.1 2.6 %collective-permute-start.3 = (f32[8,128,256]{2,1,0:T(8,128)}, f32[8,128,256]{2,1,0:T(8,128)}, u32[]{:S(2)}, u32[]{:S(2)}) collective-permute-start(f32[8,128,256]{2,1,0:T(8,128)} %bitcast.11), channel_id=1, source_target_pairs={{0,4},{2,6},{4,0},{6,2},{1,5},{3,7},{5,1},{7,3},{8,12},{10,14},{12... | collective-permute-start | bytes 3145736 | tf_op jit(solution)/shard_map/ppermute | solution.py:334
  4.4 1.2 %copy-done = f32[1,1,8,128,256]{4,3,2,1,0:T(8,128)S(1)} copy-done((f32[1,1,8,128,256]{4,3,2,1,0:T(8,128)S(1)}, f32[1,1,8,128,256]{4,3,2,1,0:T(8,128)}, u32[]{:S(2)}) %copy-start) | copy-done | bytes 1048600
  5.7 1.5 %shard_map.50 = (f32[6,128,256]{2,1,0:T(8,128)}, f32[4,128,256]{2,1,0:T(8,128)S(1)}) custom-call(f32[46]{0:T(128)S(1)} %constant_dynamic-update-slice_fusion.scalars, f32[8,128,256]{2,1,0:T(8,128)S(1)} %bitcast.12, f32[8,128,256]{2,1,0:T(8,128)S(1)} %collective-permute-done.4.beside), custom_call_target="tpu_custom_call" | custom-call | flops 1000 | bytes 1000 | tf_op jit(solution)/shard_map/pallas_call | solution.py:305
  7.2 0.8 %copy-done.3 = f32[4,128,256]{2,1,0:T(8,128)} copy-done((f32[4,128,256]{2,1,0:T(8,128)}, f32[4,128,256]{2,1,0:T(8,128)S(1)}, u32[]{:S(2)}) %copy-start.3) | copy-done | bytes 524312
  8.0 2.2 %collective-permute-start.6 = (f32[6,128,256]{2,1,0:T(8,128)}, f32[6,128,256]{2,1,0:T(8,128)}, u32[]{:S(2)}, u32[]{:S(2)}) collective-permute-start(f32[6,128,256]{2,1,0:T(8,128)} %get-tuple-element.30), channel_id=1, source_target_pairs={{0,8},{1,9},{2,26},{3,27},{4,12},{5,13},{6,30},{7,31},{8,16},{9,17... | collective-permute-start | bytes 2359304 | tf_op jit(solution)/shard_map/ppermute | solution.py:352
  10.2 0.8 %dynamic-slice_bitcast_fusion = f32[4,128,256]{2,1,0:T(8,128)} fusion(f32[1,8,128,256]{3,2,1,0:T(8,128)S(1)} %copy-done.2, s32[]{:T(128)S(6)} %select_n.7), kind=kLoop, calls=%fused_computation | loop fusion | bytes 1048580 | tf_op jit(solution)/shard_map/dynamic_slice | solution.py:364
  11.0 4.3 %collective-permute-start.1 = (f32[4,128,256]{2,1,0:T(8,128)}, f32[4,128,256]{2,1,0:T(8,128)}, u32[]{:S(2)}, u32[]{:S(2)}) collective-permute-start(f32[4,128,256]{2,1,0:T(8,128)} %dynamic-slice_bitcast_fusion), channel_id=1, source_target_pairs={{0,1},{2,3},{4,5},{6,7},{8,9},{10,11},{12,13},{14,15},{16,17},{18,... | collective-permute-start | bytes 1572872 | tf_op jit(solution)/shard_map/ppermute | solution.py:352
  15.3 1.6 %collective-permute-start.8 = (f32[4,128,256]{2,1,0:T(8,128)}, f32[4,128,256]{2,1,0:T(8,128)}, u32[]{:S(2)}, u32[]{:S(2)}) collective-permute-start(f32[4,128,256]{2,1,0:T(8,128)} %copy-done.3), channel_id=1, source_target_pairs={{0,8},{1,9},{2,26},{3,27},{4,12},{5,13},{6,30},{7,31},{8,16},{9,17... | collective-permute-start | bytes 1572872 | tf_op jit(solution)/shard_map/ppermute | solution.py:352
  18.2 9.6 %collective-permute-done.3.across = f32[8,128,256]{2,1,0:T(8,128)} collective-permute-done((f32[8,128,256]{2,1,0:T(8,128)}, f32[8,128,256]{2,1,0:T(8,128)}, u32[]{:S(2)}, u32[]{:S(2)}) %collective-permute-start.3) | collective-permute-done | bytes 1048608 | tf_op jit(solution)/shard_map/ppermute | solution.py:334
  27.8 3.0 %conditional.1 = (f32[8,128,256]{2,1,0:T(8,128)}) conditional(s32[]{:T(128)} %bitcast.5, f32[8,128,256]{2,1,0:T(8,128)} %collective-permute-done.3.across, f32[8,128,256]{2,1,0:T(8,128)} %collective-permute-done.3.across), branch_computations={%region_0.0_spmd, %region_1.0_spmd} | conditional | bytes 4194352 | solution.py:342
  27.8 3.0 %collective-permute-done = f32[8,128,256]{2,1,0:T(8,128)} collective-permute-done((f32[8,128,256]{2,1,0:T(8,128)}, f32[8,128,256]{2,1,0:T(8,128)}, u32[]{:S(2)}, u32[]{:S(2)}) %collective-permute-start) | collective-permute-done | bytes 1048608 | tf_op jit(solution)/shard_map/cond/branch_1_fun/ppermute | solution.py:337
  30.8 1.8 %collective-permute-start.7 = (f32[6,128,256]{2,1,0:T(8,128)}, f32[6,128,256]{2,1,0:T(8,128)S(1)}, u32[]{:S(2)}, u32[]{:S(2)}) collective-permute-start(f32[6,128,256]{2,1,0:T(8,128)} %collective-permute-done.6.halo_a), channel_id=1, source_target_pairs={{0,4},{2,6},{4,0},{6,2},{1,5},{3,7},{5,1},{7,3},{8,12},{10,14},{12... | collective-permute-start | bytes 2359304 | tf_op jit(solution)/shard_map/ppermute | solution.py:334
  32.6 3.3 %shard_map.51 = f32[5,128,256]{2,1,0:T(8,128)S(1)} custom-call(f32[46]{0:T(128)S(1)} %constant_dynamic-update-slice_fusion.scalars, f32[8,128,256]{2,1,0:T(8,128)S(1)} %bitcast.13, f32[8,128,256]{2,1,0:T(8,128)} %collective-permute-done.3.across, f32[8,128,256]{2,1,0:T(8,128)S(1)} %collective-permute-done.4.beside, ...), custom_call_target="tpu_custom_call" | custom-call | flops 1000 | bytes 1000 | tf_op jit(solution)/shard_map/pallas_call | solution.py:305
  35.8 3.5 %collective-permute-start.5 = (f32[5,128,256]{2,1,0:T(8,128)S(1)}, f32[5,128,256]{2,1,0:T(8,128)S(1)}, u32[]{:S(2)}, u32[]{:S(2)}) collective-permute-start(f32[5,128,256]{2,1,0:T(8,128)S(1)} %shard_map.51), channel_id=1, source_target_pairs={{0,1},{2,3},{4,5},{6,7},{8,9},{10,11},{12,13},{14,15},{16,17},{18,... | collective-permute-start | bytes 1966088 | tf_op jit(solution)/shard_map/ppermute | solution.py:352
  39.3 7.3 %shard_map.52.kept = f32[4,9,128,256]{3,2,1,0:T(8,128)S(1)} custom-call(f32[46]{0:T(128)S(1)} %constant_dynamic-update-slice_fusion.scalars, f32[8,128,256]{2,1,0:T(8,128)S(1)} %bitcast.14, f32[8,128,256]{2,1,0:T(8,128)} %collective-permute-done.3.across, f32[8,128,256]{2,1,0:T(8,128)S(1)} %collective-permute-done.4.beside, ...), custom_call_target="tpu_custom_call" | custom-call | flops 1000 | bytes 1000 | tf_op jit(solution)/shard_map/pallas_call | solution.py:305
  47.2 3.5 %collective-permute-start.11 = (f32[5,128,256]{2,1,0:T(8,128)S(1)}, f32[5,128,256]{2,1,0:T(8,128)S(1)}, u32[]{:S(2)}, u32[]{:S(2)}) collective-permute-start(f32[5,128,256]{2,1,0:T(8,128)S(1)} %shard_map.51), channel_id=1, source_target_pairs={{0,27},{2,9},{4,31},{6,13},{8,3},{10,17},{12,7},{14,21},{16,11},{1... | collective-permute-start | bytes 1966088 | tf_op jit(solution)/shard_map/ppermute | solution.py:352
  50.7 1.5 %collective-permute-start.2 = (f32[4,128,256]{2,1,0:T(8,128)}, f32[4,128,256]{2,1,0:T(8,128)S(1)}, u32[]{:S(2)}, u32[]{:S(2)}) collective-permute-start(f32[4,128,256]{2,1,0:T(8,128)} %collective-permute-done.1), channel_id=1, source_target_pairs={{1,8},{3,26},{5,12},{7,30},{9,16},{11,2},{13,20},{15,6},{17,24},{1... | collective-permute-start | bytes 1572872 | tf_op jit(solution)/shard_map/ppermute | solution.py:352
  52.2 6.6 %shard_map.53.kept = f32[4,12,128,256]{3,2,1,0:T(8,128)S(1)} custom-call(f32[46]{0:T(128)S(1)} %constant_dynamic-update-slice_fusion.scalars, f32[8,128,256]{2,1,0:T(8,128)S(1)} %bitcast.15, f32[8,128,256]{2,1,0:T(8,128)} %collective-permute-done.3.across, f32[8,128,256]{2,1,0:T(8,128)S(1)} %collective-permute-done.4.beside, ...), custom_call_target="tpu_custom_call" | custom-call | flops 1000 | bytes 1000 | tf_op jit(solution)/shard_map/pallas_call | solution.py:305
  58.9 3.0 %collective-permute-done.9.across_b = f32[4,128,256]{2,1,0:T(8,128)S(1)} collective-permute-done((f32[4,128,256]{2,1,0:T(8,128)}, f32[4,128,256]{2,1,0:T(8,128)S(1)}, u32[]{:S(2)}, u32[]{:S(2)}) %collective-permute-start.9) | collective-permute-done | bytes 524320 | tf_op jit(solution)/shard_map/ppermute | solution.py:334
  61.8 4.7 %shard_map.54.part = f32[4,2,128,256]{3,2,1,0:T(8,128)S(1)} custom-call(f32[46]{0:T(128)S(1)} %constant_dynamic-update-slice_fusion.scalars, f32[6,128,256]{2,1,0:T(8,128)} %collective-permute-done.6.halo_a, f32[6,128,256]{2,1,0:T(8,128)S(1)} %collective-permute-done.7.across_a, f32[4,128,256]{2,1,0:T(8,128)} %collective-permute-done.8.halo_b, ...), custom_call_target="tpu_custom_call" | custom-call | flops 1000 | bytes 1000 | tf_op jit(solution)/shard_map/pallas_call | solution.py:305
  67.4 1.6 %collective-permute-done.2.halo_start = f32[4,128,256]{2,1,0:T(8,128)S(1)} collective-permute-done((f32[4,128,256]{2,1,0:T(8,128)}, f32[4,128,256]{2,1,0:T(8,128)S(1)}, u32[]{:S(2)}, u32[]{:S(2)}) %collective-permute-start.2) | collective-permute-done | bytes 524320 | tf_op jit(solution)/shard_map/ppermute | solution.py:352
  69.1 3.7 %shard_map.55 = (f32[9,128,256]{2,1,0:T(8,128)S(1)}, f32[9,128,256]{2,1,0:T(8,128)S(1)}) custom-call(f32[46]{0:T(128)S(1)} %constant_dynamic-update-slice_fusion.scalars, f32[8,128,256]{2,1,0:T(8,128)S(1)} %bitcast.17, f32[4,128,256]{2,1,0:T(8,128)S(1)} %collective-permute-done.2.halo_start, f32[5,128,256]{2,1,0:T(8,128)S(1)} %collective-permute-done.5.near, ...), custom_call_target="tpu_custom_call" | custom-call | flops 1000 | bytes 1000 | tf_op jit(solution)/shard_map/pallas_call | solution.py:305
  73.0 2.7 %collective-permute-done.12.other = f32[9,128,256]{2,1,0:T(8,128)S(1)} collective-permute-done((f32[9,128,256]{2,1,0:T(8,128)S(1)}, f32[9,128,256]{2,1,0:T(8,128)S(1)}, u32[]{:S(2)}, u32[]{:S(2)}) %collective-permute-start.12) | collective-permute-done | bytes 1179680 | tf_op jit(solution)/shard_map/ppermute | solution.py:337
  75.8 2.0 %shard_map.56 = (f32[8,128,256]{2,1,0:T(8,128)}, f32[8,128,256]{2,1,0:T(8,128)}) custom-call(f32[46]{0:T(128)S(1)} %constant_dynamic-update-slice_fusion.scalars, f32[9,128,256]{2,1,0:T(8,128)S(1)} %get-tuple-element.37.mine, f32[9,128,256]{2,1,0:T(8,128)S(1)} %collective-permute-done.12.other), custom_call_target="tpu_custom_call" | custom-call | flops 1000 | bytes 1000 | tf_op jit(solution)/shard_map/pallas_call | solution.py:305
  (23 shorter events, 3.8 us)
Async XLA Ops:
  0.6 3.8 %collective-permute-start.4 = (f32[8,128,256]{2,1,0:T(8,128)}, f32[8,128,256]{2,1,0:T(8,128)S(1)}, u32[]{:S(2)}, u32[]{:S(2)}) collective-permute-start(f32[8,128,256]{2,1,0:T(8,128)} %bitcast.10), channel_id=1, source_target_pairs={{0,2},{2,0},{4,6},{6,4},{1,3},{3,1},{5,7},{7,5},{8,10},{10,8},{12,... | collective-permute-start | bytes 3145736 | tf_op jit(solution)/shard_map/ppermute | solution.py:337
  1.1 26.6 %collective-permute-start.3 = (f32[8,128,256]{2,1,0:T(8,128)}, f32[8,128,256]{2,1,0:T(8,128)}, u32[]{:S(2)}, u32[]{:S(2)}) collective-permute-start(f32[8,128,256]{2,1,0:T(8,128)} %bitcast.11), channel_id=1, source_target_pairs={{0,4},{2,6},{4,0},{6,2},{1,5},{3,7},{5,1},{7,3},{8,12},{10,14},{12... | collective-permute-start | bytes 3145736 | tf_op jit(solution)/shard_map/ppermute | solution.py:334
  4.4 1.2 %copy-start = (f32[1,1,8,128,256]{4,3,2,1,0:T(8,128)S(1)}, f32[1,1,8,128,256]{4,3,2,1,0:T(8,128)}, u32[]{:S(2)}) copy-start(f32[1,1,8,128,256]{4,3,2,1,0:T(8,128)} %param.8) | copy-start | bytes 3145732
  5.6 4.5 %copy-start.2 = (f32[1,8,128,256]{3,2,1,0:T(8,128)S(1)}, f32[1,8,128,256]{3,2,1,0:T(8,128)}, u32[]{:S(2)}) copy-start(f32[1,8,128,256]{3,2,1,0:T(8,128)} %param.7) | copy-start | bytes 3145732
  7.2 0.8 %copy-start.3 = (f32[4,128,256]{2,1,0:T(8,128)}, f32[4,128,256]{2,1,0:T(8,128)S(1)}, u32[]{:S(2)}) copy-start(f32[4,128,256]{2,1,0:T(8,128)S(1)} %get-tuple-element.34) | copy-start | bytes 1572868
  8.0 22.8 %collective-permute-start.6 = (f32[6,128,256]{2,1,0:T(8,128)}, f32[6,128,256]{2,1,0:T(8,128)}, u32[]{:S(2)}, u32[]{:S(2)}) collective-permute-start(f32[6,128,256]{2,1,0:T(8,128)} %get-tuple-element.30), channel_id=1, source_target_pairs={{0,8},{1,9},{2,26},{3,27},{4,12},{5,13},{6,30},{7,31},{8,16},{9,17... | collective-permute-start | bytes 2359304 | tf_op jit(solution)/shard_map/ppermute | solution.py:352
  11.0 21.6 %copy-start.1 = (f32[1,1,8,128,256]{4,3,2,1,0:T(8,128)S(1)}, f32[1,1,8,128,256]{4,3,2,1,0:T(8,128)}, u32[]{:S(2)}) copy-start(f32[1,1,8,128,256]{4,3,2,1,0:T(8,128)} %param.8) | copy-start | bytes 3145732
  11.0 21.6 %collective-permute-start.1 = (f32[4,128,256]{2,1,0:T(8,128)}, f32[4,128,256]{2,1,0:T(8,128)}, u32[]{:S(2)}, u32[]{:S(2)}) collective-permute-start(f32[4,128,256]{2,1,0:T(8,128)} %dynamic-slice_bitcast_fusion), channel_id=1, source_target_pairs={{0,1},{2,3},{4,5},{6,7},{8,9},{10,11},{12,13},{14,15},{16,17},{18,... | collective-permute-start | bytes 1572872 | tf_op jit(solution)/shard_map/ppermute | solution.py:352
  15.3 31.3 %collective-permute-start.8 = (f32[4,128,256]{2,1,0:T(8,128)}, f32[4,128,256]{2,1,0:T(8,128)}, u32[]{:S(2)}, u32[]{:S(2)}) collective-permute-start(f32[4,128,256]{2,1,0:T(8,128)} %copy-done.3), channel_id=1, source_target_pairs={{0,8},{1,9},{2,26},{3,27},{4,12},{5,13},{6,30},{7,31},{8,16},{9,17... | collective-permute-start | bytes 1572872 | tf_op jit(solution)/shard_map/ppermute | solution.py:352
  27.8 3.0 %collective-permute-start = (f32[8,128,256]{2,1,0:T(8,128)}, f32[8,128,256]{2,1,0:T(8,128)}, u32[]{:S(2)}, u32[]{:S(2)}) collective-permute-start(f32[8,128,256]{2,1,0:T(8,128)} %param.3), channel_id=1, source_target_pairs={{0,2},{2,0},{4,6},{6,4},{1,3},{3,1},{5,7},{7,5},{8,10},{10,8},{12,... | collective-permute-start | bytes 3145736 | tf_op jit(solution)/shard_map/cond/branch_1_fun/ppermute | solution.py:337
  30.8 21.4 %collective-permute-start.7 = (f32[6,128,256]{2,1,0:T(8,128)}, f32[6,128,256]{2,1,0:T(8,128)S(1)}, u32[]{:S(2)}, u32[]{:S(2)}) collective-permute-start(f32[6,128,256]{2,1,0:T(8,128)} %collective-permute-done.6.halo_a), channel_id=1, source_target_pairs={{0,4},{2,6},{4,0},{6,2},{1,5},{3,7},{5,1},{7,3},{8,12},{10,14},{12... | collective-permute-start | bytes 2359304 | tf_op jit(solution)/shard_map/ppermute | solution.py:334
  35.8 31.5 %collective-permute-start.5 = (f32[5,128,256]{2,1,0:T(8,128)S(1)}, f32[5,128,256]{2,1,0:T(8,128)S(1)}, u32[]{:S(2)}, u32[]{:S(2)}) collective-permute-start(f32[5,128,256]{2,1,0:T(8,128)S(1)} %shard_map.51), channel_id=1, source_target_pairs={{0,1},{2,3},{4,5},{6,7},{8,9},{10,11},{12,13},{14,15},{16,17},{18,... | collective-permute-start | bytes 1966088 | tf_op jit(solution)/shard_map/ppermute | solution.py:352
  46.6 15.2 %collective-permute-start.9 = (f32[4,128,256]{2,1,0:T(8,128)}, f32[4,128,256]{2,1,0:T(8,128)S(1)}, u32[]{:S(2)}, u32[]{:S(2)}) collective-permute-start(f32[4,128,256]{2,1,0:T(8,128)} %collective-permute-done.8.halo_b), channel_id=1, source_target_pairs={{0,4},{2,6},{4,0},{6,2},{1,5},{3,7},{5,1},{7,3},{8,12},{10,14},{12... | collective-permute-start | bytes 1572872 | tf_op jit(solution)/shard_map/ppermute | solution.py:334
  47.2 21.7 %collective-permute-start.11 = (f32[5,128,256]{2,1,0:T(8,128)S(1)}, f32[5,128,256]{2,1,0:T(8,128)S(1)}, u32[]{:S(2)}, u32[]{:S(2)}) collective-permute-start(f32[5,128,256]{2,1,0:T(8,128)S(1)} %shard_map.51), channel_id=1, source_target_pairs={{0,27},{2,9},{4,31},{6,13},{8,3},{10,17},{12,7},{14,21},{16,11},{1... | collective-permute-start | bytes 1966088 | tf_op jit(solution)/shard_map/ppermute | solution.py:352
  50.7 18.2 %collective-permute-start.2 = (f32[4,128,256]{2,1,0:T(8,128)}, f32[4,128,256]{2,1,0:T(8,128)S(1)}, u32[]{:S(2)}, u32[]{:S(2)}) collective-permute-start(f32[4,128,256]{2,1,0:T(8,128)} %collective-permute-done.1), channel_id=1, source_target_pairs={{1,8},{3,26},{5,12},{7,30},{9,16},{11,2},{13,20},{15,6},{17,24},{1... | collective-permute-start | bytes 1572872 | tf_op jit(solution)/shard_map/ppermute | solution.py:352
  67.3 1.8 %collective-permute-start.10 = (f32[3,128,256]{2,1,0:T(8,128)S(1)}, f32[3,128,256]{2,1,0:T(8,128)S(1)}, u32[]{:S(2)}, u32[]{:S(2)}) collective-permute-start(f32[3,128,256]{2,1,0:T(8,128)S(1)} %slice.16), channel_id=1, source_target_pairs={{0,2},{2,0},{4,6},{6,4},{1,3},{3,1},{5,7},{7,5},{8,10},{10,8},{12,... | collective-permute-start | bytes 1179656 | tf_op jit(solution)/shard_map/ppermute | solution.py:337
  72.8 2.9 %collective-permute-start.12 = (f32[9,128,256]{2,1,0:T(8,128)S(1)}, f32[9,128,256]{2,1,0:T(8,128)S(1)}, u32[]{:S(2)}, u32[]{:S(2)}) collective-permute-start(f32[9,128,256]{2,1,0:T(8,128)S(1)} %get-tuple-element.38), channel_id=1, source_target_pairs={{0,2},{2,0},{4,6},{6,4},{1,3},{3,1},{5,7},{7,5},{8,10},{10,8},{12,... | collective-permute-start | bytes 3538952 | tf_op jit(solution)/shard_map/ppermute | solution.py:337
